TPU v7x, 32 devices: a whole 2x2x4 slice. The times are simulated.
32 devices in a mesh: blk: 16 (over z, y, x), row: 2 (over core).
Axes of the slice: x: 2, y: 2, z: 4, core: 2. Of those that a mesh axis runs over, the one named last changes fastest.
Arguments:
- points: bfloat16 [4096, 128], P(('blk', 'row')), may hold values from -6 to 6
- w_in: bfloat16 [128, 1024], replicated, may hold values from -0.5 to 0.5
- b_in: float32 [1024], replicated, may hold values from -4 to 4
- w_out: bfloat16 [1024, 128], replicated, may hold values from -0.1875 to 0.1875
- scales: float32 [128], replicated, may hold values from 0.04 to 0.16
- left: bfloat16 [4096, 64], P(('blk', 'row')), may hold values from -2 to 2
- right: bfloat16 [4096, 64], P(('blk', 'row')), may hold values from -2 to 2
Outputs:
- feat_grad: float32 [4096, 128], P(('blk', 'row'))
- grad_w_in: float32 [128, 1024], replicated
- grad_b_in: float32 [1024], replicated
- grad_w_out: float32 [1024, 128], replicated
All inputs are finite; a program needn't handle non-finite values.
Results may differ from a plain program's by a relative error of at most 0.012.
The roundings to bfloat16 on the way count: a program that leaves them out, or rounds other values in their place, can miss the bound.
Values may be sent and summed in bfloat16 or wider, within the bound.
No kernel may reach another device: no remote copies, remote signals or barrier semaphores. Data moves between devices by JAX's collectives and lax.ppermute only.
A program may use at most 64 MiB of HBM per device.

v0:
```python
import jax
import jax.numpy as jnp
from jax import lax
from jax.sharding import PartitionSpec as P


def from_behind(value, axis, steps):
    count = lax.axis_size(axis)
    pairs = [(source, (source + steps) % count) for source in range(count)]
    return lax.ppermute(value, axis, pairs)


def silu_slope(pre):
    sig = jax.nn.sigmoid(pre)
    return sig * (1.0 + pre * (1.0 - sig))


def local(points, w_in, b_in, w_out, scales, left, right):
    pre = jnp.dot(points, w_in, preferred_element_type=jnp.float32) + b_in
    hidden = jax.nn.silu(pre).astype(jnp.bfloat16)
    feats = jnp.dot(hidden, w_out, preferred_element_type=jnp.float32)
    scaled = (feats * scales).astype(jnp.bfloat16)
    pairs_ab = jnp.concatenate([left, right], axis=1)
    pairs_ba = jnp.concatenate([right, left], axis=1)
    home_g, home_ab = (
        lax.all_gather(scaled, "row", axis=0, tiled=True),
        lax.all_gather(pairs_ab, "row", axis=0, tiled=True),
    )
    home_f = home_g.astype(jnp.float32)
    home_n = jnp.sum(home_f * home_f, axis=1)
    contract = (((1,), (1,)), ((), ()))
    down = (((0,), (0,)), ((), ()))

    def tile(visit_g, visit_ba):
        visit_f = visit_g.astype(jnp.float32)
        visit_n = jnp.sum(visit_f * visit_f, axis=1)
        cross = lax.dot_general(visit_g, home_g, contract, preferred_element_type=jnp.float32)
        kern = jnp.exp(-0.5 * (visit_n[:, None] + home_n[None, :] - 2.0 * cross))
        coup = lax.dot_general(visit_ba, home_ab, contract, preferred_element_type=jnp.float32)
        weight = coup * kern
        weight_b = weight.astype(jnp.bfloat16)
        home_term = -jnp.sum(weight, axis=0)[:, None] * home_f + lax.dot_general(
            weight_b, visit_g, down, preferred_element_type=jnp.float32
        )
        visit_term = -jnp.sum(weight, axis=1)[:, None] * visit_f + jnp.dot(
            weight_b, home_g, preferred_element_type=jnp.float32
        )
        return (home_term, visit_term)

    home_acc, unused = tile(scaled, pairs_ba)
    blocks = lax.axis_size("blk")
    half = blocks // 2

    def visit_step(step, carry):
        visit_g, visit_ba, visit_acc, total = carry
        visit_g, visit_ba, visit_acc = (
            from_behind(visit_g.astype(jnp.float32), "blk", 1).astype(visit_g.dtype),
            from_behind(visit_ba.astype(jnp.float32), "blk", 1).astype(visit_ba.dtype),
            from_behind(visit_acc, "blk", 1),
        )
        home_term, visit_term = tile(visit_g, visit_ba)
        keep = (step < half).astype(jnp.float32)
        return (visit_g, visit_ba, visit_acc + keep * visit_term, total + home_term)

    start = (scaled, pairs_ba, jnp.zeros(feats.shape, jnp.float32), home_acc)
    unused_g, unused_ba, visit_acc, home_acc = lax.fori_loop(1, half + 1, visit_step, start)
    carried = from_behind(visit_acc, "blk", -half)
    own_sum = lax.psum_scatter(home_acc, "row", scatter_dimension=0, tiled=True)
    feat_grad = (own_sum + carried) * scales
    feat_grad_b = feat_grad.astype(jnp.bfloat16)
    part_w_out = jnp.dot(hidden.T, feat_grad_b, preferred_element_type=jnp.float32)
    pre_grad = jnp.dot(feat_grad_b, w_out.T, preferred_element_type=jnp.float32) * silu_slope(pre)
    pre_grad_b = pre_grad.astype(jnp.bfloat16)
    part_w_in = jnp.dot(points.T, pre_grad_b, preferred_element_type=jnp.float32)
    part_b_in = jnp.sum(pre_grad, axis=0)
    grad_w_in, grad_b_in, grad_w_out = lax.psum((part_w_in, part_b_in, part_w_out), ("blk", "row"))
    factor = (points.shape[0] * blocks * lax.axis_size("row")) ** (-0.5)
    return (feat_grad, factor * grad_w_in, factor * grad_b_in, factor * grad_w_out)


def solution(mesh):
    placed = (
        P(("blk", "row"), None),
        P(),
        P(),
        P(),
        P(),
        P(("blk", "row"), None),
        P(("blk", "row"), None),
    )
    return jax.shard_map(
        local,
        mesh=mesh,
        in_specs=placed,
        out_specs=(P(("blk", "row"), None), P(), P(), P()),
        check_vma=False,
    )
```

profile of v0, /device:TPU:0, one launch (start us, length us, event | category | flops | bytes accessed | tf_op | source)
XLA Modules:
  0.0 246.8 jit_solution(9988218852937722153)
XLA Ops:
  7.2 1.2 convolution_add_fusion.1
  8.9 2.0 all_gather.7
  12.7 1.9 all_gather.6
  15.2 77.4 %while.20 = (s32[]{:T(128)}, bf16[128,128]{1,0:T(8,128)(2,1)S(1)}, bf16[128,128]{1,0:T(8,128)(2,1)S(1)}, f32[128,128]{1,0:T(8,128)S(1)}, f32[256,128]{1,0:T(8,12...) while((s32[]{:T(128)}, bf16[128,128]{1,0:T(8,128)(2,1)S(1)}, ...), condition=%wide.region_7.8_spmd.clone, body=%wide.region_3.7_spmd.clone.sunk | while | flops 34062212 | bytes 2138377 | solution.py:66
  15.2 2.9 %collective-permute-start.1 = (bf16[128,128]{1,0:T(8,128)(2,1)S(1)}, bf16[128,128]{1,0:T(8,128)(2,1)S(1)}, u32[]{:S(2)}, u32[]{:S(2)}) collective-permute-start(bf16[128,128]{1,0:T(8,128)(2,1)S(1)} %get-tuple-element.317), channel_id=1, source_target_pairs={{0,2},{2,4},{4,6},{6,8},{8,10},{10,12},{12,14},{14,16},{16,18},{18... | collective-permute-start | bytes 98312 | tf_op jit(solution)/shard_map/while/body/eval_jaxpr/ppermute | solution.py:10
  18.1 1.5 collective-permute-start
  19.6 1.5 collective-permute-start.2
  21.2 4.6 %collective-permute-done = bf16[128,128]{1,0:T(8,128)(2,1)S(1)} collective-permute-done((bf16[128,128]{1,0:T(8,128)(2,1)S(1)}, bf16[128,128]{1,0:T(8,128)(2,1)S(1)}, u32[]{:S(2)}, u32[]{:S(2)}) %collective-permute-start) | collective-permute-done | bytes 32800 | tf_op jit(solution)/shard_map/while/body/eval_jaxpr/ppermute | solution.py:10
  26.6 0.9 collective-permute-done.2
  28.0 0.6 collective-permute-start.2
  28.7 6.9 %collective-permute-done = bf16[128,128]{1,0:T(8,128)(2,1)S(1)} collective-permute-done((bf16[128,128]{1,0:T(8,128)(2,1)S(1)}, bf16[128,128]{1,0:T(8,128)(2,1)S(1)}, u32[]{:S(2)}, u32[]{:S(2)}) %collective-permute-start) | collective-permute-done | bytes 32800 | tf_op jit(solution)/shard_map/while/body/eval_jaxpr/ppermute | solution.py:10
  36.7 0.7 collective-permute-start
  37.5 7.1 %collective-permute-done = bf16[128,128]{1,0:T(8,128)(2,1)S(1)} collective-permute-done((bf16[128,128]{1,0:T(8,128)(2,1)S(1)}, bf16[128,128]{1,0:T(8,128)(2,1)S(1)}, u32[]{:S(2)}, u32[]{:S(2)}) %collective-permute-start) | collective-permute-done | bytes 32800 | tf_op jit(solution)/shard_map/while/body/eval_jaxpr/ppermute | solution.py:10
  46.2 7.2 %collective-permute-done = bf16[128,128]{1,0:T(8,128)(2,1)S(1)} collective-permute-done((bf16[128,128]{1,0:T(8,128)(2,1)S(1)}, bf16[128,128]{1,0:T(8,128)(2,1)S(1)}, u32[]{:S(2)}, u32[]{:S(2)}) %collective-permute-start) | collective-permute-done | bytes 32800 | tf_op jit(solution)/shard_map/while/body/eval_jaxpr/ppermute | solution.py:10
  54.5 1.4 collective-permute-start
  56.0 6.4 %collective-permute-done = bf16[128,128]{1,0:T(8,128)(2,1)S(1)} collective-permute-done((bf16[128,128]{1,0:T(8,128)(2,1)S(1)}, bf16[128,128]{1,0:T(8,128)(2,1)S(1)}, u32[]{:S(2)}, u32[]{:S(2)}) %collective-permute-start) | collective-permute-done | bytes 32800 | tf_op jit(solution)/shard_map/while/body/eval_jaxpr/ppermute | solution.py:10
  63.2 0.8 collective-permute-done.2
  64.5 8.2 %collective-permute-done = bf16[128,128]{1,0:T(8,128)(2,1)S(1)} collective-permute-done((bf16[128,128]{1,0:T(8,128)(2,1)S(1)}, bf16[128,128]{1,0:T(8,128)(2,1)S(1)}, u32[]{:S(2)}, u32[]{:S(2)}) %collective-permute-start) | collective-permute-done | bytes 32800 | tf_op jit(solution)/shard_map/while/body/eval_jaxpr/ppermute | solution.py:10
  74.5 8.2 %collective-permute-done = bf16[128,128]{1,0:T(8,128)(2,1)S(1)} collective-permute-done((bf16[128,128]{1,0:T(8,128)(2,1)S(1)}, bf16[128,128]{1,0:T(8,128)(2,1)S(1)}, u32[]{:S(2)}, u32[]{:S(2)}) %collective-permute-start) | collective-permute-done | bytes 32800 | tf_op jit(solution)/shard_map/while/body/eval_jaxpr/ppermute | solution.py:10
  84.0 7.7 %collective-permute-done = bf16[128,128]{1,0:T(8,128)(2,1)S(1)} collective-permute-done((bf16[128,128]{1,0:T(8,128)(2,1)S(1)}, bf16[128,128]{1,0:T(8,128)(2,1)S(1)}, u32[]{:S(2)}, u32[]{:S(2)}) %collective-permute-start) | collective-permute-done | bytes 32800 | tf_op jit(solution)/shard_map/while/body/eval_jaxpr/ppermute | solution.py:10
  92.6 0.8 copy.20
  93.6 5.2 %collective-permute-done.3 = f32[128,128]{0,1:T(8,128)S(1)} collective-permute-done((f32[128,128]{0,1:T(8,128)S(1)}, f32[128,128]{0,1:T(8,128)S(1)}, u32[]{:S(2)}, u32[]{:S(2)}) %collective-permute-start.3) | collective-permute-done | bytes 65568 | tf_op jit(solution)/shard_map/ppermute | solution.py:10
  98.8 0.7 reduce-scatter.2.cloned.1.call-done
  99.5 0.9 add_multiply_fusion
  100.8 1.1 fusion.18
  102.0 1.1 convolution_bitcast_fusion
  103.0 0.7 copy.22
  103.8 40.8 %psum.22 = f32[1024]{0:T(1024)S(1)} all-reduce(f32[1024]{0:T(1024)S(1)} %get-tuple-element.233), channel_id=1, replica_groups=mesh['blk'=16,'row'=2] {'blk','row'}, use_global_device_ids=true, to_apply=%region_11.12 | all-reduce | flops 1024 | bytes 8192 | tf_op jit(solution)/shard_map/psum | solution.py:76
  145.2 91.9 %all-reduce.3.cloned.1.call-done = (f32[128,1024]{0,1:T(8,128)}, f32[1024,128]{1,0:T(8,128)}) async-done(((f32[128,1024]{0,1:T(8,128)}, f32[1024,128]{1,0:T(8,128)}), (f32[128,1024]{0,1:T(8,128)}, f32[1024,128]{1,0:T(8,128)})) %all-reduce.3.cloned.1.call-update) | async-done | bytes 1048592 | tf_op jit(solution)/shard_map/psum | solution.py:76
  237.0 1.1 broadcast_multiply_fusion.1
  238.1 1.0 copy.23
  239.1 0.8 broadcast_multiply_fusion
  (146 shorter events, 14.0 us)
Async XLA Ops:
  7.2 1.3 copy-start
  7.2 92.4 %reduce-scatter.2.cloned.1.call-start = ((), (), s32[]{:S(2)}) async-start(), calls=%async_computation.1 | async-start | bytes 196608 | tf_op jit(solution)/shard_map/reduce_scatter | solution.py:68
  7.2 1.2 copy-start.5
  11.0 0.7 copy-start.3
  15.2 10.9 %collective-permute-start.1 = (bf16[128,128]{1,0:T(8,128)(2,1)S(1)}, bf16[128,128]{1,0:T(8,128)(2,1)S(1)}, u32[]{:S(2)}, u32[]{:S(2)}) collective-permute-start(bf16[128,128]{1,0:T(8,128)(2,1)S(1)} %get-tuple-element.317), channel_id=1, source_target_pairs={{0,2},{2,4},{4,6},{6,8},{8,10},{10,12},{12,14},{14,16},{16,18},{18... | collective-permute-start | bytes 98312 | tf_op jit(solution)/shard_map/while/body/eval_jaxpr/ppermute | solution.py:10
  18.1 7.7 %collective-permute-start = (bf16[128,128]{1,0:T(8,128)(2,1)S(1)}, bf16[128,128]{1,0:T(8,128)(2,1)S(1)}, u32[]{:S(2)}, u32[]{:S(2)}) collective-permute-start(bf16[128,128]{1,0:T(8,128)(2,1)S(1)} %get-tuple-element.316), channel_id=1, source_target_pairs={{0,2},{2,4},{4,6},{6,8},{8,10},{10,12},{12,14},{14,16},{16,18},{18... | collective-permute-start | bytes 98312 | tf_op jit(solution)/shard_map/while/body/eval_jaxpr/ppermute | solution.py:10
  19.6 7.9 %collective-permute-start.2 = (f32[128,128]{1,0:T(8,128)S(1)}, f32[128,128]{1,0:T(8,128)S(1)}, u32[]{:S(2)}, u32[]{:S(2)}) collective-permute-start(f32[128,128]{1,0:T(8,128)S(1)} %broadcast_select_fusion.2), channel_id=1, source_target_pairs={{0,2},{2,4},{4,6},{6,8},{8,10},{10,12},{12,14},{14,16},{16,18},{18... | collective-permute-start | bytes 196616 | tf_op jit(solution)/shard_map/while/body/eval_jaxpr/ppermute | solution.py:10
  27.7 8.2 %collective-permute-start.1 = (bf16[128,128]{1,0:T(8,128)(2,1)S(1)}, bf16[128,128]{1,0:T(8,128)(2,1)S(1)}, u32[]{:S(2)}, u32[]{:S(2)}) collective-permute-start(bf16[128,128]{1,0:T(8,128)(2,1)S(1)} %get-tuple-element.317), channel_id=1, source_target_pairs={{0,2},{2,4},{4,6},{6,8},{8,10},{10,12},{12,14},{14,16},{16,18},{18... | collective-permute-start | bytes 98312 | tf_op jit(solution)/shard_map/while/body/eval_jaxpr/ppermute | solution.py:10
  27.8 7.8 %collective-permute-start = (bf16[128,128]{1,0:T(8,128)(2,1)S(1)}, bf16[128,128]{1,0:T(8,128)(2,1)S(1)}, u32[]{:S(2)}, u32[]{:S(2)}) collective-permute-start(bf16[128,128]{1,0:T(8,128)(2,1)S(1)} %get-tuple-element.316), channel_id=1, source_target_pairs={{0,2},{2,4},{4,6},{6,8},{8,10},{10,12},{12,14},{14,16},{16,18},{18... | collective-permute-start | bytes 98312 | tf_op jit(solution)/shard_map/while/body/eval_jaxpr/ppermute | solution.py:10
  28.0 8.4 %collective-permute-start.2 = (f32[128,128]{1,0:T(8,128)S(1)}, f32[128,128]{1,0:T(8,128)S(1)}, u32[]{:S(2)}, u32[]{:S(2)}) collective-permute-start(f32[128,128]{1,0:T(8,128)S(1)} %broadcast_select_fusion.2), channel_id=1, source_target_pairs={{0,2},{2,4},{4,6},{6,8},{8,10},{10,12},{12,14},{14,16},{16,18},{18... | collective-permute-start | bytes 196616 | tf_op jit(solution)/shard_map/while/body/eval_jaxpr/ppermute | solution.py:10
  36.6 8.2 %collective-permute-start.1 = (bf16[128,128]{1,0:T(8,128)(2,1)S(1)}, bf16[128,128]{1,0:T(8,128)(2,1)S(1)}, u32[]{:S(2)}, u32[]{:S(2)}) collective-permute-start(bf16[128,128]{1,0:T(8,128)(2,1)S(1)} %get-tuple-element.317), channel_id=1, source_target_pairs={{0,2},{2,4},{4,6},{6,8},{8,10},{10,12},{12,14},{14,16},{16,18},{18... | collective-permute-start | bytes 98312 | tf_op jit(solution)/shard_map/while/body/eval_jaxpr/ppermute | solution.py:10
  36.7 7.8 %collective-permute-start = (bf16[128,128]{1,0:T(8,128)(2,1)S(1)}, bf16[128,128]{1,0:T(8,128)(2,1)S(1)}, u32[]{:S(2)}, u32[]{:S(2)}) collective-permute-start(bf16[128,128]{1,0:T(8,128)(2,1)S(1)} %get-tuple-element.316), channel_id=1, source_target_pairs={{0,2},{2,4},{4,6},{6,8},{8,10},{10,12},{12,14},{14,16},{16,18},{18... | collective-permute-start | bytes 98312 | tf_op jit(solution)/shard_map/while/body/eval_jaxpr/ppermute | solution.py:10
  37.4 8.0 %collective-permute-start.2 = (f32[128,128]{1,0:T(8,128)S(1)}, f32[128,128]{1,0:T(8,128)S(1)}, u32[]{:S(2)}, u32[]{:S(2)}) collective-permute-start(f32[128,128]{1,0:T(8,128)S(1)} %broadcast_select_fusion.2), channel_id=1, source_target_pairs={{0,2},{2,4},{4,6},{6,8},{8,10},{10,12},{12,14},{14,16},{16,18},{18... | collective-permute-start | bytes 196616 | tf_op jit(solution)/shard_map/while/body/eval_jaxpr/ppermute | solution.py:10
  45.5 8.2 %collective-permute-start.1 = (bf16[128,128]{1,0:T(8,128)(2,1)S(1)}, bf16[128,128]{1,0:T(8,128)(2,1)S(1)}, u32[]{:S(2)}, u32[]{:S(2)}) collective-permute-start(bf16[128,128]{1,0:T(8,128)(2,1)S(1)} %get-tuple-element.317), channel_id=1, source_target_pairs={{0,2},{2,4},{4,6},{6,8},{8,10},{10,12},{12,14},{14,16},{16,18},{18... | collective-permute-start | bytes 98312 | tf_op jit(solution)/shard_map/while/body/eval_jaxpr/ppermute | solution.py:10
  45.6 7.8 %collective-permute-start = (bf16[128,128]{1,0:T(8,128)(2,1)S(1)}, bf16[128,128]{1,0:T(8,128)(2,1)S(1)}, u32[]{:S(2)}, u32[]{:S(2)}) collective-permute-start(bf16[128,128]{1,0:T(8,128)(2,1)S(1)} %get-tuple-element.316), channel_id=1, source_target_pairs={{0,2},{2,4},{4,6},{6,8},{8,10},{10,12},{12,14},{14,16},{16,18},{18... | collective-permute-start | bytes 98312 | tf_op jit(solution)/shard_map/while/body/eval_jaxpr/ppermute | solution.py:10
  46.1 8.2 %collective-permute-start.2 = (f32[128,128]{1,0:T(8,128)S(1)}, f32[128,128]{1,0:T(8,128)S(1)}, u32[]{:S(2)}, u32[]{:S(2)}) collective-permute-start(f32[128,128]{1,0:T(8,128)S(1)} %broadcast_select_fusion.2), channel_id=1, source_target_pairs={{0,2},{2,4},{4,6},{6,8},{8,10},{10,12},{12,14},{14,16},{16,18},{18... | collective-permute-start | bytes 196616 | tf_op jit(solution)/shard_map/while/body/eval_jaxpr/ppermute | solution.py:10
  54.5 8.2 %collective-permute-start.1 = (bf16[128,128]{1,0:T(8,128)(2,1)S(1)}, bf16[128,128]{1,0:T(8,128)(2,1)S(1)}, u32[]{:S(2)}, u32[]{:S(2)}) collective-permute-start(bf16[128,128]{1,0:T(8,128)(2,1)S(1)} %get-tuple-element.317), channel_id=1, source_target_pairs={{0,2},{2,4},{4,6},{6,8},{8,10},{10,12},{12,14},{14,16},{16,18},{18... | collective-permute-start | bytes 98312 | tf_op jit(solution)/shard_map/while/body/eval_jaxpr/ppermute | solution.py:10
  54.5 7.8 %collective-permute-start = (bf16[128,128]{1,0:T(8,128)(2,1)S(1)}, bf16[128,128]{1,0:T(8,128)(2,1)S(1)}, u32[]{:S(2)}, u32[]{:S(2)}) collective-permute-start(bf16[128,128]{1,0:T(8,128)(2,1)S(1)} %get-tuple-element.316), channel_id=1, source_target_pairs={{0,2},{2,4},{4,6},{6,8},{8,10},{10,12},{12,14},{14,16},{16,18},{18... | collective-permute-start | bytes 98312 | tf_op jit(solution)/shard_map/while/body/eval_jaxpr/ppermute | solution.py:10
  55.9 8.1 %collective-permute-start.2 = (f32[128,128]{1,0:T(8,128)S(1)}, f32[128,128]{1,0:T(8,128)S(1)}, u32[]{:S(2)}, u32[]{:S(2)}) collective-permute-start(f32[128,128]{1,0:T(8,128)S(1)} %broadcast_select_fusion.2), channel_id=1, source_target_pairs={{0,2},{2,4},{4,6},{6,8},{8,10},{10,12},{12,14},{14,16},{16,18},{18... | collective-permute-start | bytes 196616 | tf_op jit(solution)/shard_map/while/body/eval_jaxpr/ppermute | solution.py:10
  64.2 8.8 %collective-permute-start.1 = (bf16[128,128]{1,0:T(8,128)(2,1)S(1)}, bf16[128,128]{1,0:T(8,128)(2,1)S(1)}, u32[]{:S(2)}, u32[]{:S(2)}) collective-permute-start(bf16[128,128]{1,0:T(8,128)(2,1)S(1)} %get-tuple-element.317), channel_id=1, source_target_pairs={{0,2},{2,4},{4,6},{6,8},{8,10},{10,12},{12,14},{14,16},{16,18},{18... | collective-permute-start | bytes 98312 | tf_op jit(solution)/shard_map/while/body/eval_jaxpr/ppermute | solution.py:10
  64.3 8.4 %collective-permute-start = (bf16[128,128]{1,0:T(8,128)(2,1)S(1)}, bf16[128,128]{1,0:T(8,128)(2,1)S(1)}, u32[]{:S(2)}, u32[]{:S(2)}) collective-permute-start(bf16[128,128]{1,0:T(8,128)(2,1)S(1)} %get-tuple-element.316), channel_id=1, source_target_pairs={{0,2},{2,4},{4,6},{6,8},{8,10},{10,12},{12,14},{14,16},{16,18},{18... | collective-permute-start | bytes 98312 | tf_op jit(solution)/shard_map/while/body/eval_jaxpr/ppermute | solution.py:10
  64.4 9.7 %collective-permute-start.2 = (f32[128,128]{1,0:T(8,128)S(1)}, f32[128,128]{1,0:T(8,128)S(1)}, u32[]{:S(2)}, u32[]{:S(2)}) collective-permute-start(f32[128,128]{1,0:T(8,128)S(1)} %broadcast_select_fusion.2), channel_id=1, source_target_pairs={{0,2},{2,4},{4,6},{6,8},{8,10},{10,12},{12,14},{14,16},{16,18},{18... | collective-permute-start | bytes 196616 | tf_op jit(solution)/shard_map/while/body/eval_jaxpr/ppermute | solution.py:10
  74.3 8.8 %collective-permute-start.1 = (bf16[128,128]{1,0:T(8,128)(2,1)S(1)}, bf16[128,128]{1,0:T(8,128)(2,1)S(1)}, u32[]{:S(2)}, u32[]{:S(2)}) collective-permute-start(bf16[128,128]{1,0:T(8,128)(2,1)S(1)} %get-tuple-element.317), channel_id=1, source_target_pairs={{0,2},{2,4},{4,6},{6,8},{8,10},{10,12},{12,14},{14,16},{16,18},{18... | collective-permute-start | bytes 98312 | tf_op jit(solution)/shard_map/while/body/eval_jaxpr/ppermute | solution.py:10
  74.3 8.4 %collective-permute-start = (bf16[128,128]{1,0:T(8,128)(2,1)S(1)}, bf16[128,128]{1,0:T(8,128)(2,1)S(1)}, u32[]{:S(2)}, u32[]{:S(2)}) collective-permute-start(bf16[128,128]{1,0:T(8,128)(2,1)S(1)} %get-tuple-element.316), channel_id=1, source_target_pairs={{0,2},{2,4},{4,6},{6,8},{8,10},{10,12},{12,14},{14,16},{16,18},{18... | collective-permute-start | bytes 98312 | tf_op jit(solution)/shard_map/while/body/eval_jaxpr/ppermute | solution.py:10
  74.4 9.1 %collective-permute-start.2 = (f32[128,128]{1,0:T(8,128)S(1)}, f32[128,128]{1,0:T(8,128)S(1)}, u32[]{:S(2)}, u32[]{:S(2)}) collective-permute-start(f32[128,128]{1,0:T(8,128)S(1)} %broadcast_select_fusion.2), channel_id=1, source_target_pairs={{0,2},{2,4},{4,6},{6,8},{8,10},{10,12},{12,14},{14,16},{16,18},{18... | collective-permute-start | bytes 196616 | tf_op jit(solution)/shard_map/while/body/eval_jaxpr/ppermute | solution.py:10
  83.7 8.2 %collective-permute-start.1 = (bf16[128,128]{1,0:T(8,128)(2,1)S(1)}, bf16[128,128]{1,0:T(8,128)(2,1)S(1)}, u32[]{:S(2)}, u32[]{:S(2)}) collective-permute-start(bf16[128,128]{1,0:T(8,128)(2,1)S(1)} %get-tuple-element.317), channel_id=1, source_target_pairs={{0,2},{2,4},{4,6},{6,8},{8,10},{10,12},{12,14},{14,16},{16,18},{18... | collective-permute-start | bytes 98312 | tf_op jit(solution)/shard_map/while/body/eval_jaxpr/ppermute | solution.py:10
  83.8 7.8 %collective-permute-start = (bf16[128,128]{1,0:T(8,128)(2,1)S(1)}, bf16[128,128]{1,0:T(8,128)(2,1)S(1)}, u32[]{:S(2)}, u32[]{:S(2)}) collective-permute-start(bf16[128,128]{1,0:T(8,128)(2,1)S(1)} %get-tuple-element.316), channel_id=1, source_target_pairs={{0,2},{2,4},{4,6},{6,8},{8,10},{10,12},{12,14},{14,16},{16,18},{18... | collective-permute-start | bytes 98312 | tf_op jit(solution)/shard_map/while/body/eval_jaxpr/ppermute | solution.py:10
  83.9 8.6 %collective-permute-start.2 = (f32[128,128]{1,0:T(8,128)S(1)}, f32[128,128]{1,0:T(8,128)S(1)}, u32[]{:S(2)}, u32[]{:S(2)}) collective-permute-start(f32[128,128]{1,0:T(8,128)S(1)} %broadcast_select_fusion.2), channel_id=1, source_target_pairs={{0,2},{2,4},{4,6},{6,8},{8,10},{10,12},{12,14},{14,16},{16,18},{18... | collective-permute-start | bytes 196616 | tf_op jit(solution)/shard_map/while/body/eval_jaxpr/ppermute | solution.py:10
  93.4 143.6 %all-reduce.3.cloned.1.call-start = ((), (), s32[]{:S(2)}) async-start(), calls=%async_computation.2 | async-start | bytes 2097152 | tf_op jit(solution)/shard_map/psum | solution.py:76
  93.6 5.2 %collective-permute-start.3 = (f32[128,128]{0,1:T(8,128)S(1)}, f32[128,128]{0,1:T(8,128)S(1)}, u32[]{:S(2)}, u32[]{:S(2)}) collective-permute-start(f32[128,128]{0,1:T(8,128)S(1)} %copy.21), channel_id=1, source_target_pairs={{0,16},{2,18},{4,20},{6,22},{8,24},{10,26},{12,28},{14,30},{16,0},... | collective-permute-start | bytes 196616 | tf_op jit(solution)/shard_map/ppermute | solution.py:10
  100.8 1.1 copy-start.2
  238.1 1.0 copy-start.1
  (1 other events, 0.7 us)
Sparse Core Ops, SparseCore 0:
  93.5 5.9 reduce-scatter.1
  105.5 131.4 all-reduce.2
where the time goes:
time: 247 us
  waiting for transfers between devices  156 us (63%)
  blocking collectives  44.6 us (18%)
  between operations  14.2 us (6%)
  matrix products  11 us (4%)
  starting transfers between devices  10.6 us (4%)
  local copies, waits for them, and re-layouts  4.55 us (2%)
  other arithmetic  4.49 us (2%)
    psum x1, waiting for transfers between devices, local(): lax.psum((part_w_in, part_b_in, part_w_out), ('blk', 'row'))  91.9 us
    ppermute x25, waiting for transfers between devices, from_behind(): return lax.ppermute(value, axis, pairs)  63.9 us
    psum x1, blocking collectives, local(): lax.psum((part_w_in, part_b_in, part_w_out), ('blk', 'row'))  40.8 us
    ppermute x25, starting transfers between devices, from_behind(): return lax.ppermute(value, axis, pairs)  10.5 us
  transfers between devices with their start and end apart: 27, of which 14 were waited for; matrix products, arithmetic and copies ran while one was open for 3% of the time, Pallas kernels for 0%

commit v1 on v0

--- a/solution.py
+++ b/solution.py
@@ -1,7 +1,22 @@
+import functools
+
 import jax
 import jax.numpy as jnp
 from jax import lax
+from jax.experimental import pallas as pl
+from jax.experimental.pallas import tpu as pltpu
 from jax.sharding import PartitionSpec as P
+
+F32 = jnp.float32
+BF16 = jnp.bfloat16
+LANES = 128
+GATHER_BYTES = 4 << 20
+NT = (((1,), (1,)), ((), ()))
+TN = (((0,), (0,)), ((), ()))
+
+
+def dot(a, b, dims=(((1,), (0,)), ((), ()))):
+    return lax.dot_general(a, b, dims, preferred_element_type=F32)
 
 
 def from_behind(value, axis, steps):
@@ -15,7 +30,183 @@
     return sig * (1.0 + pre * (1.0 - sig))
 
 
-def local(points, w_in, b_in, w_out, scales, left, right):
+def forward_kernel(places, raw, w_in, b_in, w_out, scales, *rest):
+    visit, points = rest[-2:]
+    din = w_in.shape[0]
+    pts = raw[:, :din]
+    pre = dot(pts, w_in[...]) + b_in[...]
+    hidden = (pre / (1.0 + jnp.exp(-pre))).astype(BF16)
+    feats = dot(hidden, w_out[...])
+    width = feats.shape[1]
+    visit[:, :width] = (feats * scales[...]).astype(BF16)
+    visit[:, width:] = raw[:, din:]
+    points[...] = pts
+
+
+def forward(raw, places, w_in, b_in, w_out, scales, held, total, rows):
+    groups = raw.shape[0] // rows
+    din, feat = w_in.shape[0], w_out.shape[1]
+    width = feat + raw.shape[1] - din
+    whole = lambda a: pl.BlockSpec(a.shape, lambda i, p: (0,) * a.ndim)
+    args = [raw, w_in, b_in, w_out, scales]
+    specs = [pl.BlockSpec((rows, raw.shape[1]), lambda i, p: (i, 0))] + [whole(a) for a in args[1:]]
+    aliases = {}
+    if held is not None:
+        args += list(held)
+        specs += [pl.BlockSpec(memory_space=pl.ANY)] * 2
+        aliases = {6: 0, 7: 1}
+    return pl.pallas_call(
+        forward_kernel,
+        grid_spec=pltpu.PrefetchScalarGridSpec(
+            num_scalar_prefetch=1,
+            grid=(groups,),
+            in_specs=specs,
+            out_specs=[
+                pl.BlockSpec((rows, width), lambda i, p: (p[i], 0)),
+                pl.BlockSpec((rows, din), lambda i, p: (p[i], 0)),
+            ],
+        ),
+        out_shape=[jax.ShapeDtypeStruct((total, width), BF16), jax.ShapeDtypeStruct((total, din), BF16)],
+        input_output_aliases=aliases,
+        cost_estimate=pl.CostEstimate(flops=4 * raw.shape[0] * w_in.size, bytes_accessed=4 * w_in.size, transcendentals=raw.shape[0] * w_in.shape[1]),
+    )(places, *args)
+
+
+def norm_lanes(feats, first, ones):
+    wide = feats.astype(F32)
+    norm = -0.5 * jnp.sum(wide * wide, axis=1, keepdims=True)
+    high = norm.astype(BF16).astype(F32)
+    mid = (norm - high).astype(BF16).astype(F32)
+    low = norm - high - mid
+    lane = lax.broadcasted_iota(jnp.int32, (feats.shape[0], LANES), 1)
+    part = jnp.where(lane == first, high, jnp.where(lane == first + 1, mid, jnp.where(lane == first + 2, low, 0.0)))
+    return jnp.where((lane >= ones) & (lane < ones + 3), 1.0, part).astype(BF16)
+
+
+def pair_sums(home, cols, cols_norm, feat, step):
+    rows = home.shape[0]
+    home_g = home[:, :feat]
+    half = (home.shape[1] - feat) // 2
+    swapped = jnp.concatenate([home[:, feat + half :], home[:, feat : feat + half]], axis=1)
+    home_x = jnp.concatenate([home_g, norm_lanes(home_g, 0, 3)], axis=1)
+    total = jnp.zeros((rows, feat), F32)
+    sums = jnp.zeros((rows, LANES), F32)
+    for at in range(0, cols.shape[0], step):
+        part = pl.ds(at, step)
+        g = cols[part, :feat]
+        kern = jnp.exp(dot(home_x, jnp.concatenate([g, cols_norm[part, :]], axis=1), NT))
+        weight = dot(swapped, cols[part, feat:], NT) * kern
+        for lane in range(0, step, LANES):
+            sums += weight[:, lane : lane + LANES]
+        total += dot(weight.astype(BF16), g)
+    return total - jnp.sum(sums, axis=1, keepdims=True) * home_g.astype(F32)
+
+
+def first_kernel(feat, step, home, cols, out, cols_norm):
+    @pl.when(pl.program_id(0) == 0)
+    def _():
+        cols_norm[...] = norm_lanes(cols[:, :feat], 3, 0)
+
+    out[...] = pair_sums(home[...], cols, cols_norm, feat, step)
+
+
+def second_kernel(feat, step, home, cols, before, points, w_in, b_in, w_out, scales, out, grads, cols_norm):
+    @pl.when(pl.program_id(0) == 0)
+    def _():
+        cols_norm[...] = norm_lanes(cols[:, :feat], 3, 0)
+        grads[...] = jnp.zeros_like(grads)
+
+    feat_grad = (before[...] + pair_sums(home[...], cols, cols_norm, feat, step)) * scales[...]
+    out[...] = feat_grad
+    feat_grad_b = feat_grad.astype(BF16)
+    din = w_in.shape[0]
+    pts = points[...]
+    pre = dot(pts, w_in[...]) + b_in[...]
+    sig = 1.0 / (1.0 + jnp.exp(-pre))
+    hidden = (pre * sig).astype(BF16)
+    pre_grad = dot(feat_grad_b, w_out[...], NT) * (sig * (1.0 + pre * (1.0 - sig)))
+    grads[:din, :] += dot(pts, pre_grad.astype(BF16), TN)
+    grads[din : din + feat, :] += dot(feat_grad_b, hidden, TN)
+    grads[din + feat :, :] += jnp.sum(pre_grad.reshape(-1, 8, pre_grad.shape[1]), axis=0)
+
+
+def pairs_first(own, feat, rows, step):
+    total, width = own.shape
+    return pl.pallas_call(
+        functools.partial(first_kernel, feat, step),
+        grid=(total // rows,),
+        in_specs=[pl.BlockSpec((rows, width), lambda i: (i, 0)), pl.BlockSpec((total, width), lambda i: (0, 0))],
+        out_specs=pl.BlockSpec((rows, feat), lambda i: (i, 0)),
+        out_shape=jax.ShapeDtypeStruct((total, feat), F32),
+        scratch_shapes=[pltpu.VMEM((total, LANES), BF16)],
+        compiler_params=pltpu.CompilerParams(vmem_limit_bytes=40 << 20),
+        cost_estimate=pl.CostEstimate(flops=6 * total * total * feat, bytes_accessed=own.size * 4, transcendentals=total * total),
+    )(own, own)
+
+
+def pairs_second(own, other, before, points, w_in, b_in, w_out, scales, rows, step):
+    total, width = own.shape
+    din, hid = w_in.shape
+    feat = w_out.shape[1]
+    whole = lambda a: pl.BlockSpec(a.shape, lambda i: (0,) * a.ndim)
+    return pl.pallas_call(
+        functools.partial(second_kernel, feat, step),
+        grid=(total // rows,),
+        in_specs=[
+            pl.BlockSpec((rows, width), lambda i: (i, 0)),
+            whole(other),
+            pl.BlockSpec((rows, feat), lambda i: (i, 0)),
+            pl.BlockSpec((rows, din), lambda i: (i, 0)),
+            whole(w_in),
+            whole(b_in),
+            whole(w_out),
+            whole(scales),
+        ],
+        out_specs=[
+            pl.BlockSpec((rows, feat), lambda i: (i, 0)),
+            pl.BlockSpec((din + feat + 8, hid), lambda i: (0, 0)),
+        ],
+        out_shape=[jax.ShapeDtypeStruct((total, feat), F32), jax.ShapeDtypeStruct((din + feat + 8, hid), F32)],
+        scratch_shapes=[pltpu.VMEM((total, LANES), BF16)],
+        compiler_params=pltpu.CompilerParams(vmem_limit_bytes=48 << 20),
+        cost_estimate=pl.CostEstimate(flops=6 * total * total * feat, bytes_accessed=own.size * 4, transcendentals=total * total),
+    )(own, other, before, points, w_in, b_in, w_out, scales)
+
+
+def swap(value, axis, bits):
+    count = lax.axis_size(axis)
+    return lax.ppermute(value, axis, [(source, source ^ bits) for source in range(count)])
+
+
+def gather_plan(inner, points, w_in, b_in, w_out, scales, left, right):
+    blocks = lax.axis_size("blk")
+    outer = blocks // inner
+    mine = lax.axis_index("blk")
+    rows = points.shape[0]
+    total = rows * blocks
+    b_in, scales = b_in[None, :], scales[None, :]
+    feat = w_out.shape[1]
+    raw = jnp.concatenate([points, left, right], axis=1)
+    column = jnp.concatenate([raw] + [swap(raw, "blk", inner * k) for k in range(1, outer)], axis=0)
+    planes = [column] + [swap(column, "blk", k) for k in range(1, inner)]
+    held = None
+    for k, plane in enumerate(planes):
+        places = jnp.bitwise_xor(mine, jnp.arange(outer, dtype=jnp.int32) * inner + k)
+        held = forward(plane, places, w_in, b_in, w_out, scales, held, total, rows)
+    own, own_points = held
+    other = swap(own, "row", 1)
+    tile = min(total, 256)
+    step = min(total, 512)
+    before = pairs_first(own, feat, tile, step)
+    grad, part = pairs_second(own, other, before, own_points, w_in, b_in, w_out, scales, tile, step)
+    feat_grad = lax.dynamic_slice_in_dim(grad, mine * rows, rows, 0)
+    factor = (total * lax.axis_size("row")) ** (-0.5)
+    both = factor * (part + swap(part, "row", 1))
+    din = w_in.shape[0]
+    return (feat_grad, both[:din], jnp.sum(both[din + feat :], axis=0), both[din : din + feat].T)
+
+
+def ring_plan(points, w_in, b_in, w_out, scales, left, right):
     pre = jnp.dot(points, w_in, preferred_element_type=jnp.float32) + b_in
     hidden = jax.nn.silu(pre).astype(jnp.bfloat16)
     feats = jnp.dot(hidden, w_out, preferred_element_type=jnp.float32)
@@ -78,6 +269,16 @@
     return (feat_grad, factor * grad_w_in, factor * grad_b_in, factor * grad_w_out)
 
 
+def local(points, w_in, b_in, w_out, scales, left, right):
+    blocks, cores = lax.axis_size("blk"), lax.axis_size("row")
+    width = points.shape[1] + left.shape[1] + right.shape[1]
+    size = points.shape[0] * blocks * cores * width * points.dtype.itemsize
+    inner = min(4, blocks)
+    fits = size <= GATHER_BYTES and cores == 2 and blocks & (blocks - 1) == 0
+    plan = functools.partial(gather_plan, inner) if fits else ring_plan
+    return plan(points, w_in, b_in, w_out, scales, left, right)
+
+
 def solution(mesh):
     placed = (
         P(("blk", "row"), None),

time: 247 us -> 79.6 us (0.32)
  waiting for transfers between devices: 156 us -> 6.54 us
  Pallas kernels: 0 us -> 48.2 us
  blocking collectives: 44.6 us -> 0 us
  between operations: 14.2 us -> 0.78 us
  matrix products: 11 us -> 0 us
  local copies, waits for them, and re-layouts: 4.55 us -> 7.52 us
    psum x1 -> x0, waiting for transfers between devices: 91.9 us -> none  [local(): lax.psum((part_w_in, part_b_in, part_w_out), ('blk', 'row'))]
    ppermute x25 -> x8, waiting for transfers between devices: 63.9 us -> 6.54 us  [swap(): lax.ppermute(value, axis, [(source, source ^ bits) for source in range(co...]
    pallas_call x0 -> x6, Pallas kernels: none -> 48.2 us  [the longest x4 18.9 us: forward(): pl.pallas_call(forward_kernel, grid_spec=pltpu.PrefetchScalarGridSpec(num...]
    psum x1 -> x0, blocking collectives: 40.8 us -> none  [local(): lax.psum((part_w_in, part_b_in, part_w_out), ('blk', 'row'))]
    dot_general x40 -> x0, matrix products: 11 us -> none  [the longest x9 2.24 us: tile(): lax.dot_general(visit_ba, home_ab, contract, preferred_element_type=jnp.f...]
    all_gather x2 -> x0, blocking collectives: 3.82 us -> none  [the longest x1 1.96 us: local(): lax.all_gather(scaled, 'row', axis=0, tiled=True)]
    unnamed x20 -> x25, local copies, waits for them, and re-layouts: 3.64 us -> 6 us
    ppermute x25 -> x8, starting transfers between devices: 10.5 us -> 9.81 us  [swap(): lax.ppermute(value, axis, [(source, source ^ bits) for source in range(co...]
  transfers between devices with their start and end apart: 27 -> 8, of which waited for: 14 -> 4; matrix products, arithmetic and copies ran while one was open for 3% -> 4% of each run, Pallas kernels for 0% -> 32%
where the time goes in v1:
time: 79.6 us; the launch traced here: 78.7 us
  Pallas kernels  48.2 us (61%)
  starting transfers between devices  9.81 us (12%)
  local copies, waits for them, and re-layouts  7.52 us (9%)
  waiting for transfers between devices  6.54 us (8%)
  other arithmetic  5.84 us (7%)
    pallas_call x4, Pallas kernels, forward(): pl.pallas_call(forward_kernel, grid_spec=pltpu.PrefetchScalarGridSpec(num...  18.9 us
    pallas_call x1, Pallas kernels, pairs_second(): pl.pallas_call(functools.partial(second_kernel, feat, step), grid=(total...  18.5 us
    pallas_call x1, Pallas kernels, pairs_first(): pl.pallas_call(functools.partial(first_kernel, feat, step), grid=(total /...  10.7 us
    ppermute x8, starting transfers between devices, swap(): lax.ppermute(value, axis, [(source, source ^ bits) for source in range(co...  9.81 us
    ppermute x8, waiting for transfers between devices, swap(): lax.ppermute(value, axis, [(source, source ^ bits) for source in range(co...  6.54 us
    unnamed x25, local copies, waits for them, and re-layouts  6 us
    xor x4, other arithmetic, gather_plan(): jnp.bitwise_xor(mine, jnp.arange(outer, dtype=jnp.int32) * inner + k)  2.14 us
  transfers between devices with their start and end apart: 8, of which 4 were waited for; matrix products, arithmetic and copies ran while one was open for 4% of the time, Pallas kernels for 32%

profile of v1, /device:TPU:0, one launch (start us, length us, event | category | flops | bytes accessed | tf_op | source)
XLA Modules:
  0.0 78.7 jit_solution(4145161231401044893)
XLA Ops:
  0.6 0.8 %copy.17 = bf16[128,64]{1,0:T(8,128)(2,1)S(1)} copy(bf16[128,64]{0,1:T(8,128)(2,1)} %param.12) | data formatting | bytes 32768 | tf_op args[5]
  1.5 0.8 %copy.18 = bf16[128,64]{1,0:T(8,128)(2,1)S(1)} copy(bf16[128,64]{0,1:T(8,128)(2,1)} %param.13) | data formatting | bytes 32768 | tf_op args[6]
  2.3 0.9 %pad_maximum_fusion.1 = bf16[128,256]{1,0:T(8,128)(2,1)S(1)} fusion(bf16[128,64]{1,0:T(8,128)(2,1)S(1)} %copy.18, bf16[128,64]{1,0:T(8,128)(2,1)S(1)} %copy.17, bf16[128,128]{1,0:T(8,128)(2,1)} %param.7), kind=kLoop, calls=%fused_computation.3 | loop fusion | flops 196608 | bytes 131072 | tf_op jit(solution)/shard_map/concatenate | solution.py:189
  3.1 5.1 %collective-permute-start.2 = (bf16[128,256]{1,0:T(8,128)(2,1)S(1)}, bf16[128,256]{1,0:T(8,128)(2,1)S(1)}, u32[]{:S(2)}, u32[]{:S(2)}) collective-permute-start(bf16[128,256]{1,0:T(8,128)(2,1)S(1)} %pad_maximum_fusion.1), channel_id=1, source_target_pairs={{0,24},{2,26},{4,28},{6,30},{8,16},{10,18},{12,20},{14,22},{16,8},... | collective-permute-start | bytes 196616 | tf_op jit(solution)/shard_map/ppermute | solution.py:178
  8.3 0.6 collective-permute-start
  8.9 0.5 add_xor_fusion.1.places
  9.4 1.4 %collective-permute-done.2 = bf16[128,256]{1,0:T(8,128)(2,1)S(1)} collective-permute-done((bf16[128,256]{1,0:T(8,128)(2,1)S(1)}, bf16[128,256]{1,0:T(8,128)(2,1)S(1)}, u32[]{:S(2)}, u32[]{:S(2)}) %collective-permute-start.2) | collective-permute-done | bytes 65568 | tf_op jit(solution)/shard_map/ppermute | solution.py:178
  10.8 3.0 %collective-permute-done.1 = bf16[128,256]{1,0:T(8,128)(2,1)S(1)} collective-permute-done((bf16[128,256]{1,0:T(8,128)(2,1)S(1)}, bf16[128,256]{1,0:T(8,128)(2,1)S(1)}, u32[]{:S(2)}, u32[]{:S(2)}) %collective-permute-start.1) | collective-permute-done | bytes 65568 | tf_op jit(solution)/shard_map/ppermute | solution.py:178
  13.9 0.8 %pad_maximum_fusion.raw = bf16[512,256]{1,0:T(8,128)(2,1)S(1)} fusion(bf16[128,256]{1,0:T(8,128)(2,1)S(1)} %collective-permute-done.2, bf16[128,256]{1,0:T(8,128)(2,1)S(1)} %collective-permute-done.1, bf16[128,256]{1,0:T(8,128)(2,1)S(1)} %collective-permute-done, bf16[128,64]{1,0:T(8,128)(2,1)S(1)} %copy.18, bf16[128,64]{1,0:T(8,128)(2,1)S(1)} %copy.17, ...), kind=kLoop, calls=%fused_computation.2 | loop fusion | flops 1572864 | bytes 524288 | tf_op jit(solution)/shard_map/concatenate | solution.py:190
  14.7 1.6 %collective-permute-start.5 = (bf16[512,256]{1,0:T(8,128)(2,1)S(1)}, bf16[512,256]{1,0:T(8,128)(2,1)S(1)}, u32[]{:S(2)}, u32[]{:S(2)}) collective-permute-start(bf16[512,256]{1,0:T(8,128)(2,1)S(1)} %pad_maximum_fusion.raw), channel_id=1, source_target_pairs={{0,2},{2,0},{4,6},{6,4},{8,10},{10,8},{12,14},{14,12},{16,18},{18,... | collective-permute-start | bytes 786440 | tf_op jit(solution)/shard_map/ppermute | solution.py:178
  16.3 0.6 add_xor_fusion.places
  16.9 1.5 %collective-permute-start.4 = (bf16[512,256]{1,0:T(8,128)(2,1)S(1)}, bf16[512,256]{1,0:T(8,128)(2,1)S(1)}, u32[]{:S(2)}, u32[]{:S(2)}) collective-permute-start(bf16[512,256]{1,0:T(8,128)(2,1)S(1)} %pad_maximum_fusion.raw), channel_id=1, source_target_pairs={{0,4},{2,6},{4,0},{6,2},{8,12},{10,14},{12,8},{14,10},{16,20},{18,... | collective-permute-start | bytes 786440 | tf_op jit(solution)/shard_map/ppermute | solution.py:178
  18.4 0.5 collective-permute-start.3
  18.9 0.5 fusion.places
  19.4 0.5 add_xor_fusion.2.places
  19.9 4.7 %shard_map.102 = (bf16[2048,256]{1,0:T(8,128)(2,1)}, bf16[2048,128]{1,0:T(8,128)(2,1)}) custom-call(s32[4]{0:T(128)} %fusion.places, bf16[512,256]{1,0:T(8,128)(2,1)} %copy-done.10, bf16[128,1024]{1,0:T(8,128)(2,1)} %w_in.9, f32[1,1024]{1,0:T(1,128)} %bitcast.4, bf16[1024,128]{1,0:T(8,128)(2,1)} %w_out.9, f32[1,128]{1,0:T(1,128)} %bitcast.9), custom_call_target="tpu_custom_call" | custom-call | flops 268435456 | bytes 524288 | tf_op jit(solution)/shard_map/pallas_call | solution.py:58
  24.7 0.7 copy-done.9
  25.4 4.7 %shard_map.103 = (bf16[2048,256]{1,0:T(8,128)(2,1)}, bf16[2048,128]{1,0:T(8,128)(2,1)}) custom-call(s32[4]{0:T(128)} %add_xor_fusion.places, bf16[512,256]{1,0:T(8,128)(2,1)} %copy-done.9, bf16[128,1024]{1,0:T(8,128)(2,1)} %w_in.9, f32[1,1024]{1,0:T(1,128)} %bitcast.5, bf16[1024,128]{1,0:T(8,128)(2,1)} %w_out.9, ...), custom_call_target="tpu_custom_call", output_to_operand_aliasing={{0}: (6, {}), {1}: (7, {})} | custom-call | flops 268435456 | bytes 524288 | tf_op jit(solution)/shard_map/pallas_call | solution.py:58
  30.3 0.7 copy-done.8
  31.0 4.7 %shard_map.104 = (bf16[2048,256]{1,0:T(8,128)(2,1)}, bf16[2048,128]{1,0:T(8,128)(2,1)}) custom-call(s32[4]{0:T(128)} %add_xor_fusion.1.places, bf16[512,256]{1,0:T(8,128)(2,1)} %copy-done.8, bf16[128,1024]{1,0:T(8,128)(2,1)} %w_in.9, f32[1,1024]{1,0:T(1,128)} %bitcast.6, bf16[1024,128]{1,0:T(8,128)(2,1)} %w_out.9, ...), custom_call_target="tpu_custom_call", output_to_operand_aliasing={{0}: (6, {}), {1}: (7, {})} | custom-call | flops 268435456 | bytes 524288 | tf_op jit(solution)/shard_map/pallas_call | solution.py:58
  35.7 0.7 copy-done.7
  36.4 4.7 %shard_map.105 = (bf16[2048,256]{1,0:T(8,128)(2,1)}, bf16[2048,128]{1,0:T(8,128)(2,1)}) custom-call(s32[4]{0:T(128)} %add_xor_fusion.2.places, bf16[512,256]{1,0:T(8,128)(2,1)} %copy-done.7, bf16[128,1024]{1,0:T(8,128)(2,1)} %w_in.9, f32[1,1024]{1,0:T(1,128)} %bitcast.7, bf16[1024,128]{1,0:T(8,128)(2,1)} %w_out.9, ...), custom_call_target="tpu_custom_call", output_to_operand_aliasing={{0}: (6, {}), {1}: (7, {})} | custom-call | flops 268435456 | bytes 524288 | tf_op jit(solution)/shard_map/pallas_call | solution.py:58
  41.1 1.2 %copy-done = bf16[2048,256]{1,0:T(8,128)(2,1)S(1)} copy-done((bf16[2048,256]{1,0:T(8,128)(2,1)S(1)}, bf16[2048,256]{1,0:T(8,128)(2,1)}, u32[]{:S(2)}) %copy-start) | copy-done | bytes 1048600
  42.4 10.7 %shard_map.106.before = f32[2048,128]{1,0:T(8,128)S(1)} custom-call(bf16[2048,256]{1,0:T(8,128)(2,1)S(1)} %copy-done, bf16[2048,256]{1,0:T(8,128)(2,1)S(1)} %copy-done), custom_call_target="tpu_custom_call" | custom-call | flops 3221225472 | bytes 2097152 | tf_op jit(solution)/shard_map/pallas_call | solution.py:135
  53.2 18.5 %shard_map.107 = (f32[2048,128]{1,0:T(8,128)S(1)}, f32[264,1024]{1,0:T(8,128)}) custom-call(bf16[2048,256]{1,0:T(8,128)(2,1)S(1)} %copy-done.1, bf16[2048,256]{1,0:T(8,128)(2,1)S(1)} %collective-permute-done.6.cols, f32[2048,128]{1,0:T(8,128)S(1)} %shard_map.106.before, bf16[2048,128]{1,0:T(8,128)(2,1)S(1)} %copy-done.2, bf16[128,1024]{1,0:T(8,128)(2,1)S(1)} %copy-done.3, ...), custom_call_target="tpu_custom_call" | custom-call | flops 3221225472 | bytes 2097152 | tf_op jit(solution)/shard_map/pallas_call | solution.py:152
  71.7 0.5 collective-permute-start.7
  72.2 0.6 constant_dynamic-slice_fusion
  72.9 1.9 %collective-permute-done.7 = f32[264,1024]{1,0:T(8,128)S(1)} collective-permute-done((f32[264,1024]{1,0:T(8,128)}, f32[264,1024]{1,0:T(8,128)S(1)}, u32[]{:S(2)}, u32[]{:S(2)}) %collective-permute-start.7) | collective-permute-done | bytes 1081376 | tf_op jit(solution)/shard_map/ppermute | solution.py:178
  74.8 1.4 %add_multiply_fusion = f32[264,1024]{1,0:T(8,128)S(1)} fusion(f32[264,1024]{1,0:T(8,128)} %get-tuple-element.23, f32[264,1024]{1,0:T(8,128)S(1)} %collective-permute-done.7), kind=kLoop, calls=%fused_computation | loop fusion | flops 540672 | bytes 3244032 | tf_op jit(solution)/shard_map/mul | solution.py:204
  76.2 0.6 slice_reduce_fusion
  76.8 0.9 %slice_bitcast_fusion = (f32[1024,128]{0,1:T(8,128)S(1)}, f32[128,1024]{1,0:T(8,128)}) fusion(f32[264,1024]{1,0:T(8,128)S(1)} %add_multiply_fusion), kind=kLoop, calls=%fused_computation.1 | loop fusion | bytes 2097152 | tf_op jit(solution)/shard_map/transpose | solution.py:206
  77.7 1.0 %copy.19 = f32[1024,128]{1,0:T(8,128)} copy(f32[1024,128]{0,1:T(8,128)S(1)} %get-tuple-element.28) | data formatting | bytes 1048576
  (25 shorter events, 0.2 us)
Async XLA Ops:
  3.1 7.7 %collective-permute-start.2 = (bf16[128,256]{1,0:T(8,128)(2,1)S(1)}, bf16[128,256]{1,0:T(8,128)(2,1)S(1)}, u32[]{:S(2)}, u32[]{:S(2)}) collective-permute-start(bf16[128,256]{1,0:T(8,128)(2,1)S(1)} %pad_maximum_fusion.1), channel_id=1, source_target_pairs={{0,24},{2,26},{4,28},{6,30},{8,16},{10,18},{12,20},{14,22},{16,8},... | collective-permute-start | bytes 196616 | tf_op jit(solution)/shard_map/ppermute | solution.py:178
  8.3 5.6 %collective-permute-start.1 = (bf16[128,256]{1,0:T(8,128)(2,1)S(1)}, bf16[128,256]{1,0:T(8,128)(2,1)S(1)}, u32[]{:S(2)}, u32[]{:S(2)}) collective-permute-start(bf16[128,256]{1,0:T(8,128)(2,1)S(1)} %pad_maximum_fusion.1), channel_id=1, source_target_pairs={{0,16},{2,18},{4,20},{6,22},{8,24},{10,26},{12,28},{14,30},{16,0},... | collective-permute-start | bytes 196616 | tf_op jit(solution)/shard_map/ppermute | solution.py:178
  8.3 5.6 %collective-permute-start = (bf16[128,256]{1,0:T(8,128)(2,1)S(1)}, bf16[128,256]{1,0:T(8,128)(2,1)S(1)}, u32[]{:S(2)}, u32[]{:S(2)}) collective-permute-start(bf16[128,256]{1,0:T(8,128)(2,1)S(1)} %pad_maximum_fusion.1), channel_id=1, source_target_pairs={{0,8},{2,10},{4,12},{6,14},{8,0},{10,2},{12,4},{14,6},{16,24},{18,... | collective-permute-start | bytes 196616 | tf_op jit(solution)/shard_map/ppermute | solution.py:178
  14.7 5.2 %copy-start.10 = (bf16[512,256]{1,0:T(8,128)(2,1)}, bf16[512,256]{1,0:T(8,128)(2,1)S(1)}, u32[]{:S(2)}) copy-start(bf16[512,256]{1,0:T(8,128)(2,1)S(1)} %pad_maximum_fusion.raw) | copy-start | bytes 786436
  14.7 9.9 %collective-permute-start.5 = (bf16[512,256]{1,0:T(8,128)(2,1)S(1)}, bf16[512,256]{1,0:T(8,128)(2,1)S(1)}, u32[]{:S(2)}, u32[]{:S(2)}) collective-permute-start(bf16[512,256]{1,0:T(8,128)(2,1)S(1)} %pad_maximum_fusion.raw), channel_id=1, source_target_pairs={{0,2},{2,0},{4,6},{6,4},{8,10},{10,8},{12,14},{14,12},{16,18},{18,... | collective-permute-start | bytes 786440 | tf_op jit(solution)/shard_map/ppermute | solution.py:178
  16.9 13.4 %collective-permute-start.4 = (bf16[512,256]{1,0:T(8,128)(2,1)S(1)}, bf16[512,256]{1,0:T(8,128)(2,1)S(1)}, u32[]{:S(2)}, u32[]{:S(2)}) collective-permute-start(bf16[512,256]{1,0:T(8,128)(2,1)S(1)} %pad_maximum_fusion.raw), channel_id=1, source_target_pairs={{0,4},{2,6},{4,0},{6,2},{8,12},{10,14},{12,8},{14,10},{16,20},{18,... | collective-permute-start | bytes 786440 | tf_op jit(solution)/shard_map/ppermute | solution.py:178
  18.4 17.3 %collective-permute-start.3 = (bf16[512,256]{1,0:T(8,128)(2,1)S(1)}, bf16[512,256]{1,0:T(8,128)(2,1)S(1)}, u32[]{:S(2)}, u32[]{:S(2)}) collective-permute-start(bf16[512,256]{1,0:T(8,128)(2,1)S(1)} %pad_maximum_fusion.raw), channel_id=1, source_target_pairs={{0,6},{2,4},{4,2},{6,0},{8,14},{10,12},{12,10},{14,8},{16,22},{18,... | collective-permute-start | bytes 786440 | tf_op jit(solution)/shard_map/ppermute | solution.py:178
  24.6 0.7 copy-start.9
  30.3 0.7 copy-start.8
  35.7 0.7 copy-start.7
  41.1 12.0 %collective-permute-start.6 = (bf16[2048,256]{1,0:T(8,128)(2,1)}, bf16[2048,256]{1,0:T(8,128)(2,1)S(1)}, u32[]{:S(2)}, u32[]{:S(2)}) collective-permute-start(bf16[2048,256]{1,0:T(8,128)(2,1)} %get-tuple-element.20.home.cols), channel_id=1, source_target_pairs={{0,1},{1,0},{2,3},{3,2},{4,5},{5,4},{6,7},{7,6},{8,9},{9,8},{10,11... | collective-permute-start | bytes 3145736 | tf_op jit(solution)/shard_map/ppermute | solution.py:178
  41.1 1.2 %copy-start = (bf16[2048,256]{1,0:T(8,128)(2,1)S(1)}, bf16[2048,256]{1,0:T(8,128)(2,1)}, u32[]{:S(2)}) copy-start(bf16[2048,256]{1,0:T(8,128)(2,1)} %get-tuple-element.20.home.cols) | copy-start | bytes 3145732
  42.3 10.8 %copy-start.1 = (bf16[2048,256]{1,0:T(8,128)(2,1)S(1)}, bf16[2048,256]{1,0:T(8,128)(2,1)}, u32[]{:S(2)}) copy-start(bf16[2048,256]{1,0:T(8,128)(2,1)} %get-tuple-element.20.home.cols) | copy-start | bytes 3145732
  42.4 10.8 %copy-start.2 = (bf16[2048,128]{1,0:T(8,128)(2,1)S(1)}, bf16[2048,128]{1,0:T(8,128)(2,1)}, u32[]{:S(2)}) copy-start(bf16[2048,128]{1,0:T(8,128)(2,1)} %get-tuple-element.21.points) | copy-start | bytes 1572868
  42.4 10.8 %copy-start.3 = (bf16[128,1024]{1,0:T(8,128)(2,1)S(1)}, bf16[128,1024]{1,0:T(8,128)(2,1)}, u32[]{:S(2)}) copy-start(bf16[128,1024]{1,0:T(8,128)(2,1)} %w_in.9) | copy-start | bytes 786436
  42.4 10.8 %copy-start.4 = (bf16[1024,128]{1,0:T(8,128)(2,1)S(1)}, bf16[1024,128]{1,0:T(8,128)(2,1)}, u32[]{:S(2)}) copy-start(bf16[1024,128]{1,0:T(8,128)(2,1)} %w_out.9) | copy-start | bytes 786436
  42.4 10.8 %copy-start.5 = (f32[1024]{0:T(1024)S(1)}, f32[1024]{0:T(1024)}, u32[]{:S(2)}) copy-start(f32[1024]{0:T(1024)} %param.9) | copy-start | bytes 12292
  42.4 10.8 %copy-start.6 = (f32[128]{0:T(128)S(1)}, f32[128]{0:T(128)}, u32[]{:S(2)}) copy-start(f32[128]{0:T(128)} %param.11) | copy-start | bytes 1540
  71.7 3.0 %collective-permute-start.7 = (f32[264,1024]{1,0:T(8,128)}, f32[264,1024]{1,0:T(8,128)S(1)}, u32[]{:S(2)}, u32[]{:S(2)}) collective-permute-start(f32[264,1024]{1,0:T(8,128)} %get-tuple-element.23), channel_id=1, source_target_pairs={{0,1},{1,0},{2,3},{3,2},{4,5},{5,4},{6,7},{7,6},{8,9},{9,8},{10,11... | collective-permute-start | bytes 3244040 | tf_op jit(solution)/shard_map/ppermute | solution.py:178

commit v2 on v0

--- a/solution.py
+++ b/solution.py
@@ -1,7 +1,22 @@
+import functools
+
 import jax
 import jax.numpy as jnp
 from jax import lax
+from jax.experimental import pallas as pl
+from jax.experimental.pallas import tpu as pltpu
 from jax.sharding import PartitionSpec as P
+
+F32 = jnp.float32
+BF16 = jnp.bfloat16
+LANES = 128
+GATHER_BYTES = 4 << 20
+NT = (((1,), (1,)), ((), ()))
+TN = (((0,), (0,)), ((), ()))
+
+
+def dot(a, b, dims=(((1,), (0,)), ((), ()))):
+    return lax.dot_general(a, b, dims, preferred_element_type=F32)
 
 
 def from_behind(value, axis, steps):
@@ -15,7 +30,197 @@
     return sig * (1.0 + pre * (1.0 - sig))
 
 
-def local(points, w_in, b_in, w_out, scales, left, right):
+VMEM = pl.BlockSpec(memory_space=pltpu.VMEM)
+
+
+def call(kernel, out, *args, scratch=(), flops=0, room=32 << 20):
+    return pl.pallas_call(
+        kernel,
+        out_shape=out,
+        in_specs=[VMEM] * len(args),
+        out_specs=jax.tree.map(lambda _: VMEM, out),
+        scratch_shapes=list(scratch),
+        compiler_params=pltpu.CompilerParams(vmem_limit_bytes=room),
+        cost_estimate=pl.CostEstimate(flops=flops, bytes_accessed=sum(a.size * a.dtype.itemsize for a in args), transcendentals=0),
+    )(*args)
+
+
+def tree(values):
+    while len(values) > 1:
+        values = [a + b for a, b in zip(values[::2], values[1::2])]
+    return values[0]
+
+
+def sigmoid(value):
+    return 0.5 * jnp.tanh(0.5 * value) + 0.5
+
+
+def pack_kernel(points, left, right, out, pts, solve, sems):
+    solves = left.shape[0]
+    pieces = ((points, pts), (left, solve.at[:solves]), (right, solve.at[solves:]))
+    copies = [pltpu.make_async_copy(source, target, sems.at[k]) for k, (source, target) in enumerate(pieces)]
+    for copy in copies:
+        copy.start()
+    for copy in copies:
+        copy.wait()
+    din = points.shape[1]
+    out[:, :din] = pts[...]
+    out[:, din:] = solve[...].T
+
+
+def plane_kernel(inner, *refs):
+    *parts, out = refs
+    rows = parts[0].shape[0]
+    mine = lax.axis_index("blk") // inner
+    for k, part in enumerate(parts):
+        out[pl.ds(pl.multiple_of((mine ^ k) * rows, rows), rows), :] = part[...]
+
+
+def half_norms(feats):
+    wide = feats.astype(F32)
+    return -0.5 * jnp.sum(wide * wide, axis=1, keepdims=True)
+
+
+def pair_terms(feat, step, home, visit, wanted):
+    half = (home[0].shape[1] - feat) // 2
+    across = {}
+    for k in sorted({k for _, k in wanted}):
+        norms = half_norms(visit[k][:, :feat])
+        across[k] = jnp.broadcast_to(norms, (norms.shape[0], LANES)).T[:1, :]
+    terms = {}
+    for i in sorted({i for i, _ in wanted}):
+        plane = home[i]
+        rows = plane.shape[0]
+        g = plane[:, :feat]
+        swapped = jnp.concatenate([plane[:, feat + half :], plane[:, feat : feat + half]], axis=1)
+        down = half_norms(g)
+        for k in sorted(k for h, k in wanted if h == i):
+            cols = visit[k]
+            term, ones = jnp.zeros((rows, feat), F32), jnp.zeros((rows, LANES), F32)
+            for at in range(0, cols.shape[0], step):
+                visit_g = cols[at : at + step, :feat]
+                kern = jnp.exp(dot(g, visit_g, NT) + down + across[k][:, at : at + step])
+                weight = dot(swapped, cols[at : at + step, feat:], NT) * kern
+                for lane in range(0, step, LANES):
+                    ones += weight[:, lane : lane + LANES]
+                term += dot(weight.astype(BF16), visit_g)
+            terms[i, k] = term - jnp.sum(ones, axis=1, keepdims=True) * g.astype(F32)
+    return terms
+
+
+def forward_kernel(raw, w_in, b_in, w_out, scales, out, hidden_out, slope_out):
+    din, feat = w_in.shape[0], w_out.shape[1]
+    pre = dot(raw[:, :din], w_in[...]) + b_in[...]
+    sig = sigmoid(pre)
+    wide = pre * sig
+    hidden = wide.astype(BF16)
+    hidden_out[...] = hidden
+    slope_out[...] = sig + wide * (1.0 - sig)
+    out[:, :feat] = (dot(hidden, w_out[...]) * scales[...]).astype(BF16)
+    out[:, feat:] = raw[:, din:]
+
+
+def own_kernel(planes, feat, step, wanted, keys, *refs):
+    own, held, outs = refs[:planes], dict(zip(keys, refs[planes : planes + len(keys)])), refs[planes + len(keys) :]
+    terms = {key: held[key][...] for key in keys} | pair_terms(feat, step, own, own, wanted)
+    for i, out in enumerate(outs):
+        out[...] = tree([terms[i, k] for k in range(planes)])
+
+
+def last_kernel(planes, inner, feat, step, factor, wanted, keys, *refs):
+    own, other, before, raw, hidden, slope = (refs[i * planes : (i + 1) * planes] for i in range(6))
+    held = dict(zip(keys, refs[6 * planes : 6 * planes + len(keys)]))
+    w_out, scales, feat_grad_out, part, mine_grad, sums = refs[6 * planes + len(keys) :]
+    rows = feat_grad_out.shape[0]
+    din = sums.shape[1] - feat - 8
+    for i in range(planes):
+        terms = {key: held[key][...] for key in keys if key[0] == i}
+        terms |= pair_terms(feat, step, own, other, [key for key in wanted if key[0] == i])
+        feat_grad = (before[i][...] + tree([terms[i, k] for k in range(planes)])) * scales[...]
+        if i == 0:
+            mine = lax.axis_index("blk") // inner
+            mine_grad[...] = feat_grad
+            feat_grad_out[...] = mine_grad[pl.ds(pl.multiple_of(mine * rows, rows), rows), :]
+        feat_grad_b = feat_grad.astype(BF16)
+        pre_grad = dot(feat_grad_b, w_out[...], NT) * slope[i][...]
+        sums[i, :din, :] = factor * dot(raw[i][:, :din], pre_grad.astype(BF16), TN)
+        sums[i, din : din + feat, :] = factor * dot(feat_grad_b, hidden[i][...], TN)
+        sums[i, din + feat :, :] = factor * jnp.sum(pre_grad.reshape(-1, 8, pre_grad.shape[1]), axis=0)
+    part[...] = tree([sums[i] for i in range(planes)])
+
+
+def join_kernel(mine, other, w_in_out, b_in_out, w_out_out):
+    din, feat = w_in_out.shape[0], w_out_out.shape[1]
+    w_in_out[...] = mine[:din, :] + other[:din, :]
+    w_out_out[...] = (mine[din : din + feat, :] + other[din : din + feat, :]).T
+    b_in_out[...] = jnp.sum(mine[din + feat :, :] + other[din + feat :, :], axis=0, keepdims=True)
+
+
+def swap(value, axis, bits):
+    count = lax.axis_size(axis)
+    return lax.ppermute(value, axis, [(source, source ^ bits) for source in range(count)])
+
+
+def gather_plan(inner, points, w_in, b_in, w_out, scales, left, right):
+    blocks = lax.axis_size("blk")
+    outer = blocks // inner
+    rows = points.shape[0]
+    size = rows * outer
+    b_in, scales = b_in[None, :], scales[None, :]
+    din, hid = w_in.shape
+    feat = w_out.shape[1]
+    width = feat + left.shape[1] + right.shape[1]
+    raw = pl.pallas_call(
+        pack_kernel,
+        out_shape=jax.ShapeDtypeStruct((rows, din + width - feat), BF16),
+        in_specs=[pl.BlockSpec(memory_space=pltpu.HBM)] * 3,
+        out_specs=VMEM,
+        scratch_shapes=[pltpu.VMEM((rows, din), BF16), pltpu.VMEM((width - feat, rows), BF16), pltpu.SemaphoreType.DMA((3,))],
+    )(points, left.T, right.T)
+    parts = [raw] + [swap(raw, "blk", inner * k) for k in range(1, outer)]
+    column = call(functools.partial(plane_kernel, inner), jax.ShapeDtypeStruct((size, raw.shape[1]), BF16), *parts)
+    raws = [column] + [swap(column, "blk", k) for k in range(1, inner)]
+    factor = (size * inner * lax.axis_size("row")) ** (-0.5)
+    step = min(size, 512)
+    flops = 6 * feat * size * size
+    grad_shape = jax.ShapeDtypeStruct((size, feat), F32)
+    own, other, hidden, slope = [], [], [], []
+    with_own, with_other = {}, {}
+    for k, plane in enumerate(raws):
+        shapes = [jax.ShapeDtypeStruct((size, width), BF16), jax.ShapeDtypeStruct((size, hid), BF16), jax.ShapeDtypeStruct((size, hid), F32)]
+        results = call(forward_kernel, shapes, plane, w_in, b_in, w_out, scales, flops=4 * size * w_in.size)
+        for store, result in zip((own, hidden, slope), results):
+            store.append(result)
+        other.append(swap(own[k], "row", 1))
+    everything = [(i, j) for i in range(inner) for j in range(inner)]
+    wanted = [key for key in everything if key not in with_own]
+    keys = list(with_own)
+    before = call(
+        functools.partial(own_kernel, inner, feat, step, wanted, keys),
+        [grad_shape] * inner,
+        *own,
+        *with_own.values(),
+        flops=flops * len(wanted),
+    )
+    wanted = [key for key in everything if key not in with_other]
+    keys = list(with_other)
+    feat_grad, part = call(
+        functools.partial(last_kernel, inner, inner, feat, step, factor, wanted, keys),
+        [jax.ShapeDtypeStruct((rows, feat), F32), jax.ShapeDtypeStruct((din + feat + 8, hid), F32)],
+        *own, *other, *before, *raws, *hidden, *slope, *with_other.values(), w_out, scales,
+        scratch=[pltpu.VMEM((size, feat), F32), pltpu.VMEM((inner, din + feat + 8, hid), F32)],
+        flops=flops * len(wanted),
+    )
+    grad_w_in, grad_b_in, grad_w_out = call(
+        join_kernel,
+        [jax.ShapeDtypeStruct(s, F32) for s in ((din, hid), (1, hid), (hid, feat))],
+        part,
+        swap(part, "row", 1),
+    )
+    return (feat_grad, grad_w_in, grad_b_in[0], grad_w_out)
+
+
+def ring_plan(points, w_in, b_in, w_out, scales, left, right):
     pre = jnp.dot(points, w_in, preferred_element_type=jnp.float32) + b_in
     hidden = jax.nn.silu(pre).astype(jnp.bfloat16)
     feats = jnp.dot(hidden, w_out, preferred_element_type=jnp.float32)
@@ -78,6 +283,16 @@
     return (feat_grad, factor * grad_w_in, factor * grad_b_in, factor * grad_w_out)
 
 
+def local(points, w_in, b_in, w_out, scales, left, right):
+    blocks, cores = lax.axis_size("blk"), lax.axis_size("row")
+    width = points.shape[1] + left.shape[1] + right.shape[1]
+    size = points.shape[0] * blocks * cores * width * points.dtype.itemsize
+    inner = min(4, blocks)
+    fits = size <= GATHER_BYTES and cores == 2 and blocks & (blocks - 1) == 0
+    plan = functools.partial(gather_plan, inner) if fits else ring_plan
+    return plan(points, w_in, b_in, w_out, scales, left, right)
+
+
 def solution(mesh):
     placed = (
         P(("blk", "row"), None),

time: 247 us -> 54 us (0.22)
  waiting for transfers between devices: 156 us -> 11.7 us
  blocking collectives: 44.6 us -> 0 us
  Pallas kernels: 0 us -> 25 us
  between operations: 14.2 us -> 0.78 us
  matrix products: 11 us -> 0 us
  other arithmetic: 4.49 us -> 0 us
    psum x1 -> x0, waiting for transfers between devices: 91.9 us -> none  [local(): lax.psum((part_w_in, part_b_in, part_w_out), ('blk', 'row'))]
    ppermute x25 -> x11, waiting for transfers between devices: 63.9 us -> 11.7 us  [swap(): lax.ppermute(value, axis, [(source, source ^ bits) for source in range(co...]
    psum x1 -> x0, blocking collectives: 40.8 us -> none  [local(): lax.psum((part_w_in, part_b_in, part_w_out), ('blk', 'row'))]
    pallas_call x0 -> x9, Pallas kernels: none -> 25 us  [the longest x8 23.5 us: call(): pl.pallas_call(kernel, out_shape=out, in_specs=[VMEM] * len(args), out_sp...]
    dot_general x40 -> x0, matrix products: 11 us -> none  [the longest x9 2.24 us: tile(): lax.dot_general(visit_ba, home_ab, contract, preferred_element_type=jnp.f...]
    all_gather x2 -> x0, blocking collectives: 3.82 us -> none  [the longest x1 1.96 us: local(): lax.all_gather(scaled, 'row', axis=0, tiled=True)]
    mul x4 -> x0, other arithmetic: 3.42 us -> none  [the longest x1 1.08 us: local(): factor * grad_w_in]
    unnamed x20 -> x18, local copies, waits for them, and re-layouts: 3.64 us -> 5.99 us
  transfers between devices with their start and end apart: 27 -> 11, of which waited for: 14 -> 5; matrix products, arithmetic and copies ran while one was open for 3% -> 0% of each run, Pallas kernels for 0% -> 22%
where the time goes in v2:
time: 54 us; the launch traced here: 53.6 us
  Pallas kernels  25 us (46%)
  waiting for transfers between devices  11.7 us (22%)
  starting transfers between devices  10.2 us (19%)
  local copies, waits for them, and re-layouts  5.99 us (11%)
  between operations  0.78 us (1%)
    pallas_call x8, Pallas kernels, call(): pl.pallas_call(kernel, out_shape=out, in_specs=[VMEM] * len(args), out_sp...  23.5 us
    ppermute x11, waiting for transfers between devices, swap(): lax.ppermute(value, axis, [(source, source ^ bits) for source in range(co...  11.7 us
    ppermute x11, starting transfers between devices, swap(): lax.ppermute(value, axis, [(source, source ^ bits) for source in range(co...  10.2 us
    unnamed x18, local copies, waits for them, and re-layouts  5.99 us
    pallas_call x1, Pallas kernels, gather_plan(): pl.pallas_call(pack_kernel, out_shape=jax.ShapeDtypeStruct((rows, din + w...  1.49 us
  transfers between devices with their start and end apart: 11, of which 5 were waited for; matrix products, arithmetic and copies ran while one was open for 0% of the time, Pallas kernels for 22%

profile of v2, /device:TPU:0, one launch (start us, length us, event | category | flops | bytes accessed | tf_op | source)
XLA Modules:
  0.0 53.6 jit_solution(9656960512781000428)
XLA Ops:
  0.6 1.5 %shard_map.102.refs_0_ = bf16[128,256]{1,0:T(8,128)(2,1)} custom-call(bf16[128,128]{1,0:T(8,128)(2,1)} %points.1, bf16[64,128]{1,0:T(8,128)(2,1)} %bitcast.14, bf16[64,128]{1,0:T(8,128)(2,1)} %bitcast.15), custom_call_target="tpu_custom_call" | custom-call | tf_op jit(solution)/shard_map/pallas_call | solution.py:173
  2.1 5.1 %collective-permute-start.2 = (bf16[128,256]{1,0:T(8,128)(2,1)}, bf16[128,256]{1,0:T(8,128)(2,1)S(1)}, u32[]{:S(2)}, u32[]{:S(2)}) collective-permute-start(bf16[128,256]{1,0:T(8,128)(2,1)} %shard_map.102.refs_0_), channel_id=1, source_target_pairs={{0,24},{2,26},{4,28},{6,30},{8,16},{10,18},{12,20},{14,22},{16,8},... | collective-permute-start | bytes 196616 | tf_op jit(solution)/shard_map/ppermute | solution.py:161
  7.2 0.6 %collective-permute-start = (bf16[128,256]{1,0:T(8,128)(2,1)}, bf16[128,256]{1,0:T(8,128)(2,1)S(1)}, u32[]{:S(2)}, u32[]{:S(2)}) collective-permute-start(bf16[128,256]{1,0:T(8,128)(2,1)} %shard_map.102.refs_0_), channel_id=1, source_target_pairs={{0,8},{2,10},{4,12},{6,14},{8,0},{10,2},{12,4},{14,6},{16,24},{18,... | collective-permute-start | bytes 196616 | tf_op jit(solution)/shard_map/ppermute | solution.py:161
  7.9 2.2 %collective-permute-done.2.refs_3_ = bf16[128,256]{1,0:T(8,128)(2,1)S(1)} collective-permute-done((bf16[128,256]{1,0:T(8,128)(2,1)}, bf16[128,256]{1,0:T(8,128)(2,1)S(1)}, u32[]{:S(2)}, u32[]{:S(2)}) %collective-permute-start.2) | collective-permute-done | bytes 65568 | tf_op jit(solution)/shard_map/ppermute | solution.py:161
  10.1 3.0 %collective-permute-done.1.refs_2_ = bf16[128,256]{1,0:T(8,128)(2,1)S(1)} collective-permute-done((bf16[128,256]{1,0:T(8,128)(2,1)}, bf16[128,256]{1,0:T(8,128)(2,1)S(1)}, u32[]{:S(2)}, u32[]{:S(2)}) %collective-permute-start.1) | collective-permute-done | bytes 65568 | tf_op jit(solution)/shard_map/ppermute | solution.py:161
  13.1 0.8 %copy-done.3 = bf16[128,256]{1,0:T(8,128)(2,1)S(1)} copy-done((bf16[128,256]{1,0:T(8,128)(2,1)S(1)}, bf16[128,256]{1,0:T(8,128)(2,1)}, u32[]{:S(2)}) %copy-start.3) | copy-done | bytes 65560
  13.9 1.6 %collective-permute-start.3 = (bf16[512,256]{1,0:T(8,128)(2,1)S(1)}, bf16[512,256]{1,0:T(8,128)(2,1)S(1)}, u32[]{:S(2)}, u32[]{:S(2)}) collective-permute-start(bf16[512,256]{1,0:T(8,128)(2,1)S(1)} %shard_map.103.raw.refs_12_), channel_id=1, source_target_pairs={{0,2},{2,0},{4,6},{6,4},{8,10},{10,8},{12,14},{14,12},{16,18},{18,... | collective-permute-start | bytes 786440 | tf_op jit(solution)/shard_map/ppermute | solution.py:161
  15.5 1.5 %collective-permute-start.4 = (bf16[512,256]{1,0:T(8,128)(2,1)S(1)}, bf16[512,256]{1,0:T(8,128)(2,1)S(1)}, u32[]{:S(2)}, u32[]{:S(2)}) collective-permute-start(bf16[512,256]{1,0:T(8,128)(2,1)S(1)} %shard_map.103.raw.refs_12_), channel_id=1, source_target_pairs={{0,4},{2,6},{4,0},{6,2},{8,12},{10,14},{12,8},{14,10},{16,20},{18,... | collective-permute-start | bytes 786440 | tf_op jit(solution)/shard_map/ppermute | solution.py:161
  17.0 0.5 collective-permute-start.5
  17.5 0.9 %copy-done = bf16[1024,128]{1,0:T(8,128)(2,1)S(1)} copy-done((bf16[1024,128]{1,0:T(8,128)(2,1)S(1)}, bf16[1024,128]{1,0:T(8,128)(2,1)}, u32[]{:S(2)}) %copy-start) | copy-done | bytes 262168
  18.4 0.7 %copy-done.4 = f32[128]{0:T(128)S(1)} copy-done((f32[128]{0:T(128)S(1)}, f32[128]{0:T(128)}, u32[]{:S(2)}) %copy-start.4) | copy-done | bytes 536
  19.1 0.9 %copy-done.6 = bf16[128,1024]{1,0:T(8,128)(2,1)S(1)} copy-done((bf16[128,1024]{1,0:T(8,128)(2,1)S(1)}, bf16[128,1024]{1,0:T(8,128)(2,1)}, u32[]{:S(2)}) %copy-start.6) | copy-done | bytes 262168
  20.0 0.7 %copy-done.8 = f32[1024]{0:T(1024)S(1)} copy-done((f32[1024]{0:T(1024)S(1)}, f32[1024]{0:T(1024)}, u32[]{:S(2)}) %copy-start.8) | copy-done | bytes 4120
  20.7 1.1 %shard_map.104 = (bf16[512,256]{1,0:T(8,128)(2,1)S(1)}, bf16[512,1024]{1,0:T(8,128)(2,1)S(1)}, f32[512,1024]{1,0:T(8,128)S(1)}) custom-call(bf16[512,256]{1,0:T(8,128)(2,1)S(1)} %shard_map.103.raw.refs_12_, bf16[128,1024]{1,0:T(8,128)(2,1)S(1)} %copy-done.6, f32[1,1024]{1,0:T(1,128)S(1)} %bitcast.10, bf16[1024,128]{1,0:T(8,128)(2,1)S(1)} %copy-done, ...), custom_call_target="tpu_custom_call" | custom-call | flops 268435456 | bytes 791040 | tf_op jit(solution)/shard_map/pallas_call | solution.py:37
  21.9 0.1 collective-permute-start.6
  22.0 1.3 %collective-permute-done.3.raw.refs_13_ = bf16[512,256]{1,0:T(8,128)(2,1)S(1)} collective-permute-done((bf16[512,256]{1,0:T(8,128)(2,1)S(1)}, bf16[512,256]{1,0:T(8,128)(2,1)S(1)}, u32[]{:S(2)}, u32[]{:S(2)}) %collective-permute-start.3) | collective-permute-done | bytes 262176 | tf_op jit(solution)/shard_map/ppermute | solution.py:161
  23.2 0.9 %copy-done.1 = bf16[1024,128]{1,0:T(8,128)(2,1)S(1)} copy-done((bf16[1024,128]{1,0:T(8,128)(2,1)S(1)}, bf16[1024,128]{1,0:T(8,128)(2,1)}, u32[]{:S(2)}) %copy-start.1) | copy-done | bytes 262168
  24.2 0.9 %copy-done.7 = bf16[128,1024]{1,0:T(8,128)(2,1)S(1)} copy-done((bf16[128,1024]{1,0:T(8,128)(2,1)S(1)}, bf16[128,1024]{1,0:T(8,128)(2,1)}, u32[]{:S(2)}) %copy-start.7) | copy-done | bytes 262168
  25.1 1.1 %shard_map.105 = (bf16[512,256]{1,0:T(8,128)(2,1)S(1)}, bf16[512,1024]{1,0:T(8,128)(2,1)S(1)}, f32[512,1024]{1,0:T(8,128)S(1)}) custom-call(bf16[512,256]{1,0:T(8,128)(2,1)S(1)} %collective-permute-done.3.raw.refs_13_, bf16[128,1024]{1,0:T(8,128)(2,1)S(1)} %copy-done.7, f32[1,1024]{1,0:T(1,128)S(1)} %bitcast.11, bf16[1024,128]{1,0:T(8,128)(2,1)S(1)} %copy-done.1, ...), custom_call_target="tpu_custom_call" | custom-call | flops 268435456 | bytes 791040 | tf_op jit(solution)/shard_map/pallas_call | solution.py:37
  26.3 0.1 collective-permute-start.7
  26.3 2.5 %collective-permute-done.4.raw.refs_14_ = bf16[512,256]{1,0:T(8,128)(2,1)S(1)} collective-permute-done((bf16[512,256]{1,0:T(8,128)(2,1)S(1)}, bf16[512,256]{1,0:T(8,128)(2,1)S(1)}, u32[]{:S(2)}, u32[]{:S(2)}) %collective-permute-start.4) | collective-permute-done | bytes 262176 | tf_op jit(solution)/shard_map/ppermute | solution.py:161
  28.9 1.1 %shard_map.106 = (bf16[512,256]{1,0:T(8,128)(2,1)S(1)}, bf16[512,1024]{1,0:T(8,128)(2,1)S(1)}, f32[512,1024]{1,0:T(8,128)S(1)}) custom-call(bf16[512,256]{1,0:T(8,128)(2,1)S(1)} %collective-permute-done.4.raw.refs_14_, bf16[128,1024]{1,0:T(8,128)(2,1)S(1)} %copy-done.7, f32[1,1024]{1,0:T(1,128)S(1)} %bitcast.12, bf16[1024,128]{1,0:T(8,128)(2,1)S(1)} %copy-done.1, ...), custom_call_target="tpu_custom_call" | custom-call | flops 268435456 | bytes 791040 | tf_op jit(solution)/shard_map/pallas_call | solution.py:37
  30.0 0.1 collective-permute-start.8
  30.1 1.1 %shard_map.107 = (bf16[512,256]{1,0:T(8,128)(2,1)S(1)}, bf16[512,1024]{1,0:T(8,128)(2,1)S(1)}, f32[512,1024]{1,0:T(8,128)S(1)}) custom-call(bf16[512,256]{1,0:T(8,128)(2,1)S(1)} %collective-permute-done.5.raw.refs_15_, bf16[128,1024]{1,0:T(8,128)(2,1)S(1)} %copy-done.7, f32[1,1024]{1,0:T(1,128)S(1)} %bitcast.13, bf16[1024,128]{1,0:T(8,128)(2,1)S(1)} %copy-done.1, ...), custom_call_target="tpu_custom_call" | custom-call | flops 268435456 | bytes 791040 | tf_op jit(solution)/shard_map/pallas_call | solution.py:37
  31.3 0.0 copy-start.2
  31.3 0.0 copy-start.5
  31.3 0.6 %collective-permute-start.9 = (bf16[512,256]{1,0:T(8,128)(2,1)S(1)}, bf16[512,256]{1,0:T(8,128)(2,1)S(1)}, u32[]{:S(2)}, u32[]{:S(2)}) collective-permute-start(bf16[512,256]{1,0:T(8,128)(2,1)S(1)} %get-tuple-element.28.refs_3_), channel_id=1, source_target_pairs={{0,1},{1,0},{2,3},{3,2},{4,5},{5,4},{6,7},{7,6},{8,9},{9,8},{10,11... | collective-permute-start | bytes 786440 | tf_op jit(solution)/shard_map/ppermute | solution.py:161
  31.9 7.2 %shard_map.108 = (f32[512,128]{1,0:T(8,128)S(1)}, f32[512,128]{1,0:T(8,128)S(1)}, f32[512,128]{1,0:T(8,128)S(1)}, f32[512,128]{1,0:T(8,128)S(1)}) custom-call(bf16[512,256]{1,0:T(8,128)(2,1)S(1)} %get-tuple-element.25.refs_0_, bf16[512,256]{1,0:T(8,128)(2,1)S(1)} %get-tuple-element.26.refs_1_, bf16[512,256]{1,0:T(8,128)(2,1)S(1)} %get-tuple-element.27.refs_2_, ...), custom_call_target="tpu_custom_call" | custom-call | flops 3221225472 | bytes 1048576 | tf_op jit(solution)/shard_map/pallas_call | solution.py:37
  39.1 10.5 %shard_map.109 = (f32[128,128]{1,0:T(8,128)}, f32[264,1024]{1,0:T(8,128)S(1)}) custom-call(bf16[512,256]{1,0:T(8,128)(2,1)S(1)} %get-tuple-element.25.refs_0_, bf16[512,256]{1,0:T(8,128)(2,1)S(1)} %get-tuple-element.26.refs_1_, bf16[512,256]{1,0:T(8,128)(2,1)S(1)} %get-tuple-element.27.refs_2_, bf16[512,256]{1,0:T(8,128)(2,1)S(1)} %get-tuple-element.28.refs_3_, ...), custom_call_target="tpu_custom_call" | custom-call | flops 3221225472 | bytes 17039872 | tf_op jit(solution)/shard_map/pallas_call | solution.py:37
  49.6 0.1 collective-permute-start.10
  49.7 2.7 %collective-permute-done.10.other = f32[264,1024]{1,0:T(8,128)S(1)} collective-permute-done((f32[264,1024]{1,0:T(8,128)S(1)}, f32[264,1024]{1,0:T(8,128)S(1)}, u32[]{:S(2)}, u32[]{:S(2)}) %collective-permute-start.10) | collective-permute-done | bytes 1081376 | tf_op jit(solution)/shard_map/ppermute | solution.py:161
  52.4 1.2 %shard_map.110 = (f32[128,1024]{1,0:T(8,128)}, f32[1,1024]{1,0:T(1,128)}, f32[1024,128]{1,0:T(8,128)}) custom-call(f32[264,1024]{1,0:T(8,128)S(1)} %get-tuple-element.42.mine, f32[264,1024]{1,0:T(8,128)S(1)} %collective-permute-done.10.other), custom_call_target="tpu_custom_call" | custom-call | bytes 2162688 | tf_op jit(solution)/shard_map/pallas_call | solution.py:37
  (17 shorter events, 0.1 us)
Async XLA Ops:
  2.1 7.9 %collective-permute-start.2 = (bf16[128,256]{1,0:T(8,128)(2,1)}, bf16[128,256]{1,0:T(8,128)(2,1)S(1)}, u32[]{:S(2)}, u32[]{:S(2)}) collective-permute-start(bf16[128,256]{1,0:T(8,128)(2,1)} %shard_map.102.refs_0_), channel_id=1, source_target_pairs={{0,24},{2,26},{4,28},{6,30},{8,16},{10,18},{12,20},{14,22},{16,8},... | collective-permute-start | bytes 196616 | tf_op jit(solution)/shard_map/ppermute | solution.py:161
  7.2 5.8 %collective-permute-start.1 = (bf16[128,256]{1,0:T(8,128)(2,1)}, bf16[128,256]{1,0:T(8,128)(2,1)S(1)}, u32[]{:S(2)}, u32[]{:S(2)}) collective-permute-start(bf16[128,256]{1,0:T(8,128)(2,1)} %shard_map.102.refs_0_), channel_id=1, source_target_pairs={{0,16},{2,18},{4,20},{6,22},{8,24},{10,26},{12,28},{14,30},{16,0},... | collective-permute-start | bytes 196616 | tf_op jit(solution)/shard_map/ppermute | solution.py:161
  7.2 5.8 %collective-permute-start = (bf16[128,256]{1,0:T(8,128)(2,1)}, bf16[128,256]{1,0:T(8,128)(2,1)S(1)}, u32[]{:S(2)}, u32[]{:S(2)}) collective-permute-start(bf16[128,256]{1,0:T(8,128)(2,1)} %shard_map.102.refs_0_), channel_id=1, source_target_pairs={{0,8},{2,10},{4,12},{6,14},{8,0},{10,2},{12,4},{14,6},{16,24},{18,... | collective-permute-start | bytes 196616 | tf_op jit(solution)/shard_map/ppermute | solution.py:161
  13.1 0.8 %copy-start.3 = (bf16[128,256]{1,0:T(8,128)(2,1)S(1)}, bf16[128,256]{1,0:T(8,128)(2,1)}, u32[]{:S(2)}) copy-start(bf16[128,256]{1,0:T(8,128)(2,1)} %shard_map.102.refs_0_) | copy-start | bytes 196612
  13.9 9.3 %collective-permute-start.3 = (bf16[512,256]{1,0:T(8,128)(2,1)S(1)}, bf16[512,256]{1,0:T(8,128)(2,1)S(1)}, u32[]{:S(2)}, u32[]{:S(2)}) collective-permute-start(bf16[512,256]{1,0:T(8,128)(2,1)S(1)} %shard_map.103.raw.refs_12_), channel_id=1, source_target_pairs={{0,2},{2,0},{4,6},{6,4},{8,10},{10,8},{12,14},{14,12},{16,18},{18,... | collective-permute-start | bytes 786440 | tf_op jit(solution)/shard_map/ppermute | solution.py:161
  15.5 13.4 %collective-permute-start.4 = (bf16[512,256]{1,0:T(8,128)(2,1)S(1)}, bf16[512,256]{1,0:T(8,128)(2,1)S(1)}, u32[]{:S(2)}, u32[]{:S(2)}) collective-permute-start(bf16[512,256]{1,0:T(8,128)(2,1)S(1)} %shard_map.103.raw.refs_12_), channel_id=1, source_target_pairs={{0,4},{2,6},{4,0},{6,2},{8,12},{10,14},{12,8},{14,10},{16,20},{18,... | collective-permute-start | bytes 786440 | tf_op jit(solution)/shard_map/ppermute | solution.py:161
  17.0 13.1 %collective-permute-start.5 = (bf16[512,256]{1,0:T(8,128)(2,1)S(1)}, bf16[512,256]{1,0:T(8,128)(2,1)S(1)}, u32[]{:S(2)}, u32[]{:S(2)}) collective-permute-start(bf16[512,256]{1,0:T(8,128)(2,1)S(1)} %shard_map.103.raw.refs_12_), channel_id=1, source_target_pairs={{0,6},{2,4},{4,2},{6,0},{8,14},{10,12},{12,10},{14,8},{16,22},{18,... | collective-permute-start | bytes 786440 | tf_op jit(solution)/shard_map/ppermute | solution.py:161
  17.5 0.9 %copy-start = (bf16[1024,128]{1,0:T(8,128)(2,1)S(1)}, bf16[1024,128]{1,0:T(8,128)(2,1)}, u32[]{:S(2)}) copy-start(bf16[1024,128]{1,0:T(8,128)(2,1)} %refs_24_.1) | copy-start | bytes 786436
  18.4 0.7 %copy-start.4 = (f32[128]{0:T(128)S(1)}, f32[128]{0:T(128)}, u32[]{:S(2)}) copy-start(f32[128]{0:T(128)} %param.11) | copy-start | bytes 1540
  19.1 0.9 %copy-start.6 = (bf16[128,1024]{1,0:T(8,128)(2,1)S(1)}, bf16[128,1024]{1,0:T(8,128)(2,1)}, u32[]{:S(2)}) copy-start(bf16[128,1024]{1,0:T(8,128)(2,1)} %w_in.7) | copy-start | bytes 786436
  20.0 0.7 %copy-start.8 = (f32[1024]{0:T(1024)S(1)}, f32[1024]{0:T(1024)}, u32[]{:S(2)}) copy-start(f32[1024]{0:T(1024)} %param.9) | copy-start | bytes 12292
  21.9 17.1 %collective-permute-start.6 = (bf16[512,256]{1,0:T(8,128)(2,1)S(1)}, bf16[512,256]{1,0:T(8,128)(2,1)S(1)}, u32[]{:S(2)}, u32[]{:S(2)}) collective-permute-start(bf16[512,256]{1,0:T(8,128)(2,1)S(1)} %get-tuple-element.25.refs_0_), channel_id=1, source_target_pairs={{0,1},{1,0},{2,3},{3,2},{4,5},{5,4},{6,7},{7,6},{8,9},{9,8},{10,11... | collective-permute-start | bytes 786440 | tf_op jit(solution)/shard_map/ppermute | solution.py:161
  23.2 1.0 %copy-start.1 = (bf16[1024,128]{1,0:T(8,128)(2,1)S(1)}, bf16[1024,128]{1,0:T(8,128)(2,1)}, u32[]{:S(2)}) copy-start(bf16[1024,128]{1,0:T(8,128)(2,1)} %refs_24_.1) | copy-start | bytes 786436
  24.2 0.9 %copy-start.7 = (bf16[128,1024]{1,0:T(8,128)(2,1)S(1)}, bf16[128,1024]{1,0:T(8,128)(2,1)}, u32[]{:S(2)}) copy-start(bf16[128,1024]{1,0:T(8,128)(2,1)} %w_in.7) | copy-start | bytes 786436
  26.3 12.8 %collective-permute-start.7 = (bf16[512,256]{1,0:T(8,128)(2,1)S(1)}, bf16[512,256]{1,0:T(8,128)(2,1)S(1)}, u32[]{:S(2)}, u32[]{:S(2)}) collective-permute-start(bf16[512,256]{1,0:T(8,128)(2,1)S(1)} %get-tuple-element.26.refs_1_), channel_id=1, source_target_pairs={{0,1},{1,0},{2,3},{3,2},{4,5},{5,4},{6,7},{7,6},{8,9},{9,8},{10,11... | collective-permute-start | bytes 786440 | tf_op jit(solution)/shard_map/ppermute | solution.py:161
  30.0 9.0 %collective-permute-start.8 = (bf16[512,256]{1,0:T(8,128)(2,1)S(1)}, bf16[512,256]{1,0:T(8,128)(2,1)S(1)}, u32[]{:S(2)}, u32[]{:S(2)}) collective-permute-start(bf16[512,256]{1,0:T(8,128)(2,1)S(1)} %get-tuple-element.27.refs_2_), channel_id=1, source_target_pairs={{0,1},{1,0},{2,3},{3,2},{4,5},{5,4},{6,7},{7,6},{8,9},{9,8},{10,11... | collective-permute-start | bytes 786440 | tf_op jit(solution)/shard_map/ppermute | solution.py:161
  31.3 7.8 %copy-start.2 = (bf16[1024,128]{1,0:T(8,128)(2,1)S(1)}, bf16[1024,128]{1,0:T(8,128)(2,1)}, u32[]{:S(2)}) copy-start(bf16[1024,128]{1,0:T(8,128)(2,1)} %refs_24_.1) | copy-start | bytes 786436
  31.3 7.8 %copy-start.5 = (f32[128]{0:T(128)S(1)}, f32[128]{0:T(128)}, u32[]{:S(2)}) copy-start(f32[128]{0:T(128)} %param.11) | copy-start | bytes 1540
  31.3 7.8 %collective-permute-start.9 = (bf16[512,256]{1,0:T(8,128)(2,1)S(1)}, bf16[512,256]{1,0:T(8,128)(2,1)S(1)}, u32[]{:S(2)}, u32[]{:S(2)}) collective-permute-start(bf16[512,256]{1,0:T(8,128)(2,1)S(1)} %get-tuple-element.28.refs_3_), channel_id=1, source_target_pairs={{0,1},{1,0},{2,3},{3,2},{4,5},{5,4},{6,7},{7,6},{8,9},{9,8},{10,11... | collective-permute-start | bytes 786440 | tf_op jit(solution)/shard_map/ppermute | solution.py:161
  49.6 2.8 %collective-permute-start.10 = (f32[264,1024]{1,0:T(8,128)S(1)}, f32[264,1024]{1,0:T(8,128)S(1)}, u32[]{:S(2)}, u32[]{:S(2)}) collective-permute-start(f32[264,1024]{1,0:T(8,128)S(1)} %get-tuple-element.42.mine), channel_id=1, source_target_pairs={{0,1},{1,0},{2,3},{3,2},{4,5},{5,4},{6,7},{7,6},{8,9},{9,8},{10,11... | collective-permute-start | bytes 3244040 | tf_op jit(solution)/shard_map/ppermute | solution.py:161

commit v3 on v2

--- a/solution.py
+++ b/solution.py
@@ -55,57 +55,14 @@
     return 0.5 * jnp.tanh(0.5 * value) + 0.5
 
 
-def pack_kernel(points, left, right, out, pts, solve, sems):
-    solves = left.shape[0]
-    pieces = ((points, pts), (left, solve.at[:solves]), (right, solve.at[solves:]))
-    copies = [pltpu.make_async_copy(source, target, sems.at[k]) for k, (source, target) in enumerate(pieces)]
-    for copy in copies:
-        copy.start()
-    for copy in copies:
-        copy.wait()
-    din = points.shape[1]
-    out[:, :din] = pts[...]
-    out[:, din:] = solve[...].T
-
-
-def plane_kernel(inner, *refs):
+def plane_kernel(inner, rows, *refs):
     *parts, out = refs
-    rows = parts[0].shape[0]
+    din = parts[0].shape[1]
     mine = lax.axis_index("blk") // inner
     for k, part in enumerate(parts):
-        out[pl.ds(pl.multiple_of((mine ^ k) * rows, rows), rows), :] = part[...]
-
-
-def half_norms(feats):
-    wide = feats.astype(F32)
-    return -0.5 * jnp.sum(wide * wide, axis=1, keepdims=True)
-
-
-def pair_terms(feat, step, home, visit, wanted):
-    half = (home[0].shape[1] - feat) // 2
-    across = {}
-    for k in sorted({k for _, k in wanted}):
-        norms = half_norms(visit[k][:, :feat])
-        across[k] = jnp.broadcast_to(norms, (norms.shape[0], LANES)).T[:1, :]
-    terms = {}
-    for i in sorted({i for i, _ in wanted}):
-        plane = home[i]
-        rows = plane.shape[0]
-        g = plane[:, :feat]
-        swapped = jnp.concatenate([plane[:, feat + half :], plane[:, feat : feat + half]], axis=1)
-        down = half_norms(g)
-        for k in sorted(k for h, k in wanted if h == i):
-            cols = visit[k]
-            term, ones = jnp.zeros((rows, feat), F32), jnp.zeros((rows, LANES), F32)
-            for at in range(0, cols.shape[0], step):
-                visit_g = cols[at : at + step, :feat]
-                kern = jnp.exp(dot(g, visit_g, NT) + down + across[k][:, at : at + step])
-                weight = dot(swapped, cols[at : at + step, feat:], NT) * kern
-                for lane in range(0, step, LANES):
-                    ones += weight[:, lane : lane + LANES]
-                term += dot(weight.astype(BF16), visit_g)
-            terms[i, k] = term - jnp.sum(ones, axis=1, keepdims=True) * g.astype(F32)
-    return terms
+        place = pl.ds(pl.multiple_of((mine ^ k) * rows, rows), rows)
+        out[place, :din] = part[:rows, :]
+        out[place, din:] = part[rows:, :].T
 
 
 def forward_kernel(raw, w_in, b_in, w_out, scales, out, hidden_out, slope_out):
@@ -120,23 +77,50 @@
     out[:, feat:] = raw[:, din:]
 
 
-def own_kernel(planes, feat, step, wanted, keys, *refs):
-    own, held, outs = refs[:planes], dict(zip(keys, refs[planes : planes + len(keys)])), refs[planes + len(keys) :]
-    terms = {key: held[key][...] for key in keys} | pair_terms(feat, step, own, own, wanted)
-    for i, out in enumerate(outs):
-        out[...] = tree([terms[i, k] for k in range(planes)])
-
-
-def last_kernel(planes, inner, feat, step, factor, wanted, keys, *refs):
-    own, other, before, raw, hidden, slope = (refs[i * planes : (i + 1) * planes] for i in range(6))
-    held = dict(zip(keys, refs[6 * planes : 6 * planes + len(keys)]))
-    w_out, scales, feat_grad_out, part, mine_grad, sums = refs[6 * planes + len(keys) :]
+def half_norms(feats):
+    wide = feats.astype(F32)
+    return -0.5 * jnp.sum(wide * wide, axis=1, keepdims=True)
+
+
+def visit_all(inner, visit, feat, cols, cols_g):
+    size = visit[0].shape[0]
+    mine = lax.axis_index("blk") % inner
+    for k, plane in enumerate(visit):
+        cols[pl.ds(pl.multiple_of((mine ^ k) * size, size), size), :] = plane[...]
+    cols_g[...] = cols[:, :feat].T
+
+
+def pair_sums(plane, feat, step, cols, cols_g):
+    half = (plane.shape[1] - feat) // 2
+    rows = plane.shape[0]
+    g = plane[:, :feat]
+    swapped = jnp.concatenate([plane[:, feat + half :], plane[:, feat : feat + half]], axis=1)
+    across = jnp.broadcast_to(half_norms(g), (rows, LANES)).T[:1, :]
+    total, sums = jnp.zeros((feat, rows), F32), jnp.zeros((8, rows), F32)
+    for at in range(0, cols.shape[0], step):
+        visit_g = cols[at : at + step, :feat]
+        kern = jnp.exp(dot(visit_g, g, NT) + half_norms(visit_g) + across)
+        weight = dot(cols[at : at + step, feat:], swapped, NT) * kern
+        sums += jnp.sum(weight.reshape(step // 8, 8, rows), axis=0)
+        total += dot(cols_g[:, at : at + step], weight.astype(BF16))
+    return total - jnp.sum(sums, axis=0, keepdims=True) * g.astype(F32).T
+
+
+def own_kernel(inner, feat, step, *refs):
+    own, outs, (cols, cols_g) = refs[:inner], refs[inner:-2], refs[-2:]
+    visit_all(inner, own, feat, cols, cols_g)
+    for plane, out in zip(own, outs):
+        out[...] = pair_sums(plane, feat, step, cols, cols_g)
+
+
+def last_kernel(inner, feat, step, factor, *refs):
+    own, other, before, raw, hidden, slope = (refs[i * inner : (i + 1) * inner] for i in range(6))
+    w_out, scales, feat_grad_out, part, mine_grad, sums, cols, cols_g = refs[6 * inner :]
     rows = feat_grad_out.shape[0]
     din = sums.shape[1] - feat - 8
-    for i in range(planes):
-        terms = {key: held[key][...] for key in keys if key[0] == i}
-        terms |= pair_terms(feat, step, own, other, [key for key in wanted if key[0] == i])
-        feat_grad = (before[i][...] + tree([terms[i, k] for k in range(planes)])) * scales[...]
+    visit_all(inner, other, feat, cols, cols_g)
+    for i in range(inner):
+        feat_grad = (before[i][...] + pair_sums(own[i], feat, step, cols, cols_g)).T * scales[...]
         if i == 0:
             mine = lax.axis_index("blk") // inner
             mine_grad[...] = feat_grad
@@ -146,7 +130,7 @@
         sums[i, :din, :] = factor * dot(raw[i][:, :din], pre_grad.astype(BF16), TN)
         sums[i, din : din + feat, :] = factor * dot(feat_grad_b, hidden[i][...], TN)
         sums[i, din + feat :, :] = factor * jnp.sum(pre_grad.reshape(-1, 8, pre_grad.shape[1]), axis=0)
-    part[...] = tree([sums[i] for i in range(planes)])
+    part[...] = tree([sums[i] for i in range(inner)])
 
 
 def join_kernel(mine, other, w_in_out, b_in_out, w_out_out):
@@ -170,46 +154,29 @@
     din, hid = w_in.shape
     feat = w_out.shape[1]
     width = feat + left.shape[1] + right.shape[1]
-    raw = pl.pallas_call(
-        pack_kernel,
-        out_shape=jax.ShapeDtypeStruct((rows, din + width - feat), BF16),
-        in_specs=[pl.BlockSpec(memory_space=pltpu.HBM)] * 3,
-        out_specs=VMEM,
-        scratch_shapes=[pltpu.VMEM((rows, din), BF16), pltpu.VMEM((width - feat, rows), BF16), pltpu.SemaphoreType.DMA((3,))],
-    )(points, left.T, right.T)
+    raw = jnp.concatenate([points, left.T, right.T], axis=0)
     parts = [raw] + [swap(raw, "blk", inner * k) for k in range(1, outer)]
-    column = call(functools.partial(plane_kernel, inner), jax.ShapeDtypeStruct((size, raw.shape[1]), BF16), *parts)
+    column = call(functools.partial(plane_kernel, inner, rows), jax.ShapeDtypeStruct((size, din + width - feat), BF16), *parts)
     raws = [column] + [swap(column, "blk", k) for k in range(1, inner)]
     factor = (size * inner * lax.axis_size("row")) ** (-0.5)
-    step = min(size, 512)
-    flops = 6 * feat * size * size
-    grad_shape = jax.ShapeDtypeStruct((size, feat), F32)
+    step = min(size * inner, 2048)
+    flops = 6 * feat * (size * inner) ** 2
+    grad_shape = jax.ShapeDtypeStruct((feat, size), F32)
     own, other, hidden, slope = [], [], [], []
-    with_own, with_other = {}, {}
     for k, plane in enumerate(raws):
         shapes = [jax.ShapeDtypeStruct((size, width), BF16), jax.ShapeDtypeStruct((size, hid), BF16), jax.ShapeDtypeStruct((size, hid), F32)]
         results = call(forward_kernel, shapes, plane, w_in, b_in, w_out, scales, flops=4 * size * w_in.size)
         for store, result in zip((own, hidden, slope), results):
             store.append(result)
         other.append(swap(own[k], "row", 1))
-    everything = [(i, j) for i in range(inner) for j in range(inner)]
-    wanted = [key for key in everything if key not in with_own]
-    keys = list(with_own)
-    before = call(
-        functools.partial(own_kernel, inner, feat, step, wanted, keys),
-        [grad_shape] * inner,
-        *own,
-        *with_own.values(),
-        flops=flops * len(wanted),
-    )
-    wanted = [key for key in everything if key not in with_other]
-    keys = list(with_other)
+    together = [pltpu.VMEM((size * inner, width), BF16), pltpu.VMEM((feat, size * inner), BF16)]
+    before = call(functools.partial(own_kernel, inner, feat, step), [grad_shape] * inner, *own, scratch=together, flops=flops)
     feat_grad, part = call(
-        functools.partial(last_kernel, inner, inner, feat, step, factor, wanted, keys),
+        functools.partial(last_kernel, inner, feat, step, factor),
         [jax.ShapeDtypeStruct((rows, feat), F32), jax.ShapeDtypeStruct((din + feat + 8, hid), F32)],
-        *own, *other, *before, *raws, *hidden, *slope, *with_other.values(), w_out, scales,
-        scratch=[pltpu.VMEM((size, feat), F32), pltpu.VMEM((inner, din + feat + 8, hid), F32)],
-        flops=flops * len(wanted),
+        *own, *other, *before, *raws, *hidden, *slope, w_out, scales,
+        scratch=[pltpu.VMEM((size, feat), F32), pltpu.VMEM((inner, din + feat + 8, hid), F32), *together],
+        flops=flops,
     )
     grad_w_in, grad_b_in, grad_w_out = call(
         join_kernel,
@@ -288,7 +255,7 @@
     width = points.shape[1] + left.shape[1] + right.shape[1]
     size = points.shape[0] * blocks * cores * width * points.dtype.itemsize
     inner = min(4, blocks)
-    fits = size <= GATHER_BYTES and cores == 2 and blocks & (blocks - 1) == 0
+    fits = size <= GATHER_BYTES and cores == 2 and blocks & (blocks - 1) == 0 and points.shape[0] == points.shape[1]
     plan = functools.partial(gather_plan, inner) if fits else ring_plan
     return plan(points, w_in, b_in, w_out, scales, left, right)
 

time: 54 us -> 51.5 us (0.954)
  Pallas kernels: 25 us -> 22.8 us
  local copies, waits for them, and re-layouts: 5.99 us -> 5.15 us
  other arithmetic: 0 us -> 0.8 us
    pallas_call x1 -> x0, Pallas kernels: 1.49 us -> none  [gather_plan(): pl.pallas_call(pack_kernel, out_shape=jax.ShapeDtypeStruct((rows, din + w...]
    unnamed x18 -> x16, local copies, waits for them, and re-layouts: 5.99 us -> 5.15 us
    concatenate x0 -> x1, other arithmetic: none -> 0.8 us  [gather_plan(): raw = jnp.concatenate([points, left.T, right.T], axis=0)]
    pallas_call x8, Pallas kernels: 23.5 us -> 22.8 us  [call(): pl.pallas_call(kernel, out_shape=out, in_specs=[VMEM] * len(args), out_sp...]
where the time goes in v3:
time: 51.5 us; the launch traced here: 51.1 us
  Pallas kernels  22.8 us (44%)
  waiting for transfers between devices  11.5 us (22%)
  starting transfers between devices  10.1 us (20%)
  local copies, waits for them, and re-layouts  5.15 us (10%)
  other arithmetic  0.8 us (2%)
  between operations  0.78 us (2%)
    pallas_call x8, Pallas kernels, call(): pl.pallas_call(kernel, out_shape=out, in_specs=[VMEM] * len(args), out_sp...  22.8 us
    ppermute x11, waiting for transfers between devices, swap(): lax.ppermute(value, axis, [(source, source ^ bits) for source in range(co...  11.5 us
    ppermute x11, starting transfers between devices, swap(): lax.ppermute(value, axis, [(source, source ^ bits) for source in range(co...  10.1 us
    unnamed x16, local copies, waits for them, and re-layouts  5.15 us
  transfers between devices with their start and end apart: 11, of which 5 were waited for; matrix products, arithmetic and copies ran while one was open for 0% of the time, Pallas kernels for 22%

profile of v3, /device:TPU:0, one launch (start us, length us, event | category | flops | bytes accessed | tf_op | source)
XLA Modules:
  0.0 51.1 jit_solution(6740453381098217278)
XLA Ops:
  0.6 0.8 %pad_maximum_fusion.refs_0_ = bf16[256,128]{1,0:T(8,128)(2,1)S(1)} fusion(bf16[64,128]{1,0:T(8,128)(2,1)} %bitcast.14, bf16[64,128]{1,0:T(8,128)(2,1)} %bitcast.15, bf16[128,128]{1,0:T(8,128)(2,1)} %param.7), kind=kLoop, calls=%fused_computation | loop fusion | flops 196608 | bytes 131072 | tf_op jit(solution)/shard_map/concatenate | solution.py:157
  1.4 5.0 %collective-permute-start.2 = (bf16[256,128]{1,0:T(8,128)(2,1)S(1)}, bf16[256,128]{1,0:T(8,128)(2,1)S(1)}, u32[]{:S(2)}, u32[]{:S(2)}) collective-permute-start(bf16[256,128]{1,0:T(8,128)(2,1)S(1)} %pad_maximum_fusion.refs_0_), channel_id=1, source_target_pairs={{0,24},{2,26},{4,28},{6,30},{8,16},{10,18},{12,20},{14,22},{16,8},... | collective-permute-start | bytes 196616 | tf_op jit(solution)/shard_map/ppermute | solution.py:145
  6.5 0.6 %collective-permute-start = (bf16[256,128]{1,0:T(8,128)(2,1)S(1)}, bf16[256,128]{1,0:T(8,128)(2,1)S(1)}, u32[]{:S(2)}, u32[]{:S(2)}) collective-permute-start(bf16[256,128]{1,0:T(8,128)(2,1)S(1)} %pad_maximum_fusion.refs_0_), channel_id=1, source_target_pairs={{0,8},{2,10},{4,12},{6,14},{8,0},{10,2},{12,4},{14,6},{16,24},{18,... | collective-permute-start | bytes 196616 | tf_op jit(solution)/shard_map/ppermute | solution.py:145
  7.1 1.9 %collective-permute-done.2.refs_3_ = bf16[256,128]{1,0:T(8,128)(2,1)S(1)} collective-permute-done((bf16[256,128]{1,0:T(8,128)(2,1)S(1)}, bf16[256,128]{1,0:T(8,128)(2,1)S(1)}, u32[]{:S(2)}, u32[]{:S(2)}) %collective-permute-start.2) | collective-permute-done | bytes 65568 | tf_op jit(solution)/shard_map/ppermute | solution.py:145
  9.0 3.0 %collective-permute-done.1.refs_2_ = bf16[256,128]{1,0:T(8,128)(2,1)S(1)} collective-permute-done((bf16[256,128]{1,0:T(8,128)(2,1)S(1)}, bf16[256,128]{1,0:T(8,128)(2,1)S(1)}, u32[]{:S(2)}, u32[]{:S(2)}) %collective-permute-start.1) | collective-permute-done | bytes 65568 | tf_op jit(solution)/shard_map/ppermute | solution.py:145
  12.1 0.1 shard_map.102.raw.refs_12_
  12.2 1.6 %collective-permute-start.3 = (bf16[512,256]{1,0:T(8,128)(2,1)S(1)}, bf16[512,256]{1,0:T(8,128)(2,1)S(1)}, u32[]{:S(2)}, u32[]{:S(2)}) collective-permute-start(bf16[512,256]{1,0:T(8,128)(2,1)S(1)} %shard_map.102.raw.refs_12_), channel_id=1, source_target_pairs={{0,2},{2,0},{4,6},{6,4},{8,10},{10,8},{12,14},{14,12},{16,18},{18,... | collective-permute-start | bytes 786440 | tf_op jit(solution)/shard_map/ppermute | solution.py:145
  13.7 1.5 %collective-permute-start.4 = (bf16[512,256]{1,0:T(8,128)(2,1)S(1)}, bf16[512,256]{1,0:T(8,128)(2,1)S(1)}, u32[]{:S(2)}, u32[]{:S(2)}) collective-permute-start(bf16[512,256]{1,0:T(8,128)(2,1)S(1)} %shard_map.102.raw.refs_12_), channel_id=1, source_target_pairs={{0,4},{2,6},{4,0},{6,2},{8,12},{10,14},{12,8},{14,10},{16,20},{18,... | collective-permute-start | bytes 786440 | tf_op jit(solution)/shard_map/ppermute | solution.py:145
  15.3 0.5 collective-permute-start.5
  15.7 0.9 %copy-done = bf16[1024,128]{1,0:T(8,128)(2,1)S(1)} copy-done((bf16[1024,128]{1,0:T(8,128)(2,1)S(1)}, bf16[1024,128]{1,0:T(8,128)(2,1)}, u32[]{:S(2)}) %copy-start) | copy-done | bytes 262168
  16.7 0.7 %copy-done.3 = f32[128]{0:T(128)S(1)} copy-done((f32[128]{0:T(128)S(1)}, f32[128]{0:T(128)}, u32[]{:S(2)}) %copy-start.3) | copy-done | bytes 536
  17.3 0.9 %copy-done.5 = bf16[128,1024]{1,0:T(8,128)(2,1)S(1)} copy-done((bf16[128,1024]{1,0:T(8,128)(2,1)S(1)}, bf16[128,1024]{1,0:T(8,128)(2,1)}, u32[]{:S(2)}) %copy-start.5) | copy-done | bytes 262168
  18.3 0.7 %copy-done.7 = f32[1024]{0:T(1024)S(1)} copy-done((f32[1024]{0:T(1024)S(1)}, f32[1024]{0:T(1024)}, u32[]{:S(2)}) %copy-start.7) | copy-done | bytes 4120
  19.0 1.1 %shard_map.103 = (bf16[512,256]{1,0:T(8,128)(2,1)S(1)}, bf16[512,1024]{1,0:T(8,128)(2,1)S(1)}, f32[512,1024]{1,0:T(8,128)S(1)}) custom-call(bf16[512,256]{1,0:T(8,128)(2,1)S(1)} %shard_map.102.raw.refs_12_, bf16[128,1024]{1,0:T(8,128)(2,1)S(1)} %copy-done.5, f32[1,1024]{1,0:T(1,128)S(1)} %bitcast.10, bf16[1024,128]{1,0:T(8,128)(2,1)S(1)} %copy-done, ...), custom_call_target="tpu_custom_call" | custom-call | flops 268435456 | bytes 791040 | tf_op jit(solution)/shard_map/pallas_call | solution.py:37
  20.1 0.1 collective-permute-start.6
  20.2 1.3 %collective-permute-done.3.raw.refs_13_ = bf16[512,256]{1,0:T(8,128)(2,1)S(1)} collective-permute-done((bf16[512,256]{1,0:T(8,128)(2,1)S(1)}, bf16[512,256]{1,0:T(8,128)(2,1)S(1)}, u32[]{:S(2)}, u32[]{:S(2)}) %collective-permute-start.3) | collective-permute-done | bytes 262176 | tf_op jit(solution)/shard_map/ppermute | solution.py:145
  21.5 0.9 %copy-done.1 = bf16[1024,128]{1,0:T(8,128)(2,1)S(1)} copy-done((bf16[1024,128]{1,0:T(8,128)(2,1)S(1)}, bf16[1024,128]{1,0:T(8,128)(2,1)}, u32[]{:S(2)}) %copy-start.1) | copy-done | bytes 262168
  22.4 0.9 %copy-done.6 = bf16[128,1024]{1,0:T(8,128)(2,1)S(1)} copy-done((bf16[128,1024]{1,0:T(8,128)(2,1)S(1)}, bf16[128,1024]{1,0:T(8,128)(2,1)}, u32[]{:S(2)}) %copy-start.6) | copy-done | bytes 262168
  23.4 1.1 %shard_map.104 = (bf16[512,256]{1,0:T(8,128)(2,1)S(1)}, bf16[512,1024]{1,0:T(8,128)(2,1)S(1)}, f32[512,1024]{1,0:T(8,128)S(1)}) custom-call(bf16[512,256]{1,0:T(8,128)(2,1)S(1)} %collective-permute-done.3.raw.refs_13_, bf16[128,1024]{1,0:T(8,128)(2,1)S(1)} %copy-done.6, f32[1,1024]{1,0:T(1,128)S(1)} %bitcast.11, bf16[1024,128]{1,0:T(8,128)(2,1)S(1)} %copy-done.1, ...), custom_call_target="tpu_custom_call" | custom-call | flops 268435456 | bytes 791040 | tf_op jit(solution)/shard_map/pallas_call | solution.py:37
  24.5 0.1 collective-permute-start.7
  24.6 2.5 %collective-permute-done.4.raw.refs_14_ = bf16[512,256]{1,0:T(8,128)(2,1)S(1)} collective-permute-done((bf16[512,256]{1,0:T(8,128)(2,1)S(1)}, bf16[512,256]{1,0:T(8,128)(2,1)S(1)}, u32[]{:S(2)}, u32[]{:S(2)}) %collective-permute-start.4) | collective-permute-done | bytes 262176 | tf_op jit(solution)/shard_map/ppermute | solution.py:145
  27.1 1.1 %shard_map.105 = (bf16[512,256]{1,0:T(8,128)(2,1)S(1)}, bf16[512,1024]{1,0:T(8,128)(2,1)S(1)}, f32[512,1024]{1,0:T(8,128)S(1)}) custom-call(bf16[512,256]{1,0:T(8,128)(2,1)S(1)} %collective-permute-done.4.raw.refs_14_, bf16[128,1024]{1,0:T(8,128)(2,1)S(1)} %copy-done.6, f32[1,1024]{1,0:T(1,128)S(1)} %bitcast.12, bf16[1024,128]{1,0:T(8,128)(2,1)S(1)} %copy-done.1, ...), custom_call_target="tpu_custom_call" | custom-call | flops 268435456 | bytes 791040 | tf_op jit(solution)/shard_map/pallas_call | solution.py:37
  28.3 0.1 collective-permute-start.8
  28.4 1.1 %shard_map.106 = (bf16[512,256]{1,0:T(8,128)(2,1)S(1)}, bf16[512,1024]{1,0:T(8,128)(2,1)S(1)}, f32[512,1024]{1,0:T(8,128)S(1)}) custom-call(bf16[512,256]{1,0:T(8,128)(2,1)S(1)} %collective-permute-done.5.raw.refs_15_, bf16[128,1024]{1,0:T(8,128)(2,1)S(1)} %copy-done.6, f32[1,1024]{1,0:T(1,128)S(1)} %bitcast.13, bf16[1024,128]{1,0:T(8,128)(2,1)S(1)} %copy-done.1, ...), custom_call_target="tpu_custom_call" | custom-call | flops 268435456 | bytes 791040 | tf_op jit(solution)/shard_map/pallas_call | solution.py:37
  29.5 0.0 copy-start.2
  29.5 0.0 copy-start.4
  29.5 0.6 %collective-permute-start.9 = (bf16[512,256]{1,0:T(8,128)(2,1)S(1)}, bf16[512,256]{1,0:T(8,128)(2,1)S(1)}, u32[]{:S(2)}, u32[]{:S(2)}) collective-permute-start(bf16[512,256]{1,0:T(8,128)(2,1)S(1)} %get-tuple-element.28.refs_3_), channel_id=1, source_target_pairs={{0,1},{1,0},{2,3},{3,2},{4,5},{5,4},{6,7},{7,6},{8,9},{9,8},{10,11... | collective-permute-start | bytes 786440 | tf_op jit(solution)/shard_map/ppermute | solution.py:145
  30.1 6.9 %shard_map.107 = (f32[128,512]{1,0:T(8,128)S(1)}, f32[128,512]{1,0:T(8,128)S(1)}, f32[128,512]{1,0:T(8,128)S(1)}, f32[128,512]{1,0:T(8,128)S(1)}) custom-call(bf16[512,256]{1,0:T(8,128)(2,1)S(1)} %get-tuple-element.25.refs_0_, bf16[512,256]{1,0:T(8,128)(2,1)S(1)} %get-tuple-element.26.refs_1_, bf16[512,256]{1,0:T(8,128)(2,1)S(1)} %get-tuple-element.27.refs_2_, ...), custom_call_target="tpu_custom_call" | custom-call | flops 3221225472 | bytes 1048576 | tf_op jit(solution)/shard_map/pallas_call | solution.py:37
  37.1 10.1 %shard_map.108 = (f32[128,128]{1,0:T(8,128)}, f32[264,1024]{1,0:T(8,128)S(1)}) custom-call(bf16[512,256]{1,0:T(8,128)(2,1)S(1)} %get-tuple-element.25.refs_0_, bf16[512,256]{1,0:T(8,128)(2,1)S(1)} %get-tuple-element.26.refs_1_, bf16[512,256]{1,0:T(8,128)(2,1)S(1)} %get-tuple-element.27.refs_2_, bf16[512,256]{1,0:T(8,128)(2,1)S(1)} %get-tuple-element.28.refs_3_, ...), custom_call_target="tpu_custom_call" | custom-call | flops 3221225472 | bytes 17039872 | tf_op jit(solution)/shard_map/pallas_call | solution.py:37
  47.2 0.1 collective-permute-start.10
  47.3 2.7 %collective-permute-done.10.other = f32[264,1024]{1,0:T(8,128)S(1)} collective-permute-done((f32[264,1024]{1,0:T(8,128)S(1)}, f32[264,1024]{1,0:T(8,128)S(1)}, u32[]{:S(2)}, u32[]{:S(2)}) %collective-permute-start.10) | collective-permute-done | bytes 1081376 | tf_op jit(solution)/shard_map/ppermute | solution.py:145
  50.0 1.2 %shard_map.109 = (f32[128,1024]{1,0:T(8,128)}, f32[1,1024]{1,0:T(1,128)}, f32[1024,128]{1,0:T(8,128)}) custom-call(f32[264,1024]{1,0:T(8,128)S(1)} %get-tuple-element.42.mine, f32[264,1024]{1,0:T(8,128)S(1)} %collective-permute-done.10.other), custom_call_target="tpu_custom_call" | custom-call | bytes 2162688 | tf_op jit(solution)/shard_map/pallas_call | solution.py:37
  (15 shorter events, 0.0 us)
Async XLA Ops:
  1.4 7.6 %collective-permute-start.2 = (bf16[256,128]{1,0:T(8,128)(2,1)S(1)}, bf16[256,128]{1,0:T(8,128)(2,1)S(1)}, u32[]{:S(2)}, u32[]{:S(2)}) collective-permute-start(bf16[256,128]{1,0:T(8,128)(2,1)S(1)} %pad_maximum_fusion.refs_0_), channel_id=1, source_target_pairs={{0,24},{2,26},{4,28},{6,30},{8,16},{10,18},{12,20},{14,22},{16,8},... | collective-permute-start | bytes 196616 | tf_op jit(solution)/shard_map/ppermute | solution.py:145
  6.5 5.6 %collective-permute-start.1 = (bf16[256,128]{1,0:T(8,128)(2,1)S(1)}, bf16[256,128]{1,0:T(8,128)(2,1)S(1)}, u32[]{:S(2)}, u32[]{:S(2)}) collective-permute-start(bf16[256,128]{1,0:T(8,128)(2,1)S(1)} %pad_maximum_fusion.refs_0_), channel_id=1, source_target_pairs={{0,16},{2,18},{4,20},{6,22},{8,24},{10,26},{12,28},{14,30},{16,0},... | collective-permute-start | bytes 196616 | tf_op jit(solution)/shard_map/ppermute | solution.py:145
  6.5 5.6 %collective-permute-start = (bf16[256,128]{1,0:T(8,128)(2,1)S(1)}, bf16[256,128]{1,0:T(8,128)(2,1)S(1)}, u32[]{:S(2)}, u32[]{:S(2)}) collective-permute-start(bf16[256,128]{1,0:T(8,128)(2,1)S(1)} %pad_maximum_fusion.refs_0_), channel_id=1, source_target_pairs={{0,8},{2,10},{4,12},{6,14},{8,0},{10,2},{12,4},{14,6},{16,24},{18,... | collective-permute-start | bytes 196616 | tf_op jit(solution)/shard_map/ppermute | solution.py:145
  12.2 9.3 %collective-permute-start.3 = (bf16[512,256]{1,0:T(8,128)(2,1)S(1)}, bf16[512,256]{1,0:T(8,128)(2,1)S(1)}, u32[]{:S(2)}, u32[]{:S(2)}) collective-permute-start(bf16[512,256]{1,0:T(8,128)(2,1)S(1)} %shard_map.102.raw.refs_12_), channel_id=1, source_target_pairs={{0,2},{2,0},{4,6},{6,4},{8,10},{10,8},{12,14},{14,12},{16,18},{18,... | collective-permute-start | bytes 786440 | tf_op jit(solution)/shard_map/ppermute | solution.py:145
  13.7 13.4 %collective-permute-start.4 = (bf16[512,256]{1,0:T(8,128)(2,1)S(1)}, bf16[512,256]{1,0:T(8,128)(2,1)S(1)}, u32[]{:S(2)}, u32[]{:S(2)}) collective-permute-start(bf16[512,256]{1,0:T(8,128)(2,1)S(1)} %shard_map.102.raw.refs_12_), channel_id=1, source_target_pairs={{0,4},{2,6},{4,0},{6,2},{8,12},{10,14},{12,8},{14,10},{16,20},{18,... | collective-permute-start | bytes 786440 | tf_op jit(solution)/shard_map/ppermute | solution.py:145
  15.3 13.1 %collective-permute-start.5 = (bf16[512,256]{1,0:T(8,128)(2,1)S(1)}, bf16[512,256]{1,0:T(8,128)(2,1)S(1)}, u32[]{:S(2)}, u32[]{:S(2)}) collective-permute-start(bf16[512,256]{1,0:T(8,128)(2,1)S(1)} %shard_map.102.raw.refs_12_), channel_id=1, source_target_pairs={{0,6},{2,4},{4,2},{6,0},{8,14},{10,12},{12,10},{14,8},{16,22},{18,... | collective-permute-start | bytes 786440 | tf_op jit(solution)/shard_map/ppermute | solution.py:145
  15.7 0.9 %copy-start = (bf16[1024,128]{1,0:T(8,128)(2,1)S(1)}, bf16[1024,128]{1,0:T(8,128)(2,1)}, u32[]{:S(2)}) copy-start(bf16[1024,128]{1,0:T(8,128)(2,1)} %refs_24_.1) | copy-start | bytes 786436
  16.7 0.7 %copy-start.3 = (f32[128]{0:T(128)S(1)}, f32[128]{0:T(128)}, u32[]{:S(2)}) copy-start(f32[128]{0:T(128)} %param.11) | copy-start | bytes 1540
  17.3 0.9 %copy-start.5 = (bf16[128,1024]{1,0:T(8,128)(2,1)S(1)}, bf16[128,1024]{1,0:T(8,128)(2,1)}, u32[]{:S(2)}) copy-start(bf16[128,1024]{1,0:T(8,128)(2,1)} %w_in.7) | copy-start | bytes 786436
  18.3 0.7 %copy-start.7 = (f32[1024]{0:T(1024)S(1)}, f32[1024]{0:T(1024)}, u32[]{:S(2)}) copy-start(f32[1024]{0:T(1024)} %param.9) | copy-start | bytes 12292
  20.1 16.9 %collective-permute-start.6 = (bf16[512,256]{1,0:T(8,128)(2,1)S(1)}, bf16[512,256]{1,0:T(8,128)(2,1)S(1)}, u32[]{:S(2)}, u32[]{:S(2)}) collective-permute-start(bf16[512,256]{1,0:T(8,128)(2,1)S(1)} %get-tuple-element.25.refs_0_), channel_id=1, source_target_pairs={{0,1},{1,0},{2,3},{3,2},{4,5},{5,4},{6,7},{7,6},{8,9},{9,8},{10,11... | collective-permute-start | bytes 786440 | tf_op jit(solution)/shard_map/ppermute | solution.py:145
  21.5 1.0 %copy-start.1 = (bf16[1024,128]{1,0:T(8,128)(2,1)S(1)}, bf16[1024,128]{1,0:T(8,128)(2,1)}, u32[]{:S(2)}) copy-start(bf16[1024,128]{1,0:T(8,128)(2,1)} %refs_24_.1) | copy-start | bytes 786436
  22.4 0.9 %copy-start.6 = (bf16[128,1024]{1,0:T(8,128)(2,1)S(1)}, bf16[128,1024]{1,0:T(8,128)(2,1)}, u32[]{:S(2)}) copy-start(bf16[128,1024]{1,0:T(8,128)(2,1)} %w_in.7) | copy-start | bytes 786436
  24.5 12.5 %collective-permute-start.7 = (bf16[512,256]{1,0:T(8,128)(2,1)S(1)}, bf16[512,256]{1,0:T(8,128)(2,1)S(1)}, u32[]{:S(2)}, u32[]{:S(2)}) collective-permute-start(bf16[512,256]{1,0:T(8,128)(2,1)S(1)} %get-tuple-element.26.refs_1_), channel_id=1, source_target_pairs={{0,1},{1,0},{2,3},{3,2},{4,5},{5,4},{6,7},{7,6},{8,9},{9,8},{10,11... | collective-permute-start | bytes 786440 | tf_op jit(solution)/shard_map/ppermute | solution.py:145
  28.3 8.7 %collective-permute-start.8 = (bf16[512,256]{1,0:T(8,128)(2,1)S(1)}, bf16[512,256]{1,0:T(8,128)(2,1)S(1)}, u32[]{:S(2)}, u32[]{:S(2)}) collective-permute-start(bf16[512,256]{1,0:T(8,128)(2,1)S(1)} %get-tuple-element.27.refs_2_), channel_id=1, source_target_pairs={{0,1},{1,0},{2,3},{3,2},{4,5},{5,4},{6,7},{7,6},{8,9},{9,8},{10,11... | collective-permute-start | bytes 786440 | tf_op jit(solution)/shard_map/ppermute | solution.py:145
  29.5 7.5 %copy-start.2 = (bf16[1024,128]{1,0:T(8,128)(2,1)S(1)}, bf16[1024,128]{1,0:T(8,128)(2,1)}, u32[]{:S(2)}) copy-start(bf16[1024,128]{1,0:T(8,128)(2,1)} %refs_24_.1) | copy-start | bytes 786436
  29.5 7.5 %copy-start.4 = (f32[128]{0:T(128)S(1)}, f32[128]{0:T(128)}, u32[]{:S(2)}) copy-start(f32[128]{0:T(128)} %param.11) | copy-start | bytes 1540
  29.5 7.5 %collective-permute-start.9 = (bf16[512,256]{1,0:T(8,128)(2,1)S(1)}, bf16[512,256]{1,0:T(8,128)(2,1)S(1)}, u32[]{:S(2)}, u32[]{:S(2)}) collective-permute-start(bf16[512,256]{1,0:T(8,128)(2,1)S(1)} %get-tuple-element.28.refs_3_), channel_id=1, source_target_pairs={{0,1},{1,0},{2,3},{3,2},{4,5},{5,4},{6,7},{7,6},{8,9},{9,8},{10,11... | collective-permute-start | bytes 786440 | tf_op jit(solution)/shard_map/ppermute | solution.py:145
  47.2 2.8 %collective-permute-start.10 = (f32[264,1024]{1,0:T(8,128)S(1)}, f32[264,1024]{1,0:T(8,128)S(1)}, u32[]{:S(2)}, u32[]{:S(2)}) collective-permute-start(f32[264,1024]{1,0:T(8,128)S(1)} %get-tuple-element.42.mine), channel_id=1, source_target_pairs={{0,1},{1,0},{2,3},{3,2},{4,5},{5,4},{6,7},{7,6},{8,9},{9,8},{10,11... | collective-permute-start | bytes 3244040 | tf_op jit(solution)/shard_map/ppermute | solution.py:145

commit v4 on v3

--- a/solution.py
+++ b/solution.py
@@ -82,9 +82,9 @@
     return -0.5 * jnp.sum(wide * wide, axis=1, keepdims=True)
 
 
-def visit_all(inner, visit, feat, cols, cols_g):
+def visit_all(visit, feat, cols, cols_g):
     size = visit[0].shape[0]
-    mine = lax.axis_index("blk") % inner
+    mine = lax.axis_index("blk") % len(visit)
     for k, plane in enumerate(visit):
         cols[pl.ds(pl.multiple_of((mine ^ k) * size, size), size), :] = plane[...]
     cols_g[...] = cols[:, :feat].T
@@ -106,38 +106,56 @@
     return total - jnp.sum(sums, axis=0, keepdims=True) * g.astype(F32).T
 
 
-def own_kernel(inner, feat, step, *refs):
-    own, outs, (cols, cols_g) = refs[:inner], refs[inner:-2], refs[-2:]
-    visit_all(inner, own, feat, cols, cols_g)
+def early_kernel(half, feat, *refs):
+    own, outs, (cols, cols_g) = refs[:half], refs[half:-2], refs[-2:]
+    visit_all(own, feat, cols, cols_g)
     for plane, out in zip(own, outs):
-        out[...] = pair_sums(plane, feat, step, cols, cols_g)
-
-
-def last_kernel(inner, feat, step, factor, *refs):
-    own, other, before, raw, hidden, slope = (refs[i * inner : (i + 1) * inner] for i in range(6))
-    w_out, scales, feat_grad_out, part, mine_grad, sums, cols, cols_g = refs[6 * inner :]
+        out[...] = pair_sums(plane, feat, cols.shape[0], cols, cols_g)
+
+
+def own_kernel(inner, half, feat, *refs):
+    own, early, outs = refs[:inner], refs[inner : inner + half], refs[inner + half : -4]
+    first, second = refs[-4:-2], refs[-2:]
+    visit_all(own[:half], feat, *first)
+    visit_all(own[half:], feat, *second)
+    for k, (plane, out) in enumerate(zip(own, outs)):
+        here = early[k][...] if k < half else pair_sums(plane, feat, first[0].shape[0], *first)
+        out[...] = here + pair_sums(plane, feat, second[0].shape[0], *second)
+
+
+def last_kernel(inner, feat, factor, *refs):
+    own, other, before, raw, slope = (refs[i * inner : (i + 1) * inner] for i in range(5))
+    w_out, scales, feat_grad_out, part = refs[5 * inner : 5 * inner + 4]
+    grads, (mine_grad, sums, cols, cols_g) = refs[5 * inner + 4 : -4], refs[-4:]
     rows = feat_grad_out.shape[0]
-    din = sums.shape[1] - feat - 8
-    visit_all(inner, other, feat, cols, cols_g)
+    din = sums.shape[1] - 8
+    visit_all(other, feat, cols, cols_g)
     for i in range(inner):
-        feat_grad = (before[i][...] + pair_sums(own[i], feat, step, cols, cols_g)).T * scales[...]
+        feat_grad = (before[i][...] + pair_sums(own[i], feat, cols.shape[0], cols, cols_g)).T * scales[...]
         if i == 0:
             mine = lax.axis_index("blk") // inner
             mine_grad[...] = feat_grad
             feat_grad_out[...] = mine_grad[pl.ds(pl.multiple_of(mine * rows, rows), rows), :]
         feat_grad_b = feat_grad.astype(BF16)
+        grads[i][...] = feat_grad_b
         pre_grad = dot(feat_grad_b, w_out[...], NT) * slope[i][...]
         sums[i, :din, :] = factor * dot(raw[i][:, :din], pre_grad.astype(BF16), TN)
-        sums[i, din : din + feat, :] = factor * dot(feat_grad_b, hidden[i][...], TN)
-        sums[i, din + feat :, :] = factor * jnp.sum(pre_grad.reshape(-1, 8, pre_grad.shape[1]), axis=0)
+        sums[i, din:, :] = factor * jnp.sum(pre_grad.reshape(-1, 8, pre_grad.shape[1]), axis=0)
     part[...] = tree([sums[i] for i in range(inner)])
 
 
-def join_kernel(mine, other, w_in_out, b_in_out, w_out_out):
-    din, feat = w_in_out.shape[0], w_out_out.shape[1]
+def out_kernel(inner, factor, *refs):
+    grads, hidden, (part, sums) = refs[:inner], refs[inner : 2 * inner], refs[2 * inner :]
+    for i in range(inner):
+        sums[i] = factor * dot(grads[i][...], hidden[i][...], TN)
+    part[...] = tree([sums[i] for i in range(inner)])
+
+
+def join_kernel(mine, other, mine_out, other_out, w_in_out, b_in_out, w_out_out):
+    din = w_in_out.shape[0]
     w_in_out[...] = mine[:din, :] + other[:din, :]
-    w_out_out[...] = (mine[din : din + feat, :] + other[din : din + feat, :]).T
-    b_in_out[...] = jnp.sum(mine[din + feat :, :] + other[din + feat :, :], axis=0, keepdims=True)
+    w_out_out[...] = (mine_out[...] + other_out[...]).T
+    b_in_out[...] = jnp.sum(mine[din:, :] + other[din:, :], axis=0, keepdims=True)
 
 
 def swap(value, axis, bits):
@@ -159,30 +177,47 @@
     column = call(functools.partial(plane_kernel, inner, rows), jax.ShapeDtypeStruct((size, din + width - feat), BF16), *parts)
     raws = [column] + [swap(column, "blk", k) for k in range(1, inner)]
     factor = (size * inner * lax.axis_size("row")) ** (-0.5)
-    step = min(size * inner, 2048)
     flops = 6 * feat * (size * inner) ** 2
     grad_shape = jax.ShapeDtypeStruct((feat, size), F32)
     own, other, hidden, slope = [], [], [], []
-    for k, plane in enumerate(raws):
+    half = inner // 2
+    part_of = lambda count: [pltpu.VMEM((size * count, width), BF16), pltpu.VMEM((feat, size * count), BF16)]
+    for k in range(inner):
         shapes = [jax.ShapeDtypeStruct((size, width), BF16), jax.ShapeDtypeStruct((size, hid), BF16), jax.ShapeDtypeStruct((size, hid), F32)]
-        results = call(forward_kernel, shapes, plane, w_in, b_in, w_out, scales, flops=4 * size * w_in.size)
+        results = call(forward_kernel, shapes, raws[k], w_in, b_in, w_out, scales, flops=4 * size * w_in.size)
         for store, result in zip((own, hidden, slope), results):
             store.append(result)
         other.append(swap(own[k], "row", 1))
-    together = [pltpu.VMEM((size * inner, width), BF16), pltpu.VMEM((feat, size * inner), BF16)]
-    before = call(functools.partial(own_kernel, inner, feat, step), [grad_shape] * inner, *own, scratch=together, flops=flops)
-    feat_grad, part = call(
-        functools.partial(last_kernel, inner, feat, step, factor),
-        [jax.ShapeDtypeStruct((rows, feat), F32), jax.ShapeDtypeStruct((din + feat + 8, hid), F32)],
-        *own, *other, *before, *raws, *hidden, *slope, w_out, scales,
-        scratch=[pltpu.VMEM((size, feat), F32), pltpu.VMEM((inner, din + feat + 8, hid), F32), *together],
+        if k == half - 1:
+            early = call(functools.partial(early_kernel, half, feat), [grad_shape] * half, *own, scratch=part_of(half), flops=flops // 4)
+            for later in range(half, inner):
+                raws[later], early = lax.optimization_barrier((raws[later], early))
+    before = call(functools.partial(own_kernel, inner, half, feat), [grad_shape] * inner, *own, *early, scratch=part_of(half) * 2, flops=flops)
+    feat_grad, part, *grads = call(
+        functools.partial(last_kernel, inner, feat, factor),
+        [
+            jax.ShapeDtypeStruct((rows, feat), F32),
+            jax.ShapeDtypeStruct((din + 8, hid), F32),
+            *[jax.ShapeDtypeStruct((size, feat), BF16)] * inner,
+        ],
+        *own, *other, *before, *raws, *slope, w_out, scales,
+        scratch=[pltpu.VMEM((size, feat), F32), pltpu.VMEM((inner, din + 8, hid), F32), *part_of(inner)],
         flops=flops,
+    )
+    part_out = call(
+        functools.partial(out_kernel, inner, factor),
+        jax.ShapeDtypeStruct((feat, hid), F32),
+        *grads,
+        *hidden,
+        scratch=[pltpu.VMEM((inner, feat, hid), F32)],
     )
     grad_w_in, grad_b_in, grad_w_out = call(
         join_kernel,
         [jax.ShapeDtypeStruct(s, F32) for s in ((din, hid), (1, hid), (hid, feat))],
         part,
         swap(part, "row", 1),
+        part_out,
+        swap(part_out, "row", 1),
     )
     return (feat_grad, grad_w_in, grad_b_in[0], grad_w_out)
 
@@ -255,7 +290,7 @@
     width = points.shape[1] + left.shape[1] + right.shape[1]
     size = points.shape[0] * blocks * cores * width * points.dtype.itemsize
     inner = min(4, blocks)
-    fits = size <= GATHER_BYTES and cores == 2 and blocks & (blocks - 1) == 0 and points.shape[0] == points.shape[1]
+    fits = size <= GATHER_BYTES and cores == 2 and blocks & (blocks - 1) == 0 and blocks >= 4 and points.shape[0] == points.shape[1]
     plan = functools.partial(gather_plan, inner) if fits else ring_plan
     return plan(points, w_in, b_in, w_out, scales, left, right)
 

time: 51.5 us -> 49.7 us (0.965)
  waiting for transfers between devices: 11.5 us -> 8.3 us
  Pallas kernels: 22.8 us -> 23.7 us
    ppermute x11 -> x12, waiting for transfers between devices: 11.5 us -> 8.3 us  [swap(): lax.ppermute(value, axis, [(source, source ^ bits) for source in range(co...]
    pallas_call x8 -> x10, Pallas kernels: 22.8 us -> 23.7 us  [call(): pl.pallas_call(kernel, out_shape=out, in_specs=[VMEM] * len(args), out_sp...]
    ppermute x11 -> x12, starting transfers between devices: 10.1 us -> 10.6 us  [swap(): lax.ppermute(value, axis, [(source, source ^ bits) for source in range(co...]
  transfers between devices with their start and end apart: 11 -> 12, of which waited for: 5 -> 5; matrix products, arithmetic and copies ran while one was open for 0% -> 0% of each run, Pallas kernels for 22% -> 26%
where the time goes in v4:
time: 49.7 us; the launch traced here: 49.4 us
  Pallas kernels  23.7 us (48%)
  starting transfers between devices  10.6 us (21%)
  waiting for transfers between devices  8.3 us (17%)
  local copies, waits for them, and re-layouts  5.15 us (10%)
  other arithmetic  0.8 us (2%)
  between operations  0.76 us (2%)
    pallas_call x10, Pallas kernels, call(): pl.pallas_call(kernel, out_shape=out, in_specs=[VMEM] * len(args), out_sp...  23.7 us
    ppermute x12, starting transfers between devices, swap(): lax.ppermute(value, axis, [(source, source ^ bits) for source in range(co...  10.6 us
    ppermute x12, waiting for transfers between devices, swap(): lax.ppermute(value, axis, [(source, source ^ bits) for source in range(co...  8.3 us
    unnamed x16, local copies, waits for them, and re-layouts  5.15 us
  transfers between devices with their start and end apart: 12, of which 5 were waited for; matrix products, arithmetic and copies ran while one was open for 0% of the time, Pallas kernels for 26%

profile of v4, /device:TPU:0, one launch (start us, length us, event | category | flops | bytes accessed | tf_op | source)
XLA Modules:
  0.0 49.4 jit_solution(3364338018051213337)
XLA Ops:
  0.6 0.8 %pad_maximum_fusion.refs_0_ = bf16[256,128]{1,0:T(8,128)(2,1)S(1)} fusion(bf16[64,128]{1,0:T(8,128)(2,1)} %bitcast.14, bf16[64,128]{1,0:T(8,128)(2,1)} %bitcast.15, bf16[128,128]{1,0:T(8,128)(2,1)} %param.7), kind=kLoop, calls=%fused_computation | loop fusion | flops 196608 | bytes 131072 | tf_op jit(solution)/shard_map/concatenate | solution.py:175
  1.4 5.0 %collective-permute-start.2 = (bf16[256,128]{1,0:T(8,128)(2,1)S(1)}, bf16[256,128]{1,0:T(8,128)(2,1)S(1)}, u32[]{:S(2)}, u32[]{:S(2)}) collective-permute-start(bf16[256,128]{1,0:T(8,128)(2,1)S(1)} %pad_maximum_fusion.refs_0_), channel_id=1, source_target_pairs={{0,24},{2,26},{4,28},{6,30},{8,16},{10,18},{12,20},{14,22},{16,8},... | collective-permute-start | bytes 196616 | tf_op jit(solution)/shard_map/ppermute | solution.py:163
  6.5 0.6 %collective-permute-start = (bf16[256,128]{1,0:T(8,128)(2,1)S(1)}, bf16[256,128]{1,0:T(8,128)(2,1)S(1)}, u32[]{:S(2)}, u32[]{:S(2)}) collective-permute-start(bf16[256,128]{1,0:T(8,128)(2,1)S(1)} %pad_maximum_fusion.refs_0_), channel_id=1, source_target_pairs={{0,8},{2,10},{4,12},{6,14},{8,0},{10,2},{12,4},{14,6},{16,24},{18,... | collective-permute-start | bytes 196616 | tf_op jit(solution)/shard_map/ppermute | solution.py:163
  7.1 1.9 %collective-permute-done.2.refs_3_ = bf16[256,128]{1,0:T(8,128)(2,1)S(1)} collective-permute-done((bf16[256,128]{1,0:T(8,128)(2,1)S(1)}, bf16[256,128]{1,0:T(8,128)(2,1)S(1)}, u32[]{:S(2)}, u32[]{:S(2)}) %collective-permute-start.2) | collective-permute-done | bytes 65568 | tf_op jit(solution)/shard_map/ppermute | solution.py:163
  9.0 3.0 %collective-permute-done.1.refs_2_ = bf16[256,128]{1,0:T(8,128)(2,1)S(1)} collective-permute-done((bf16[256,128]{1,0:T(8,128)(2,1)S(1)}, bf16[256,128]{1,0:T(8,128)(2,1)S(1)}, u32[]{:S(2)}, u32[]{:S(2)}) %collective-permute-start.1) | collective-permute-done | bytes 65568 | tf_op jit(solution)/shard_map/ppermute | solution.py:163
  12.1 0.1 shard_map.102.raw.refs_12_
  12.2 1.6 %collective-permute-start.3 = (bf16[512,256]{1,0:T(8,128)(2,1)S(1)}, bf16[512,256]{1,0:T(8,128)(2,1)S(1)}, u32[]{:S(2)}, u32[]{:S(2)}) collective-permute-start(bf16[512,256]{1,0:T(8,128)(2,1)S(1)} %shard_map.102.raw.refs_12_), channel_id=1, source_target_pairs={{0,2},{2,0},{4,6},{6,4},{8,10},{10,8},{12,14},{14,12},{16,18},{18,... | collective-permute-start | bytes 786440 | tf_op jit(solution)/shard_map/ppermute | solution.py:163
  13.7 1.5 %collective-permute-start.4 = (bf16[512,256]{1,0:T(8,128)(2,1)S(1)}, bf16[512,256]{1,0:T(8,128)(2,1)S(1)}, u32[]{:S(2)}, u32[]{:S(2)}) collective-permute-start(bf16[512,256]{1,0:T(8,128)(2,1)S(1)} %shard_map.102.raw.refs_12_), channel_id=1, source_target_pairs={{0,4},{2,6},{4,0},{6,2},{8,12},{10,14},{12,8},{14,10},{16,20},{18,... | collective-permute-start | bytes 786440 | tf_op jit(solution)/shard_map/ppermute | solution.py:163
  15.3 0.5 collective-permute-start.5
  15.7 0.9 %copy-done = bf16[1024,128]{1,0:T(8,128)(2,1)S(1)} copy-done((bf16[1024,128]{1,0:T(8,128)(2,1)S(1)}, bf16[1024,128]{1,0:T(8,128)(2,1)}, u32[]{:S(2)}) %copy-start) | copy-done | bytes 262168
  16.7 0.7 %copy-done.3 = f32[128]{0:T(128)S(1)} copy-done((f32[128]{0:T(128)S(1)}, f32[128]{0:T(128)}, u32[]{:S(2)}) %copy-start.3) | copy-done | bytes 536
  17.3 0.9 %copy-done.5 = bf16[128,1024]{1,0:T(8,128)(2,1)S(1)} copy-done((bf16[128,1024]{1,0:T(8,128)(2,1)S(1)}, bf16[128,1024]{1,0:T(8,128)(2,1)}, u32[]{:S(2)}) %copy-start.5) | copy-done | bytes 262168
  18.3 0.7 %copy-done.7 = f32[1024]{0:T(1024)S(1)} copy-done((f32[1024]{0:T(1024)S(1)}, f32[1024]{0:T(1024)}, u32[]{:S(2)}) %copy-start.7) | copy-done | bytes 4120
  19.0 1.1 %shard_map.103 = (bf16[512,256]{1,0:T(8,128)(2,1)S(1)}, bf16[512,1024]{1,0:T(8,128)(2,1)S(1)}, f32[512,1024]{1,0:T(8,128)S(1)}) custom-call(bf16[512,256]{1,0:T(8,128)(2,1)S(1)} %shard_map.102.raw.refs_12_, bf16[128,1024]{1,0:T(8,128)(2,1)S(1)} %copy-done.5, f32[1,1024]{1,0:T(1,128)S(1)} %bitcast.10, bf16[1024,128]{1,0:T(8,128)(2,1)S(1)} %copy-done, ...), custom_call_target="tpu_custom_call" | custom-call | flops 268435456 | bytes 791040 | tf_op jit(solution)/shard_map/pallas_call | solution.py:37
  20.2 1.3 %collective-permute-done.3.raw.refs_13_ = bf16[512,256]{1,0:T(8,128)(2,1)S(1)} collective-permute-done((bf16[512,256]{1,0:T(8,128)(2,1)S(1)}, bf16[512,256]{1,0:T(8,128)(2,1)S(1)}, u32[]{:S(2)}, u32[]{:S(2)}) %collective-permute-start.3) | collective-permute-done | bytes 262176 | tf_op jit(solution)/shard_map/ppermute | solution.py:163
  21.5 0.9 %copy-done.1 = bf16[1024,128]{1,0:T(8,128)(2,1)S(1)} copy-done((bf16[1024,128]{1,0:T(8,128)(2,1)S(1)}, bf16[1024,128]{1,0:T(8,128)(2,1)}, u32[]{:S(2)}) %copy-start.1) | copy-done | bytes 262168
  22.4 0.9 %copy-done.6 = bf16[128,1024]{1,0:T(8,128)(2,1)S(1)} copy-done((bf16[128,1024]{1,0:T(8,128)(2,1)S(1)}, bf16[128,1024]{1,0:T(8,128)(2,1)}, u32[]{:S(2)}) %copy-start.6) | copy-done | bytes 262168
  23.4 1.1 %shard_map.104 = (bf16[512,256]{1,0:T(8,128)(2,1)S(1)}, bf16[512,1024]{1,0:T(8,128)(2,1)S(1)}, f32[512,1024]{1,0:T(8,128)S(1)}) custom-call(bf16[512,256]{1,0:T(8,128)(2,1)S(1)} %collective-permute-done.3.raw.refs_13_, bf16[128,1024]{1,0:T(8,128)(2,1)S(1)} %copy-done.6, f32[1,1024]{1,0:T(1,128)S(1)} %bitcast.11, bf16[1024,128]{1,0:T(8,128)(2,1)S(1)} %copy-done.1, ...), custom_call_target="tpu_custom_call" | custom-call | flops 268435456 | bytes 791040 | tf_op jit(solution)/shard_map/pallas_call | solution.py:37
  24.5 0.1 collective-permute-start.7
  24.6 2.0 %shard_map.105 = (f32[128,512]{1,0:T(8,128)S(1)}, f32[128,512]{1,0:T(8,128)S(1)}) custom-call(bf16[512,256]{1,0:T(8,128)(2,1)S(1)} %get-tuple-element.37.refs_0_, bf16[512,256]{1,0:T(8,128)(2,1)S(1)} %get-tuple-element.38.refs_1_), custom_call_target="tpu_custom_call" | custom-call | flops 805306368 | bytes 524288 | tf_op jit(solution)/shard_map/pallas_call | solution.py:37
  26.6 0.5 %collective-permute-done.4.raw.refs_14_ = bf16[512,256]{1,0:T(8,128)(2,1)S(1)} collective-permute-done((bf16[512,256]{1,0:T(8,128)(2,1)S(1)}, bf16[512,256]{1,0:T(8,128)(2,1)S(1)}, u32[]{:S(2)}, u32[]{:S(2)}) %collective-permute-start.4) | collective-permute-done | bytes 262176 | tf_op jit(solution)/shard_map/ppermute | solution.py:163
  27.1 1.1 %shard_map.107 = (bf16[512,256]{1,0:T(8,128)(2,1)S(1)}, bf16[512,1024]{1,0:T(8,128)(2,1)S(1)}, f32[512,1024]{1,0:T(8,128)S(1)}) custom-call(bf16[512,256]{1,0:T(8,128)(2,1)S(1)} %collective-permute-done.5.raw.refs_15_, bf16[128,1024]{1,0:T(8,128)(2,1)S(1)} %copy-done.6, f32[1,1024]{1,0:T(1,128)S(1)} %bitcast.12, bf16[1024,128]{1,0:T(8,128)(2,1)S(1)} %copy-done.2, ...), custom_call_target="tpu_custom_call" | custom-call | flops 268435456 | bytes 791040 | tf_op jit(solution)/shard_map/pallas_call | solution.py:37
  28.3 0.1 collective-permute-start.9
  28.4 1.1 %shard_map.106 = (bf16[512,256]{1,0:T(8,128)(2,1)S(1)}, bf16[512,1024]{1,0:T(8,128)(2,1)S(1)}, f32[512,1024]{1,0:T(8,128)S(1)}) custom-call(bf16[512,256]{1,0:T(8,128)(2,1)S(1)} %collective-permute-done.4.raw.refs_14_, bf16[128,1024]{1,0:T(8,128)(2,1)S(1)} %copy-done.6, f32[1,1024]{1,0:T(1,128)S(1)} %bitcast.13, bf16[1024,128]{1,0:T(8,128)(2,1)S(1)} %copy-done.2, ...), custom_call_target="tpu_custom_call" | custom-call | flops 268435456 | bytes 791040 | tf_op jit(solution)/shard_map/pallas_call | solution.py:37
  29.5 0.6 %collective-permute-start.8 = (bf16[512,256]{1,0:T(8,128)(2,1)S(1)}, bf16[512,256]{1,0:T(8,128)(2,1)S(1)}, u32[]{:S(2)}, u32[]{:S(2)}) collective-permute-start(bf16[512,256]{1,0:T(8,128)(2,1)S(1)} %get-tuple-element.42.refs_2_), channel_id=1, source_target_pairs={{0,1},{1,0},{2,3},{3,2},{4,5},{5,4},{6,7},{7,6},{8,9},{9,8},{10,11... | collective-permute-start | bytes 786440 | tf_op jit(solution)/shard_map/ppermute | solution.py:163
  30.1 5.7 %shard_map.108 = (f32[128,512]{1,0:T(8,128)S(1)}, f32[128,512]{1,0:T(8,128)S(1)}, f32[128,512]{1,0:T(8,128)S(1)}, f32[128,512]{1,0:T(8,128)S(1)}) custom-call(bf16[512,256]{1,0:T(8,128)(2,1)S(1)} %get-tuple-element.37.refs_0_, bf16[512,256]{1,0:T(8,128)(2,1)S(1)} %get-tuple-element.38.refs_1_, bf16[512,256]{1,0:T(8,128)(2,1)S(1)} %get-tuple-element.42.refs_2_, ...), custom_call_target="tpu_custom_call" | custom-call | flops 3221225472 | bytes 1572864 | tf_op jit(solution)/shard_map/pallas_call | solution.py:37
  35.9 9.4 %shard_map.109 = (f32[128,128]{1,0:T(8,128)}, f32[136,1024]{1,0:T(8,128)S(1)}, bf16[512,128]{1,0:T(8,128)(2,1)S(1)}, bf16[512,128]{1,0:T(8,128)(2,1)S(1)}, bf16[...) custom-call(bf16[512,256]{1,0:T(8,128)(2,1)S(1)} %get-tuple-element.37.refs_0_, ...), custom_call_target="tpu_custom_call" | custom-call | flops 3221225472 | bytes 12845568 | tf_op jit(solution)/shard_map/pallas_call | solution.py:37
  45.3 0.1 collective-permute-start.10
  45.4 0.8 %shard_map.110.mine_out = f32[128,1024]{1,0:T(8,128)S(1)} custom-call(bf16[512,128]{1,0:T(8,128)(2,1)S(1)} %get-tuple-element.59.refs_0_, bf16[512,128]{1,0:T(8,128)(2,1)S(1)} %get-tuple-element.60.refs_1_, bf16[512,128]{1,0:T(8,128)(2,1)S(1)} %get-tuple-element.61.refs_2_, bf16[512,128]{1,0:T(8,128)(2,1)S(1)} %get-tuple-element.62.refs_3_, ...), custom_call_target="tpu_custom_call" | custom-call | bytes 4718592 | tf_op jit(solution)/shard_map/pallas_call | solution.py:37
  46.1 0.5 %collective-permute-start.11 = (f32[128,1024]{1,0:T(8,128)S(1)}, f32[128,1024]{1,0:T(8,128)S(1)}, u32[]{:S(2)}, u32[]{:S(2)}) collective-permute-start(f32[128,1024]{1,0:T(8,128)S(1)} %shard_map.110.mine_out), channel_id=1, source_target_pairs={{0,1},{1,0},{2,3},{3,2},{4,5},{5,4},{6,7},{7,6},{8,9},{9,8},{10,11... | collective-permute-start | bytes 1572872 | tf_op jit(solution)/shard_map/ppermute | solution.py:163
  46.7 1.5 %collective-permute-done.11.other_out = f32[128,1024]{1,0:T(8,128)S(1)} collective-permute-done((f32[128,1024]{1,0:T(8,128)S(1)}, f32[128,1024]{1,0:T(8,128)S(1)}, u32[]{:S(2)}, u32[]{:S(2)}) %collective-permute-start.11) | collective-permute-done | bytes 524320 | tf_op jit(solution)/shard_map/ppermute | solution.py:163
  48.2 1.2 %shard_map.111 = (f32[128,1024]{1,0:T(8,128)}, f32[1,1024]{1,0:T(1,128)}, f32[1024,128]{1,0:T(8,128)}) custom-call(f32[136,1024]{1,0:T(8,128)S(1)} %get-tuple-element.58.mine, f32[136,1024]{1,0:T(8,128)S(1)} %collective-permute-done.10.other, f32[128,1024]{1,0:T(8,128)S(1)} %shard_map.110.mine_out, f32[128,1024]{1,0:T(8,128)S(1)} %collective-permute-done.11.other_out), custom_call_target="tpu_custom_call" | custom-call | bytes 2162688 | tf_op jit(solution)/shard_map/pallas_call | solution.py:37
  (19 shorter events, 0.1 us)
Async XLA Ops:
  1.4 7.6 %collective-permute-start.2 = (bf16[256,128]{1,0:T(8,128)(2,1)S(1)}, bf16[256,128]{1,0:T(8,128)(2,1)S(1)}, u32[]{:S(2)}, u32[]{:S(2)}) collective-permute-start(bf16[256,128]{1,0:T(8,128)(2,1)S(1)} %pad_maximum_fusion.refs_0_), channel_id=1, source_target_pairs={{0,24},{2,26},{4,28},{6,30},{8,16},{10,18},{12,20},{14,22},{16,8},... | collective-permute-start | bytes 196616 | tf_op jit(solution)/shard_map/ppermute | solution.py:163
  6.5 5.6 %collective-permute-start.1 = (bf16[256,128]{1,0:T(8,128)(2,1)S(1)}, bf16[256,128]{1,0:T(8,128)(2,1)S(1)}, u32[]{:S(2)}, u32[]{:S(2)}) collective-permute-start(bf16[256,128]{1,0:T(8,128)(2,1)S(1)} %pad_maximum_fusion.refs_0_), channel_id=1, source_target_pairs={{0,16},{2,18},{4,20},{6,22},{8,24},{10,26},{12,28},{14,30},{16,0},... | collective-permute-start | bytes 196616 | tf_op jit(solution)/shard_map/ppermute | solution.py:163
  6.5 5.6 %collective-permute-start = (bf16[256,128]{1,0:T(8,128)(2,1)S(1)}, bf16[256,128]{1,0:T(8,128)(2,1)S(1)}, u32[]{:S(2)}, u32[]{:S(2)}) collective-permute-start(bf16[256,128]{1,0:T(8,128)(2,1)S(1)} %pad_maximum_fusion.refs_0_), channel_id=1, source_target_pairs={{0,8},{2,10},{4,12},{6,14},{8,0},{10,2},{12,4},{14,6},{16,24},{18,... | collective-permute-start | bytes 196616 | tf_op jit(solution)/shard_map/ppermute | solution.py:163
  12.2 9.3 %collective-permute-start.3 = (bf16[512,256]{1,0:T(8,128)(2,1)S(1)}, bf16[512,256]{1,0:T(8,128)(2,1)S(1)}, u32[]{:S(2)}, u32[]{:S(2)}) collective-permute-start(bf16[512,256]{1,0:T(8,128)(2,1)S(1)} %shard_map.102.raw.refs_12_), channel_id=1, source_target_pairs={{0,2},{2,0},{4,6},{6,4},{8,10},{10,8},{12,14},{14,12},{16,18},{18,... | collective-permute-start | bytes 786440 | tf_op jit(solution)/shard_map/ppermute | solution.py:163
  13.7 13.4 %collective-permute-start.4 = (bf16[512,256]{1,0:T(8,128)(2,1)S(1)}, bf16[512,256]{1,0:T(8,128)(2,1)S(1)}, u32[]{:S(2)}, u32[]{:S(2)}) collective-permute-start(bf16[512,256]{1,0:T(8,128)(2,1)S(1)} %shard_map.102.raw.refs_12_), channel_id=1, source_target_pairs={{0,4},{2,6},{4,0},{6,2},{8,12},{10,14},{12,8},{14,10},{16,20},{18,... | collective-permute-start | bytes 786440 | tf_op jit(solution)/shard_map/ppermute | solution.py:163
  15.3 11.9 %collective-permute-start.5 = (bf16[512,256]{1,0:T(8,128)(2,1)S(1)}, bf16[512,256]{1,0:T(8,128)(2,1)S(1)}, u32[]{:S(2)}, u32[]{:S(2)}) collective-permute-start(bf16[512,256]{1,0:T(8,128)(2,1)S(1)} %shard_map.102.raw.refs_12_), channel_id=1, source_target_pairs={{0,6},{2,4},{4,2},{6,0},{8,14},{10,12},{12,10},{14,8},{16,22},{18,... | collective-permute-start | bytes 786440 | tf_op jit(solution)/shard_map/ppermute | solution.py:163
  15.7 0.9 %copy-start = (bf16[1024,128]{1,0:T(8,128)(2,1)S(1)}, bf16[1024,128]{1,0:T(8,128)(2,1)}, u32[]{:S(2)}) copy-start(bf16[1024,128]{1,0:T(8,128)(2,1)} %refs_20_.1) | copy-start | bytes 786436
  16.7 0.7 %copy-start.3 = (f32[128]{0:T(128)S(1)}, f32[128]{0:T(128)}, u32[]{:S(2)}) copy-start(f32[128]{0:T(128)} %param.11) | copy-start | bytes 1540
  17.3 0.9 %copy-start.5 = (bf16[128,1024]{1,0:T(8,128)(2,1)S(1)}, bf16[128,1024]{1,0:T(8,128)(2,1)}, u32[]{:S(2)}) copy-start(bf16[128,1024]{1,0:T(8,128)(2,1)} %w_in.7) | copy-start | bytes 786436
  18.3 0.7 %copy-start.7 = (f32[1024]{0:T(1024)S(1)}, f32[1024]{0:T(1024)}, u32[]{:S(2)}) copy-start(f32[1024]{0:T(1024)} %param.9) | copy-start | bytes 12292
  19.0 8.2 %copy-start.2 = (bf16[1024,128]{1,0:T(8,128)(2,1)S(1)}, bf16[1024,128]{1,0:T(8,128)(2,1)}, u32[]{:S(2)}) copy-start(bf16[1024,128]{1,0:T(8,128)(2,1)} %refs_20_.1) | copy-start | bytes 786436
  20.1 15.7 %collective-permute-start.6 = (bf16[512,256]{1,0:T(8,128)(2,1)S(1)}, bf16[512,256]{1,0:T(8,128)(2,1)S(1)}, u32[]{:S(2)}, u32[]{:S(2)}) collective-permute-start(bf16[512,256]{1,0:T(8,128)(2,1)S(1)} %get-tuple-element.37.refs_0_), channel_id=1, source_target_pairs={{0,1},{1,0},{2,3},{3,2},{4,5},{5,4},{6,7},{7,6},{8,9},{9,8},{10,11... | collective-permute-start | bytes 786440 | tf_op jit(solution)/shard_map/ppermute | solution.py:163
  21.5 1.0 %copy-start.1 = (bf16[1024,128]{1,0:T(8,128)(2,1)S(1)}, bf16[1024,128]{1,0:T(8,128)(2,1)}, u32[]{:S(2)}) copy-start(bf16[1024,128]{1,0:T(8,128)(2,1)} %refs_20_.1) | copy-start | bytes 786436
  22.4 0.9 %copy-start.6 = (bf16[128,1024]{1,0:T(8,128)(2,1)S(1)}, bf16[128,1024]{1,0:T(8,128)(2,1)}, u32[]{:S(2)}) copy-start(bf16[128,1024]{1,0:T(8,128)(2,1)} %w_in.7) | copy-start | bytes 786436
  24.5 11.3 %collective-permute-start.7 = (bf16[512,256]{1,0:T(8,128)(2,1)S(1)}, bf16[512,256]{1,0:T(8,128)(2,1)S(1)}, u32[]{:S(2)}, u32[]{:S(2)}) collective-permute-start(bf16[512,256]{1,0:T(8,128)(2,1)S(1)} %get-tuple-element.38.refs_1_), channel_id=1, source_target_pairs={{0,1},{1,0},{2,3},{3,2},{4,5},{5,4},{6,7},{7,6},{8,9},{9,8},{10,11... | collective-permute-start | bytes 786440 | tf_op jit(solution)/shard_map/ppermute | solution.py:163
  28.3 7.5 %collective-permute-start.9 = (bf16[512,256]{1,0:T(8,128)(2,1)S(1)}, bf16[512,256]{1,0:T(8,128)(2,1)S(1)}, u32[]{:S(2)}, u32[]{:S(2)}) collective-permute-start(bf16[512,256]{1,0:T(8,128)(2,1)S(1)} %get-tuple-element.46.refs_3_), channel_id=1, source_target_pairs={{0,1},{1,0},{2,3},{3,2},{4,5},{5,4},{6,7},{7,6},{8,9},{9,8},{10,11... | collective-permute-start | bytes 786440 | tf_op jit(solution)/shard_map/ppermute | solution.py:163
  29.5 6.3 %copy-start.4 = (f32[128]{0:T(128)S(1)}, f32[128]{0:T(128)}, u32[]{:S(2)}) copy-start(f32[128]{0:T(128)} %param.11) | copy-start | bytes 1540
  29.5 6.3 %collective-permute-start.8 = (bf16[512,256]{1,0:T(8,128)(2,1)S(1)}, bf16[512,256]{1,0:T(8,128)(2,1)S(1)}, u32[]{:S(2)}, u32[]{:S(2)}) collective-permute-start(bf16[512,256]{1,0:T(8,128)(2,1)S(1)} %get-tuple-element.42.refs_2_), channel_id=1, source_target_pairs={{0,1},{1,0},{2,3},{3,2},{4,5},{5,4},{6,7},{7,6},{8,9},{9,8},{10,11... | collective-permute-start | bytes 786440 | tf_op jit(solution)/shard_map/ppermute | solution.py:163
  45.3 2.9 %collective-permute-start.10 = (f32[136,1024]{1,0:T(8,128)S(1)}, f32[136,1024]{1,0:T(8,128)S(1)}, u32[]{:S(2)}, u32[]{:S(2)}) collective-permute-start(f32[136,1024]{1,0:T(8,128)S(1)} %get-tuple-element.58.mine), channel_id=1, source_target_pairs={{0,1},{1,0},{2,3},{3,2},{4,5},{5,4},{6,7},{7,6},{8,9},{9,8},{10,11... | collective-permute-start | bytes 1671176 | tf_op jit(solution)/shard_map/ppermute | solution.py:163
  46.1 2.1 %collective-permute-start.11 = (f32[128,1024]{1,0:T(8,128)S(1)}, f32[128,1024]{1,0:T(8,128)S(1)}, u32[]{:S(2)}, u32[]{:S(2)}) collective-permute-start(f32[128,1024]{1,0:T(8,128)S(1)} %shard_map.110.mine_out), channel_id=1, source_target_pairs={{0,1},{1,0},{2,3},{3,2},{4,5},{5,4},{6,7},{7,6},{8,9},{9,8},{10,11... | collective-permute-start | bytes 1572872 | tf_op jit(solution)/shard_map/ppermute | solution.py:163

commit v5 on v4

--- a/solution.py
+++ b/solution.py
@@ -65,7 +65,9 @@
         out[place, din:] = part[rows:, :].T
 
 
-def forward_kernel(raw, w_in, b_in, w_out, scales, out, hidden_out, slope_out):
+def forward_kernel(raw, w_in, b_in, w_out, scales, out, hidden_out, slope_out, *handed_on):
+    for source, target in zip((w_in, b_in, w_out, scales), handed_on):
+        target[...] = source[...]
     din, feat = w_in.shape[0], w_out.shape[1]
     pre = dot(raw[:, :din], w_in[...]) + b_in[...]
     sig = sigmoid(pre)
@@ -107,31 +109,35 @@
 
 
 def early_kernel(half, feat, *refs):
-    own, outs, (cols, cols_g) = refs[:half], refs[half:-2], refs[-2:]
-    visit_all(own, feat, cols, cols_g)
+    own, visit, outs, (cols, cols_g) = refs[:half], refs[half : 2 * half], refs[2 * half : -2], refs[-2:]
+    visit_all(visit, feat, cols, cols_g)
     for plane, out in zip(own, outs):
         out[...] = pair_sums(plane, feat, cols.shape[0], cols, cols_g)
 
 
+def all_sums(half, feat, home, visit, early, first, second):
+    visit_all(visit[:half], feat, *first)
+    visit_all(visit[half:], feat, *second)
+    for k, plane in enumerate(home):
+        here = early[k][...] if k < half else pair_sums(plane, feat, first[0].shape[0], *first)
+        yield here + pair_sums(plane, feat, second[0].shape[0], *second)
+
+
 def own_kernel(inner, half, feat, *refs):
     own, early, outs = refs[:inner], refs[inner : inner + half], refs[inner + half : -4]
-    first, second = refs[-4:-2], refs[-2:]
-    visit_all(own[:half], feat, *first)
-    visit_all(own[half:], feat, *second)
-    for k, (plane, out) in enumerate(zip(own, outs)):
-        here = early[k][...] if k < half else pair_sums(plane, feat, first[0].shape[0], *first)
-        out[...] = here + pair_sums(plane, feat, second[0].shape[0], *second)
-
-
-def last_kernel(inner, feat, factor, *refs):
+    for out, value in zip(outs, all_sums(half, feat, own, own, early, refs[-4:-2], refs[-2:])):
+        out[...] = value
+
+
+def last_kernel(inner, half, feat, factor, *refs):
     own, other, before, raw, slope = (refs[i * inner : (i + 1) * inner] for i in range(5))
-    w_out, scales, feat_grad_out, part = refs[5 * inner : 5 * inner + 4]
-    grads, (mine_grad, sums, cols, cols_g) = refs[5 * inner + 4 : -4], refs[-4:]
+    early, refs = refs[5 * inner : 5 * inner + half], refs[5 * inner + half :]
+    w_out, scales, feat_grad_out, part = refs[:4]
+    grads, (mine_grad, sums), first, second = refs[4:-6], refs[-6:-4], refs[-4:-2], refs[-2:]
     rows = feat_grad_out.shape[0]
     din = sums.shape[1] - 8
-    visit_all(other, feat, cols, cols_g)
-    for i in range(inner):
-        feat_grad = (before[i][...] + pair_sums(own[i], feat, cols.shape[0], cols, cols_g)).T * scales[...]
+    for i, value in enumerate(all_sums(half, feat, own, other, early, first, second)):
+        feat_grad = (before[i][...] + value).T * scales[...]
         if i == 0:
             mine = lax.axis_index("blk") // inner
             mine_grad[...] = feat_grad
@@ -179,29 +185,37 @@
     factor = (size * inner * lax.axis_size("row")) ** (-0.5)
     flops = 6 * feat * (size * inner) ** 2
     grad_shape = jax.ShapeDtypeStruct((feat, size), F32)
-    own, other, hidden, slope = [], [], [], []
     half = inner // 2
+    own, other, hidden, slope = ([None] * inner for _ in range(4))
     part_of = lambda count: [pltpu.VMEM((size * count, width), BF16), pltpu.VMEM((feat, size * count), BF16)]
-    for k in range(inner):
+    for k in [*range(half), *reversed(range(half, inner))]:
+        if k >= half:
+            raws[k] = lax.optimization_barrier((raws[k], done))[0]
         shapes = [jax.ShapeDtypeStruct((size, width), BF16), jax.ShapeDtypeStruct((size, hid), BF16), jax.ShapeDtypeStruct((size, hid), F32)]
-        results = call(forward_kernel, shapes, raws[k], w_in, b_in, w_out, scales, flops=4 * size * w_in.size)
-        for store, result in zip((own, hidden, slope), results):
-            store.append(result)
-        other.append(swap(own[k], "row", 1))
+        weights = (w_in, b_in, w_out, scales)
+        if k == 0:
+            shapes += [jax.ShapeDtypeStruct(a.shape, a.dtype) for a in weights]
+        own[k], hidden[k], slope[k], *handed_on = call(forward_kernel, shapes, raws[k], *weights, flops=4 * size * w_in.size)
+        if k == 0:
+            w_in, b_in, w_out, scales = handed_on
+        other[k] = swap(own[k], "row", 1)
+        done = own[k]
         if k == half - 1:
-            early = call(functools.partial(early_kernel, half, feat), [grad_shape] * half, *own, scratch=part_of(half), flops=flops // 4)
-            for later in range(half, inner):
-                raws[later], early = lax.optimization_barrier((raws[later], early))
+            early, early_other = (
+                call(functools.partial(early_kernel, half, feat), [grad_shape] * half, *own[:half], *visit[:half], scratch=part_of(half), flops=flops * scale)
+                for visit, scale in ((own, 8), (other, 1))
+            )
+            done = (early, early_other)
     before = call(functools.partial(own_kernel, inner, half, feat), [grad_shape] * inner, *own, *early, scratch=part_of(half) * 2, flops=flops)
     feat_grad, part, *grads = call(
-        functools.partial(last_kernel, inner, feat, factor),
+        functools.partial(last_kernel, inner, half, feat, factor),
         [
             jax.ShapeDtypeStruct((rows, feat), F32),
             jax.ShapeDtypeStruct((din + 8, hid), F32),
             *[jax.ShapeDtypeStruct((size, feat), BF16)] * inner,
         ],
-        *own, *other, *before, *raws, *slope, w_out, scales,
-        scratch=[pltpu.VMEM((size, feat), F32), pltpu.VMEM((inner, din + 8, hid), F32), *part_of(inner)],
+        *own, *other, *before, *raws, *slope, *early_other, w_out, scales,
+        scratch=[pltpu.VMEM((size, feat), F32), pltpu.VMEM((inner, din + 8, hid), F32), *part_of(half), *part_of(half)],
         flops=flops,
     )
     part_out = call(

time: 49.7 us -> 48.5 us (0.976)
  local copies, waits for them, and re-layouts: 5.15 us -> 3.24 us
  Pallas kernels: 23.7 us -> 24.7 us
    unnamed x16 -> x8, local copies, waits for them, and re-layouts: 5.15 us -> 3.24 us
    pallas_call x10 -> x11, Pallas kernels: 23.7 us -> 24.7 us  [call(): pl.pallas_call(kernel, out_shape=out, in_specs=[VMEM] * len(args), out_sp...]
  transfers between devices with their start and end apart: 12 -> 12, of which waited for: 5 -> 5; matrix products, arithmetic and copies ran while one was open for 0% -> 0% of each run, Pallas kernels for 26% -> 31%
where the time goes in v5:
time: 48.5 us; the launch traced here: 48.2 us
  Pallas kernels  24.7 us (51%)
  starting transfers between devices  10.6 us (22%)
  waiting for transfers between devices  8.16 us (17%)
  local copies, waits for them, and re-layouts  3.24 us (7%)
  other arithmetic  0.8 us (2%)
  between operations  0.74 us (2%)
    pallas_call x11, Pallas kernels, call(): pl.pallas_call(kernel, out_shape=out, in_specs=[VMEM] * len(args), out_sp...  24.7 us
    ppermute x12, starting transfers between devices, swap(): lax.ppermute(value, axis, [(source, source ^ bits) for source in range(co...  10.6 us
    ppermute x12, waiting for transfers between devices, swap(): lax.ppermute(value, axis, [(source, source ^ bits) for source in range(co...  8.16 us
    unnamed x8, local copies, waits for them, and re-layouts  3.24 us
  transfers between devices with their start and end apart: 12, of which 5 were waited for; matrix products, arithmetic and copies ran while one was open for 0% of the time, Pallas kernels for 31%

profile of v5, /device:TPU:0, one launch (start us, length us, event | category | flops | bytes accessed | tf_op | source)
XLA Modules:
  0.0 48.2 jit_solution(2778187281880523426)
XLA Ops:
  0.6 0.8 %pad_maximum_fusion.refs_0_ = bf16[256,128]{1,0:T(8,128)(2,1)S(1)} fusion(bf16[64,128]{1,0:T(8,128)(2,1)} %bitcast.7, bf16[64,128]{1,0:T(8,128)(2,1)} %bitcast.8, bf16[128,128]{1,0:T(8,128)(2,1)} %param.7), kind=kLoop, calls=%fused_computation | loop fusion | flops 196608 | bytes 131072 | tf_op jit(solution)/shard_map/concatenate | solution.py:181
  1.4 5.0 %collective-permute-start.2 = (bf16[256,128]{1,0:T(8,128)(2,1)S(1)}, bf16[256,128]{1,0:T(8,128)(2,1)S(1)}, u32[]{:S(2)}, u32[]{:S(2)}) collective-permute-start(bf16[256,128]{1,0:T(8,128)(2,1)S(1)} %pad_maximum_fusion.refs_0_), channel_id=1, source_target_pairs={{0,24},{2,26},{4,28},{6,30},{8,16},{10,18},{12,20},{14,22},{16,8},... | collective-permute-start | bytes 196616 | tf_op jit(solution)/shard_map/ppermute | solution.py:169
  6.5 0.6 %collective-permute-start = (bf16[256,128]{1,0:T(8,128)(2,1)S(1)}, bf16[256,128]{1,0:T(8,128)(2,1)S(1)}, u32[]{:S(2)}, u32[]{:S(2)}) collective-permute-start(bf16[256,128]{1,0:T(8,128)(2,1)S(1)} %pad_maximum_fusion.refs_0_), channel_id=1, source_target_pairs={{0,8},{2,10},{4,12},{6,14},{8,0},{10,2},{12,4},{14,6},{16,24},{18,... | collective-permute-start | bytes 196616 | tf_op jit(solution)/shard_map/ppermute | solution.py:169
  7.1 1.9 %collective-permute-done.2.refs_3_ = bf16[256,128]{1,0:T(8,128)(2,1)S(1)} collective-permute-done((bf16[256,128]{1,0:T(8,128)(2,1)S(1)}, bf16[256,128]{1,0:T(8,128)(2,1)S(1)}, u32[]{:S(2)}, u32[]{:S(2)}) %collective-permute-start.2) | collective-permute-done | bytes 65568 | tf_op jit(solution)/shard_map/ppermute | solution.py:169
  9.0 3.0 %collective-permute-done.1.refs_2_ = bf16[256,128]{1,0:T(8,128)(2,1)S(1)} collective-permute-done((bf16[256,128]{1,0:T(8,128)(2,1)S(1)}, bf16[256,128]{1,0:T(8,128)(2,1)S(1)}, u32[]{:S(2)}, u32[]{:S(2)}) %collective-permute-start.1) | collective-permute-done | bytes 65568 | tf_op jit(solution)/shard_map/ppermute | solution.py:169
  12.1 0.1 shard_map.102.raw.refs_12_
  12.2 1.6 %collective-permute-start.3 = (bf16[512,256]{1,0:T(8,128)(2,1)S(1)}, bf16[512,256]{1,0:T(8,128)(2,1)S(1)}, u32[]{:S(2)}, u32[]{:S(2)}) collective-permute-start(bf16[512,256]{1,0:T(8,128)(2,1)S(1)} %shard_map.102.raw.refs_12_), channel_id=1, source_target_pairs={{0,2},{2,0},{4,6},{6,4},{8,10},{10,8},{12,14},{14,12},{16,18},{18,... | collective-permute-start | bytes 786440 | tf_op jit(solution)/shard_map/ppermute | solution.py:169
  13.7 1.5 %collective-permute-start.5 = (bf16[512,256]{1,0:T(8,128)(2,1)S(1)}, bf16[512,256]{1,0:T(8,128)(2,1)S(1)}, u32[]{:S(2)}, u32[]{:S(2)}) collective-permute-start(bf16[512,256]{1,0:T(8,128)(2,1)S(1)} %shard_map.102.raw.refs_12_), channel_id=1, source_target_pairs={{0,6},{2,4},{4,2},{6,0},{8,14},{10,12},{12,10},{14,8},{16,22},{18,... | collective-permute-start | bytes 786440 | tf_op jit(solution)/shard_map/ppermute | solution.py:169
  15.2 0.5 %collective-permute-start.4 = (bf16[512,256]{1,0:T(8,128)(2,1)S(1)}, bf16[512,256]{1,0:T(8,128)(2,1)S(1)}, u32[]{:S(2)}, u32[]{:S(2)}) collective-permute-start(bf16[512,256]{1,0:T(8,128)(2,1)S(1)} %shard_map.102.raw.refs_12_), channel_id=1, source_target_pairs={{0,4},{2,6},{4,0},{6,2},{8,12},{10,14},{12,8},{14,10},{16,20},{18,... | collective-permute-start | bytes 786440 | tf_op jit(solution)/shard_map/ppermute | solution.py:169
  15.7 0.9 %copy-done = bf16[128,1024]{1,0:T(8,128)(2,1)S(1)} copy-done((bf16[128,1024]{1,0:T(8,128)(2,1)S(1)}, bf16[128,1024]{1,0:T(8,128)(2,1)}, u32[]{:S(2)}) %copy-start) | copy-done | bytes 262168
  16.7 0.9 %copy-done.1 = bf16[1024,128]{1,0:T(8,128)(2,1)S(1)} copy-done((bf16[1024,128]{1,0:T(8,128)(2,1)S(1)}, bf16[1024,128]{1,0:T(8,128)(2,1)}, u32[]{:S(2)}) %copy-start.1) | copy-done | bytes 262168
  17.6 0.7 %copy-done.2 = f32[1024]{0:T(1024)S(1)} copy-done((f32[1024]{0:T(1024)S(1)}, f32[1024]{0:T(1024)}, u32[]{:S(2)}) %copy-start.2) | copy-done | bytes 4120
  18.3 0.7 %copy-done.3 = f32[128]{0:T(128)S(1)} copy-done((f32[128]{0:T(128)S(1)}, f32[128]{0:T(128)}, u32[]{:S(2)}) %copy-start.3) | copy-done | bytes 536
  19.0 1.1 %shard_map.103 = (bf16[512,256]{1,0:T(8,128)(2,1)S(1)}, bf16[512,1024]{1,0:T(8,128)(2,1)S(1)}, f32[512,1024]{1,0:T(8,128)S(1)}, bf16[128,1024]{1,0:T(8,128)(2,1)...) custom-call(bf16[512,256]{1,0:T(8,128)(2,1)S(1)} %shard_map.102.raw.refs_12_, ...), custom_call_target="tpu_custom_call" | custom-call | flops 268435456 | bytes 791040 | tf_op jit(solution)/shard_map/pallas_call | solution.py:37
  20.1 0.1 collective-permute-start.6
  20.2 1.3 %collective-permute-done.3.raw.refs_13_ = bf16[512,256]{1,0:T(8,128)(2,1)S(1)} collective-permute-done((bf16[512,256]{1,0:T(8,128)(2,1)S(1)}, bf16[512,256]{1,0:T(8,128)(2,1)S(1)}, u32[]{:S(2)}, u32[]{:S(2)}) %collective-permute-start.3) | collective-permute-done | bytes 262176 | tf_op jit(solution)/shard_map/ppermute | solution.py:169
  21.5 1.1 %shard_map.104 = (bf16[512,256]{1,0:T(8,128)(2,1)S(1)}, bf16[512,1024]{1,0:T(8,128)(2,1)S(1)}, f32[512,1024]{1,0:T(8,128)S(1)}) custom-call(bf16[512,256]{1,0:T(8,128)(2,1)S(1)} %collective-permute-done.3.raw.refs_13_, bf16[128,1024]{1,0:T(8,128)(2,1)S(1)} %get-tuple-element.40.w_in, f32[1,1024]{1,0:T(1,128)S(1)} %get-tuple-element.41.b_in, ...), custom_call_target="tpu_custom_call" | custom-call | flops 268435456 | bytes 791040 | tf_op jit(solution)/shard_map/pallas_call | solution.py:37
  22.6 0.1 collective-permute-start.7
  22.7 2.0 %shard_map.105 = (f32[128,512]{1,0:T(8,128)S(1)}, f32[128,512]{1,0:T(8,128)S(1)}) custom-call(bf16[512,256]{1,0:T(8,128)(2,1)S(1)} %get-tuple-element.39.refs_0_.refs_2_, bf16[512,256]{1,0:T(8,128)(2,1)S(1)} %get-tuple-element.44.refs_1_.refs_3_, bf16[512,256]{1,0:T(8,128)(2,1)S(1)} %get-tuple-element.39.refs_0_.refs_2_, ...), custom_call_target="tpu_custom_call" | custom-call | flops 25769803776 | bytes 1048576 | tf_op jit(solution)/shard_map/pallas_call | solution.py:37
  24.7 2.0 %shard_map.106 = (f32[128,512]{1,0:T(8,128)S(1)}, f32[128,512]{1,0:T(8,128)S(1)}) custom-call(bf16[512,256]{1,0:T(8,128)(2,1)S(1)} %get-tuple-element.39.refs_0_.refs_2_, bf16[512,256]{1,0:T(8,128)(2,1)S(1)} %get-tuple-element.44.refs_1_.refs_3_, bf16[512,256]{1,0:T(8,128)(2,1)S(1)} %collective-permute-done.6.refs_2_.refs_4_, ...), custom_call_target="tpu_custom_call" | custom-call | flops 3221225472 | bytes 1048576 | tf_op jit(solution)/shard_map/pallas_call | solution.py:37
  26.8 0.2 collective-permute-done.5.raw.refs_15_
  27.0 1.1 %shard_map.107 = (bf16[512,256]{1,0:T(8,128)(2,1)S(1)}, bf16[512,1024]{1,0:T(8,128)(2,1)S(1)}, f32[512,1024]{1,0:T(8,128)S(1)}) custom-call(bf16[512,256]{1,0:T(8,128)(2,1)S(1)} %collective-permute-done.5.raw.refs_15_, bf16[128,1024]{1,0:T(8,128)(2,1)S(1)} %get-tuple-element.40.w_in, f32[1,1024]{1,0:T(1,128)S(1)} %get-tuple-element.41.b_in, ...), custom_call_target="tpu_custom_call" | custom-call | flops 268435456 | bytes 791040 | tf_op jit(solution)/shard_map/pallas_call | solution.py:37
  28.1 0.3 collective-permute-start.9
  28.5 1.1 %shard_map.108 = (bf16[512,256]{1,0:T(8,128)(2,1)S(1)}, bf16[512,1024]{1,0:T(8,128)(2,1)S(1)}, f32[512,1024]{1,0:T(8,128)S(1)}) custom-call(bf16[512,256]{1,0:T(8,128)(2,1)S(1)} %collective-permute-done.4.raw.refs_14_, bf16[128,1024]{1,0:T(8,128)(2,1)S(1)} %get-tuple-element.40.w_in, f32[1,1024]{1,0:T(1,128)S(1)} %get-tuple-element.41.b_in, ...), custom_call_target="tpu_custom_call" | custom-call | flops 268435456 | bytes 791040 | tf_op jit(solution)/shard_map/pallas_call | solution.py:37
  29.6 0.3 collective-permute-start.8
  29.9 5.7 %shard_map.109 = (f32[128,512]{1,0:T(8,128)S(1)}, f32[128,512]{1,0:T(8,128)S(1)}, f32[128,512]{1,0:T(8,128)S(1)}, f32[128,512]{1,0:T(8,128)S(1)}) custom-call(bf16[512,256]{1,0:T(8,128)(2,1)S(1)} %get-tuple-element.39.refs_0_.refs_2_, bf16[512,256]{1,0:T(8,128)(2,1)S(1)} %get-tuple-element.44.refs_1_.refs_3_, ...), custom_call_target="tpu_custom_call" | custom-call | flops 3221225472 | bytes 1572864 | tf_op jit(solution)/shard_map/pallas_call | solution.py:37
  35.7 8.4 %shard_map.110 = (f32[128,128]{1,0:T(8,128)}, f32[136,1024]{1,0:T(8,128)S(1)}, bf16[512,128]{1,0:T(8,128)(2,1)S(1)}, bf16[512,128]{1,0:T(8,128)(2,1)S(1)}, bf16[...) custom-call(bf16[512,256]{1,0:T(8,128)(2,1)S(1)} %get-tuple-element.39.refs_0_.refs_2_, ...), custom_call_target="tpu_custom_call" | custom-call | flops 3221225472 | bytes 13369856 | tf_op jit(solution)/shard_map/pallas_call | solution.py:37
  44.0 0.3 collective-permute-start.10
  44.3 0.8 %shard_map.111.mine_out = f32[128,1024]{1,0:T(8,128)S(1)} custom-call(bf16[512,128]{1,0:T(8,128)(2,1)S(1)} %get-tuple-element.63.refs_0_, bf16[512,128]{1,0:T(8,128)(2,1)S(1)} %get-tuple-element.64.refs_1_, bf16[512,128]{1,0:T(8,128)(2,1)S(1)} %get-tuple-element.65.refs_2_, bf16[512,128]{1,0:T(8,128)(2,1)S(1)} %get-tuple-element.66.refs_3_, ...), custom_call_target="tpu_custom_call" | custom-call | bytes 4718592 | tf_op jit(solution)/shard_map/pallas_call | solution.py:37
  45.1 0.3 collective-permute-start.11
  45.4 1.7 %collective-permute-done.11.other_out = f32[128,1024]{1,0:T(8,128)S(1)} collective-permute-done((f32[128,1024]{1,0:T(8,128)S(1)}, f32[128,1024]{1,0:T(8,128)S(1)}, u32[]{:S(2)}, u32[]{:S(2)}) %collective-permute-start.11) | collective-permute-done | bytes 524320 | tf_op jit(solution)/shard_map/ppermute | solution.py:169
  47.0 1.2 %shard_map.112 = (f32[128,1024]{1,0:T(8,128)}, f32[1,1024]{1,0:T(1,128)}, f32[1024,128]{1,0:T(8,128)}) custom-call(f32[136,1024]{1,0:T(8,128)S(1)} %get-tuple-element.62.mine, f32[136,1024]{1,0:T(8,128)S(1)} %collective-permute-done.10.other, f32[128,1024]{1,0:T(8,128)S(1)} %shard_map.111.mine_out, f32[128,1024]{1,0:T(8,128)S(1)} %collective-permute-done.11.other_out), custom_call_target="tpu_custom_call" | custom-call | bytes 2162688 | tf_op jit(solution)/shard_map/pallas_call | solution.py:37
  (12 shorter events, 0.0 us)
Async XLA Ops:
  1.4 7.6 %collective-permute-start.2 = (bf16[256,128]{1,0:T(8,128)(2,1)S(1)}, bf16[256,128]{1,0:T(8,128)(2,1)S(1)}, u32[]{:S(2)}, u32[]{:S(2)}) collective-permute-start(bf16[256,128]{1,0:T(8,128)(2,1)S(1)} %pad_maximum_fusion.refs_0_), channel_id=1, source_target_pairs={{0,24},{2,26},{4,28},{6,30},{8,16},{10,18},{12,20},{14,22},{16,8},... | collective-permute-start | bytes 196616 | tf_op jit(solution)/shard_map/ppermute | solution.py:169
  6.5 5.6 %collective-permute-start.1 = (bf16[256,128]{1,0:T(8,128)(2,1)S(1)}, bf16[256,128]{1,0:T(8,128)(2,1)S(1)}, u32[]{:S(2)}, u32[]{:S(2)}) collective-permute-start(bf16[256,128]{1,0:T(8,128)(2,1)S(1)} %pad_maximum_fusion.refs_0_), channel_id=1, source_target_pairs={{0,16},{2,18},{4,20},{6,22},{8,24},{10,26},{12,28},{14,30},{16,0},... | collective-permute-start | bytes 196616 | tf_op jit(solution)/shard_map/ppermute | solution.py:169
  6.5 5.6 %collective-permute-start = (bf16[256,128]{1,0:T(8,128)(2,1)S(1)}, bf16[256,128]{1,0:T(8,128)(2,1)S(1)}, u32[]{:S(2)}, u32[]{:S(2)}) collective-permute-start(bf16[256,128]{1,0:T(8,128)(2,1)S(1)} %pad_maximum_fusion.refs_0_), channel_id=1, source_target_pairs={{0,8},{2,10},{4,12},{6,14},{8,0},{10,2},{12,4},{14,6},{16,24},{18,... | collective-permute-start | bytes 196616 | tf_op jit(solution)/shard_map/ppermute | solution.py:169
  12.2 9.3 %collective-permute-start.3 = (bf16[512,256]{1,0:T(8,128)(2,1)S(1)}, bf16[512,256]{1,0:T(8,128)(2,1)S(1)}, u32[]{:S(2)}, u32[]{:S(2)}) collective-permute-start(bf16[512,256]{1,0:T(8,128)(2,1)S(1)} %shard_map.102.raw.refs_12_), channel_id=1, source_target_pairs={{0,2},{2,0},{4,6},{6,4},{8,10},{10,8},{12,14},{14,12},{16,18},{18,... | collective-permute-start | bytes 786440 | tf_op jit(solution)/shard_map/ppermute | solution.py:169
  13.7 13.2 %collective-permute-start.5 = (bf16[512,256]{1,0:T(8,128)(2,1)S(1)}, bf16[512,256]{1,0:T(8,128)(2,1)S(1)}, u32[]{:S(2)}, u32[]{:S(2)}) collective-permute-start(bf16[512,256]{1,0:T(8,128)(2,1)S(1)} %shard_map.102.raw.refs_12_), channel_id=1, source_target_pairs={{0,6},{2,4},{4,2},{6,0},{8,14},{10,12},{12,10},{14,8},{16,22},{18,... | collective-permute-start | bytes 786440 | tf_op jit(solution)/shard_map/ppermute | solution.py:169
  15.2 13.2 %collective-permute-start.4 = (bf16[512,256]{1,0:T(8,128)(2,1)S(1)}, bf16[512,256]{1,0:T(8,128)(2,1)S(1)}, u32[]{:S(2)}, u32[]{:S(2)}) collective-permute-start(bf16[512,256]{1,0:T(8,128)(2,1)S(1)} %shard_map.102.raw.refs_12_), channel_id=1, source_target_pairs={{0,4},{2,6},{4,0},{6,2},{8,12},{10,14},{12,8},{14,10},{16,20},{18,... | collective-permute-start | bytes 786440 | tf_op jit(solution)/shard_map/ppermute | solution.py:169
  15.7 0.9 %copy-start = (bf16[128,1024]{1,0:T(8,128)(2,1)S(1)}, bf16[128,1024]{1,0:T(8,128)(2,1)}, u32[]{:S(2)}) copy-start(bf16[128,1024]{1,0:T(8,128)(2,1)} %w_in.1) | copy-start | bytes 786436
  16.7 0.9 %copy-start.1 = (bf16[1024,128]{1,0:T(8,128)(2,1)S(1)}, bf16[1024,128]{1,0:T(8,128)(2,1)}, u32[]{:S(2)}) copy-start(bf16[1024,128]{1,0:T(8,128)(2,1)} %w_out.1) | copy-start | bytes 786436
  17.6 0.7 %copy-start.2 = (f32[1024]{0:T(1024)S(1)}, f32[1024]{0:T(1024)}, u32[]{:S(2)}) copy-start(f32[1024]{0:T(1024)} %param.9) | copy-start | bytes 12292
  18.3 0.7 %copy-start.3 = (f32[128]{0:T(128)S(1)}, f32[128]{0:T(128)}, u32[]{:S(2)}) copy-start(f32[128]{0:T(128)} %param.11) | copy-start | bytes 1540
  20.1 4.6 %collective-permute-start.6 = (bf16[512,256]{1,0:T(8,128)(2,1)S(1)}, bf16[512,256]{1,0:T(8,128)(2,1)S(1)}, u32[]{:S(2)}, u32[]{:S(2)}) collective-permute-start(bf16[512,256]{1,0:T(8,128)(2,1)S(1)} %get-tuple-element.39.refs_0_.refs_2_), channel_id=1, source_target_pairs={{0,1},{1,0},{2,3},{3,2},{4,5},{5,4},{6,7},{7,6},{8,9},{9,8},{10,11... | collective-permute-start | bytes 786440 | tf_op jit(solution)/shard_map/ppermute | solution.py:169
  22.6 2.1 %collective-permute-start.7 = (bf16[512,256]{1,0:T(8,128)(2,1)S(1)}, bf16[512,256]{1,0:T(8,128)(2,1)S(1)}, u32[]{:S(2)}, u32[]{:S(2)}) collective-permute-start(bf16[512,256]{1,0:T(8,128)(2,1)S(1)} %get-tuple-element.44.refs_1_.refs_3_), channel_id=1, source_target_pairs={{0,1},{1,0},{2,3},{3,2},{4,5},{5,4},{6,7},{7,6},{8,9},{9,8},{10,11... | collective-permute-start | bytes 786440 | tf_op jit(solution)/shard_map/ppermute | solution.py:169
  28.1 7.5 %collective-permute-start.9 = (bf16[512,256]{1,0:T(8,128)(2,1)S(1)}, bf16[512,256]{1,0:T(8,128)(2,1)S(1)}, u32[]{:S(2)}, u32[]{:S(2)}) collective-permute-start(bf16[512,256]{1,0:T(8,128)(2,1)S(1)} %get-tuple-element.50.refs_3_), channel_id=1, source_target_pairs={{0,1},{1,0},{2,3},{3,2},{4,5},{5,4},{6,7},{7,6},{8,9},{9,8},{10,11... | collective-permute-start | bytes 786440 | tf_op jit(solution)/shard_map/ppermute | solution.py:169
  29.6 6.0 %collective-permute-start.8 = (bf16[512,256]{1,0:T(8,128)(2,1)S(1)}, bf16[512,256]{1,0:T(8,128)(2,1)S(1)}, u32[]{:S(2)}, u32[]{:S(2)}) collective-permute-start(bf16[512,256]{1,0:T(8,128)(2,1)S(1)} %get-tuple-element.52.refs_2_), channel_id=1, source_target_pairs={{0,1},{1,0},{2,3},{3,2},{4,5},{5,4},{6,7},{7,6},{8,9},{9,8},{10,11... | collective-permute-start | bytes 786440 | tf_op jit(solution)/shard_map/ppermute | solution.py:169
  44.0 3.0 %collective-permute-start.10 = (f32[136,1024]{1,0:T(8,128)S(1)}, f32[136,1024]{1,0:T(8,128)S(1)}, u32[]{:S(2)}, u32[]{:S(2)}) collective-permute-start(f32[136,1024]{1,0:T(8,128)S(1)} %get-tuple-element.62.mine), channel_id=1, source_target_pairs={{0,1},{1,0},{2,3},{3,2},{4,5},{5,4},{6,7},{7,6},{8,9},{9,8},{10,11... | collective-permute-start | bytes 1671176 | tf_op jit(solution)/shard_map/ppermute | solution.py:169
  45.1 2.0 %collective-permute-start.11 = (f32[128,1024]{1,0:T(8,128)S(1)}, f32[128,1024]{1,0:T(8,128)S(1)}, u32[]{:S(2)}, u32[]{:S(2)}) collective-permute-start(f32[128,1024]{1,0:T(8,128)S(1)} %shard_map.111.mine_out), channel_id=1, source_target_pairs={{0,1},{1,0},{2,3},{3,2},{4,5},{5,4},{6,7},{7,6},{8,9},{9,8},{10,11... | collective-permute-start | bytes 1572872 | tf_op jit(solution)/shard_map/ppermute | solution.py:169

commit v6 on v5

--- a/solution.py
+++ b/solution.py
@@ -84,15 +84,16 @@
     return -0.5 * jnp.sum(wide * wide, axis=1, keepdims=True)
 
 
-def visit_all(visit, feat, cols, cols_g):
+def visit_all(visit, feat, cols, cols_g, cols_n):
     size = visit[0].shape[0]
     mine = lax.axis_index("blk") % len(visit)
     for k, plane in enumerate(visit):
         cols[pl.ds(pl.multiple_of((mine ^ k) * size, size), size), :] = plane[...]
     cols_g[...] = cols[:, :feat].T
-
-
-def pair_sums(plane, feat, step, cols, cols_g):
+    cols_n[...] = jnp.broadcast_to(half_norms(cols[:, :feat]), cols_n.shape)
+
+
+def pair_sums(plane, feat, step, cols, cols_g, cols_n):
     half = (plane.shape[1] - feat) // 2
     rows = plane.shape[0]
     g = plane[:, :feat]
@@ -101,7 +102,8 @@
     total, sums = jnp.zeros((feat, rows), F32), jnp.zeros((8, rows), F32)
     for at in range(0, cols.shape[0], step):
         visit_g = cols[at : at + step, :feat]
-        kern = jnp.exp(dot(visit_g, g, NT) + half_norms(visit_g) + across)
+        down = jnp.concatenate([cols_n[at : at + step, :]] * (rows // LANES), axis=1)
+        kern = jnp.exp(dot(visit_g, g, NT) + down + across)
         weight = dot(cols[at : at + step, feat:], swapped, NT) * kern
         sums += jnp.sum(weight.reshape(step // 8, 8, rows), axis=0)
         total += dot(cols_g[:, at : at + step], weight.astype(BF16))
@@ -109,10 +111,10 @@
 
 
 def early_kernel(half, feat, *refs):
-    own, visit, outs, (cols, cols_g) = refs[:half], refs[half : 2 * half], refs[2 * half : -2], refs[-2:]
-    visit_all(visit, feat, cols, cols_g)
+    own, visit, outs, near = refs[:half], refs[half : 2 * half], refs[2 * half : -3], refs[-3:]
+    visit_all(visit, feat, *near)
     for plane, out in zip(own, outs):
-        out[...] = pair_sums(plane, feat, cols.shape[0], cols, cols_g)
+        out[...] = pair_sums(plane, feat, near[0].shape[0], *near)
 
 
 def all_sums(half, feat, home, visit, early, first, second):
@@ -124,8 +126,8 @@
 
 
 def own_kernel(inner, half, feat, *refs):
-    own, early, outs = refs[:inner], refs[inner : inner + half], refs[inner + half : -4]
-    for out, value in zip(outs, all_sums(half, feat, own, own, early, refs[-4:-2], refs[-2:])):
+    own, early, outs = refs[:inner], refs[inner : inner + half], refs[inner + half : -6]
+    for out, value in zip(outs, all_sums(half, feat, own, own, early, refs[-6:-3], refs[-3:])):
         out[...] = value
 
 
@@ -133,7 +135,7 @@
     own, other, before, raw, slope = (refs[i * inner : (i + 1) * inner] for i in range(5))
     early, refs = refs[5 * inner : 5 * inner + half], refs[5 * inner + half :]
     w_out, scales, feat_grad_out, part = refs[:4]
-    grads, (mine_grad, sums), first, second = refs[4:-6], refs[-6:-4], refs[-4:-2], refs[-2:]
+    grads, (mine_grad, sums), first, second = refs[4:-8], refs[-8:-6], refs[-6:-3], refs[-3:]
     rows = feat_grad_out.shape[0]
     din = sums.shape[1] - 8
     for i, value in enumerate(all_sums(half, feat, own, other, early, first, second)):
@@ -187,7 +189,7 @@
     grad_shape = jax.ShapeDtypeStruct((feat, size), F32)
     half = inner // 2
     own, other, hidden, slope = ([None] * inner for _ in range(4))
-    part_of = lambda count: [pltpu.VMEM((size * count, width), BF16), pltpu.VMEM((feat, size * count), BF16)]
+    part_of = lambda count: [pltpu.VMEM((size * count, width), BF16), pltpu.VMEM((feat, size * count), BF16), pltpu.VMEM((size * count, LANES), F32)]
     for k in [*range(half), *reversed(range(half, inner))]:
         if k >= half:
             raws[k] = lax.optimization_barrier((raws[k], done))[0]

time: 48.5 us -> 48.3 us (level)
  no operation moved by 1% of the time
where the time goes in v6:
time: 48.3 us; the launch traced here: 48 us
  Pallas kernels  24.5 us (51%)
  starting transfers between devices  10.6 us (22%)
  waiting for transfers between devices  8.15 us (17%)
  local copies, waits for them, and re-layouts  3.24 us (7%)
  other arithmetic  0.8 us (2%)
  between operations  0.74 us (2%)
    pallas_call x11, Pallas kernels, call(): pl.pallas_call(kernel, out_shape=out, in_specs=[VMEM] * len(args), out_sp...  24.5 us
    ppermute x12, starting transfers between devices, swap(): lax.ppermute(value, axis, [(source, source ^ bits) for source in range(co...  10.6 us
    ppermute x12, waiting for transfers between devices, swap(): lax.ppermute(value, axis, [(source, source ^ bits) for source in range(co...  8.15 us
    unnamed x8, local copies, waits for them, and re-layouts  3.24 us
  transfers between devices with their start and end apart: 12, of which 5 were waited for; matrix products, arithmetic and copies ran while one was open for 0% of the time, Pallas kernels for 31%

profile of v6, /device:TPU:0, one launch (start us, length us, event | category | flops | bytes accessed | tf_op | source)
XLA Modules:
  0.0 48.0 jit_solution(10549086925196398313)
XLA Ops:
  0.6 0.8 %pad_maximum_fusion.refs_0_ = bf16[256,128]{1,0:T(8,128)(2,1)S(1)} fusion(bf16[64,128]{1,0:T(8,128)(2,1)} %bitcast.7, bf16[64,128]{1,0:T(8,128)(2,1)} %bitcast.8, bf16[128,128]{1,0:T(8,128)(2,1)} %param.7), kind=kLoop, calls=%fused_computation | loop fusion | flops 196608 | bytes 131072 | tf_op jit(solution)/shard_map/concatenate | solution.py:183
  1.4 5.0 %collective-permute-start.2 = (bf16[256,128]{1,0:T(8,128)(2,1)S(1)}, bf16[256,128]{1,0:T(8,128)(2,1)S(1)}, u32[]{:S(2)}, u32[]{:S(2)}) collective-permute-start(bf16[256,128]{1,0:T(8,128)(2,1)S(1)} %pad_maximum_fusion.refs_0_), channel_id=1, source_target_pairs={{0,24},{2,26},{4,28},{6,30},{8,16},{10,18},{12,20},{14,22},{16,8},... | collective-permute-start | bytes 196616 | tf_op jit(solution)/shard_map/ppermute | solution.py:171
  6.5 0.6 %collective-permute-start = (bf16[256,128]{1,0:T(8,128)(2,1)S(1)}, bf16[256,128]{1,0:T(8,128)(2,1)S(1)}, u32[]{:S(2)}, u32[]{:S(2)}) collective-permute-start(bf16[256,128]{1,0:T(8,128)(2,1)S(1)} %pad_maximum_fusion.refs_0_), channel_id=1, source_target_pairs={{0,8},{2,10},{4,12},{6,14},{8,0},{10,2},{12,4},{14,6},{16,24},{18,... | collective-permute-start | bytes 196616 | tf_op jit(solution)/shard_map/ppermute | solution.py:171
  7.1 1.9 %collective-permute-done.2.refs_3_ = bf16[256,128]{1,0:T(8,128)(2,1)S(1)} collective-permute-done((bf16[256,128]{1,0:T(8,128)(2,1)S(1)}, bf16[256,128]{1,0:T(8,128)(2,1)S(1)}, u32[]{:S(2)}, u32[]{:S(2)}) %collective-permute-start.2) | collective-permute-done | bytes 65568 | tf_op jit(solution)/shard_map/ppermute | solution.py:171
  9.0 3.0 %collective-permute-done.1.refs_2_ = bf16[256,128]{1,0:T(8,128)(2,1)S(1)} collective-permute-done((bf16[256,128]{1,0:T(8,128)(2,1)S(1)}, bf16[256,128]{1,0:T(8,128)(2,1)S(1)}, u32[]{:S(2)}, u32[]{:S(2)}) %collective-permute-start.1) | collective-permute-done | bytes 65568 | tf_op jit(solution)/shard_map/ppermute | solution.py:171
  12.1 0.1 shard_map.102.raw.refs_12_
  12.2 1.6 %collective-permute-start.3 = (bf16[512,256]{1,0:T(8,128)(2,1)S(1)}, bf16[512,256]{1,0:T(8,128)(2,1)S(1)}, u32[]{:S(2)}, u32[]{:S(2)}) collective-permute-start(bf16[512,256]{1,0:T(8,128)(2,1)S(1)} %shard_map.102.raw.refs_12_), channel_id=1, source_target_pairs={{0,2},{2,0},{4,6},{6,4},{8,10},{10,8},{12,14},{14,12},{16,18},{18,... | collective-permute-start | bytes 786440 | tf_op jit(solution)/shard_map/ppermute | solution.py:171
  13.7 1.5 %collective-permute-start.5 = (bf16[512,256]{1,0:T(8,128)(2,1)S(1)}, bf16[512,256]{1,0:T(8,128)(2,1)S(1)}, u32[]{:S(2)}, u32[]{:S(2)}) collective-permute-start(bf16[512,256]{1,0:T(8,128)(2,1)S(1)} %shard_map.102.raw.refs_12_), channel_id=1, source_target_pairs={{0,6},{2,4},{4,2},{6,0},{8,14},{10,12},{12,10},{14,8},{16,22},{18,... | collective-permute-start | bytes 786440 | tf_op jit(solution)/shard_map/ppermute | solution.py:171
  15.2 0.5 %collective-permute-start.4 = (bf16[512,256]{1,0:T(8,128)(2,1)S(1)}, bf16[512,256]{1,0:T(8,128)(2,1)S(1)}, u32[]{:S(2)}, u32[]{:S(2)}) collective-permute-start(bf16[512,256]{1,0:T(8,128)(2,1)S(1)} %shard_map.102.raw.refs_12_), channel_id=1, source_target_pairs={{0,4},{2,6},{4,0},{6,2},{8,12},{10,14},{12,8},{14,10},{16,20},{18,... | collective-permute-start | bytes 786440 | tf_op jit(solution)/shard_map/ppermute | solution.py:171
  15.7 0.9 %copy-done = bf16[128,1024]{1,0:T(8,128)(2,1)S(1)} copy-done((bf16[128,1024]{1,0:T(8,128)(2,1)S(1)}, bf16[128,1024]{1,0:T(8,128)(2,1)}, u32[]{:S(2)}) %copy-start) | copy-done | bytes 262168
  16.7 0.9 %copy-done.1 = bf16[1024,128]{1,0:T(8,128)(2,1)S(1)} copy-done((bf16[1024,128]{1,0:T(8,128)(2,1)S(1)}, bf16[1024,128]{1,0:T(8,128)(2,1)}, u32[]{:S(2)}) %copy-start.1) | copy-done | bytes 262168
  17.6 0.7 %copy-done.2 = f32[1024]{0:T(1024)S(1)} copy-done((f32[1024]{0:T(1024)S(1)}, f32[1024]{0:T(1024)}, u32[]{:S(2)}) %copy-start.2) | copy-done | bytes 4120
  18.3 0.7 %copy-done.3 = f32[128]{0:T(128)S(1)} copy-done((f32[128]{0:T(128)S(1)}, f32[128]{0:T(128)}, u32[]{:S(2)}) %copy-start.3) | copy-done | bytes 536
  19.0 1.1 %shard_map.103 = (bf16[512,256]{1,0:T(8,128)(2,1)S(1)}, bf16[512,1024]{1,0:T(8,128)(2,1)S(1)}, f32[512,1024]{1,0:T(8,128)S(1)}, bf16[128,1024]{1,0:T(8,128)(2,1)...) custom-call(bf16[512,256]{1,0:T(8,128)(2,1)S(1)} %shard_map.102.raw.refs_12_, ...), custom_call_target="tpu_custom_call" | custom-call | flops 268435456 | bytes 791040 | tf_op jit(solution)/shard_map/pallas_call | solution.py:37
  20.1 0.1 collective-permute-start.6
  20.2 1.3 %collective-permute-done.3.raw.refs_13_ = bf16[512,256]{1,0:T(8,128)(2,1)S(1)} collective-permute-done((bf16[512,256]{1,0:T(8,128)(2,1)S(1)}, bf16[512,256]{1,0:T(8,128)(2,1)S(1)}, u32[]{:S(2)}, u32[]{:S(2)}) %collective-permute-start.3) | collective-permute-done | bytes 262176 | tf_op jit(solution)/shard_map/ppermute | solution.py:171
  21.5 1.1 %shard_map.104 = (bf16[512,256]{1,0:T(8,128)(2,1)S(1)}, bf16[512,1024]{1,0:T(8,128)(2,1)S(1)}, f32[512,1024]{1,0:T(8,128)S(1)}) custom-call(bf16[512,256]{1,0:T(8,128)(2,1)S(1)} %collective-permute-done.3.raw.refs_13_, bf16[128,1024]{1,0:T(8,128)(2,1)S(1)} %get-tuple-element.40.w_in, f32[1,1024]{1,0:T(1,128)S(1)} %get-tuple-element.41.b_in, ...), custom_call_target="tpu_custom_call" | custom-call | flops 268435456 | bytes 791040 | tf_op jit(solution)/shard_map/pallas_call | solution.py:37
  22.6 0.1 collective-permute-start.7
  22.7 2.0 %shard_map.105 = (f32[128,512]{1,0:T(8,128)S(1)}, f32[128,512]{1,0:T(8,128)S(1)}) custom-call(bf16[512,256]{1,0:T(8,128)(2,1)S(1)} %get-tuple-element.39.refs_0_.refs_2_, bf16[512,256]{1,0:T(8,128)(2,1)S(1)} %get-tuple-element.44.refs_1_.refs_3_, bf16[512,256]{1,0:T(8,128)(2,1)S(1)} %get-tuple-element.39.refs_0_.refs_2_, ...), custom_call_target="tpu_custom_call" | custom-call | flops 25769803776 | bytes 1048576 | tf_op jit(solution)/shard_map/pallas_call | solution.py:37
  24.8 2.1 %shard_map.106 = (f32[128,512]{1,0:T(8,128)S(1)}, f32[128,512]{1,0:T(8,128)S(1)}) custom-call(bf16[512,256]{1,0:T(8,128)(2,1)S(1)} %get-tuple-element.39.refs_0_.refs_2_, bf16[512,256]{1,0:T(8,128)(2,1)S(1)} %get-tuple-element.44.refs_1_.refs_3_, bf16[512,256]{1,0:T(8,128)(2,1)S(1)} %collective-permute-done.6.refs_2_.refs_4_, ...), custom_call_target="tpu_custom_call" | custom-call | flops 3221225472 | bytes 1048576 | tf_op jit(solution)/shard_map/pallas_call | solution.py:37
  26.8 0.2 collective-permute-done.5.raw.refs_15_
  27.0 1.1 %shard_map.107 = (bf16[512,256]{1,0:T(8,128)(2,1)S(1)}, bf16[512,1024]{1,0:T(8,128)(2,1)S(1)}, f32[512,1024]{1,0:T(8,128)S(1)}) custom-call(bf16[512,256]{1,0:T(8,128)(2,1)S(1)} %collective-permute-done.5.raw.refs_15_, bf16[128,1024]{1,0:T(8,128)(2,1)S(1)} %get-tuple-element.40.w_in, f32[1,1024]{1,0:T(1,128)S(1)} %get-tuple-element.41.b_in, ...), custom_call_target="tpu_custom_call" | custom-call | flops 268435456 | bytes 791040 | tf_op jit(solution)/shard_map/pallas_call | solution.py:37
  28.1 0.4 collective-permute-start.9
  28.5 1.1 %shard_map.108 = (bf16[512,256]{1,0:T(8,128)(2,1)S(1)}, bf16[512,1024]{1,0:T(8,128)(2,1)S(1)}, f32[512,1024]{1,0:T(8,128)S(1)}) custom-call(bf16[512,256]{1,0:T(8,128)(2,1)S(1)} %collective-permute-done.4.raw.refs_14_, bf16[128,1024]{1,0:T(8,128)(2,1)S(1)} %get-tuple-element.40.w_in, f32[1,1024]{1,0:T(1,128)S(1)} %get-tuple-element.41.b_in, ...), custom_call_target="tpu_custom_call" | custom-call | flops 268435456 | bytes 791040 | tf_op jit(solution)/shard_map/pallas_call | solution.py:37
  29.7 0.2 collective-permute-start.8
  29.9 5.6 %shard_map.109 = (f32[128,512]{1,0:T(8,128)S(1)}, f32[128,512]{1,0:T(8,128)S(1)}, f32[128,512]{1,0:T(8,128)S(1)}, f32[128,512]{1,0:T(8,128)S(1)}) custom-call(bf16[512,256]{1,0:T(8,128)(2,1)S(1)} %get-tuple-element.39.refs_0_.refs_2_, bf16[512,256]{1,0:T(8,128)(2,1)S(1)} %get-tuple-element.44.refs_1_.refs_3_, ...), custom_call_target="tpu_custom_call" | custom-call | flops 3221225472 | bytes 1572864 | tf_op jit(solution)/shard_map/pallas_call | solution.py:37
  35.5 8.2 %shard_map.110 = (f32[128,128]{1,0:T(8,128)}, f32[136,1024]{1,0:T(8,128)S(1)}, bf16[512,128]{1,0:T(8,128)(2,1)S(1)}, bf16[512,128]{1,0:T(8,128)(2,1)S(1)}, bf16[...) custom-call(bf16[512,256]{1,0:T(8,128)(2,1)S(1)} %get-tuple-element.39.refs_0_.refs_2_, ...), custom_call_target="tpu_custom_call" | custom-call | flops 3221225472 | bytes 13369856 | tf_op jit(solution)/shard_map/pallas_call | solution.py:37
  43.7 0.3 collective-permute-start.10
  44.1 0.8 %shard_map.111.mine_out = f32[128,1024]{1,0:T(8,128)S(1)} custom-call(bf16[512,128]{1,0:T(8,128)(2,1)S(1)} %get-tuple-element.63.refs_0_, bf16[512,128]{1,0:T(8,128)(2,1)S(1)} %get-tuple-element.64.refs_1_, bf16[512,128]{1,0:T(8,128)(2,1)S(1)} %get-tuple-element.65.refs_2_, bf16[512,128]{1,0:T(8,128)(2,1)S(1)} %get-tuple-element.66.refs_3_, ...), custom_call_target="tpu_custom_call" | custom-call | bytes 4718592 | tf_op jit(solution)/shard_map/pallas_call | solution.py:37
  44.8 0.2 collective-permute-start.11
  45.1 1.7 %collective-permute-done.11.other_out = f32[128,1024]{1,0:T(8,128)S(1)} collective-permute-done((f32[128,1024]{1,0:T(8,128)S(1)}, f32[128,1024]{1,0:T(8,128)S(1)}, u32[]{:S(2)}, u32[]{:S(2)}) %collective-permute-start.11) | collective-permute-done | bytes 524320 | tf_op jit(solution)/shard_map/ppermute | solution.py:171
  46.8 1.2 %shard_map.112 = (f32[128,1024]{1,0:T(8,128)}, f32[1,1024]{1,0:T(1,128)}, f32[1024,128]{1,0:T(8,128)}) custom-call(f32[136,1024]{1,0:T(8,128)S(1)} %get-tuple-element.62.mine, f32[136,1024]{1,0:T(8,128)S(1)} %collective-permute-done.10.other, f32[128,1024]{1,0:T(8,128)S(1)} %shard_map.111.mine_out, f32[128,1024]{1,0:T(8,128)S(1)} %collective-permute-done.11.other_out), custom_call_target="tpu_custom_call" | custom-call | bytes 2162688 | tf_op jit(solution)/shard_map/pallas_call | solution.py:37
  (12 shorter events, 0.0 us)
Async XLA Ops:
  1.4 7.6 %collective-permute-start.2 = (bf16[256,128]{1,0:T(8,128)(2,1)S(1)}, bf16[256,128]{1,0:T(8,128)(2,1)S(1)}, u32[]{:S(2)}, u32[]{:S(2)}) collective-permute-start(bf16[256,128]{1,0:T(8,128)(2,1)S(1)} %pad_maximum_fusion.refs_0_), channel_id=1, source_target_pairs={{0,24},{2,26},{4,28},{6,30},{8,16},{10,18},{12,20},{14,22},{16,8},... | collective-permute-start | bytes 196616 | tf_op jit(solution)/shard_map/ppermute | solution.py:171
  6.5 5.6 %collective-permute-start.1 = (bf16[256,128]{1,0:T(8,128)(2,1)S(1)}, bf16[256,128]{1,0:T(8,128)(2,1)S(1)}, u32[]{:S(2)}, u32[]{:S(2)}) collective-permute-start(bf16[256,128]{1,0:T(8,128)(2,1)S(1)} %pad_maximum_fusion.refs_0_), channel_id=1, source_target_pairs={{0,16},{2,18},{4,20},{6,22},{8,24},{10,26},{12,28},{14,30},{16,0},... | collective-permute-start | bytes 196616 | tf_op jit(solution)/shard_map/ppermute | solution.py:171
  6.5 5.6 %collective-permute-start = (bf16[256,128]{1,0:T(8,128)(2,1)S(1)}, bf16[256,128]{1,0:T(8,128)(2,1)S(1)}, u32[]{:S(2)}, u32[]{:S(2)}) collective-permute-start(bf16[256,128]{1,0:T(8,128)(2,1)S(1)} %pad_maximum_fusion.refs_0_), channel_id=1, source_target_pairs={{0,8},{2,10},{4,12},{6,14},{8,0},{10,2},{12,4},{14,6},{16,24},{18,... | collective-permute-start | bytes 196616 | tf_op jit(solution)/shard_map/ppermute | solution.py:171
  12.2 9.3 %collective-permute-start.3 = (bf16[512,256]{1,0:T(8,128)(2,1)S(1)}, bf16[512,256]{1,0:T(8,128)(2,1)S(1)}, u32[]{:S(2)}, u32[]{:S(2)}) collective-permute-start(bf16[512,256]{1,0:T(8,128)(2,1)S(1)} %shard_map.102.raw.refs_12_), channel_id=1, source_target_pairs={{0,2},{2,0},{4,6},{6,4},{8,10},{10,8},{12,14},{14,12},{16,18},{18,... | collective-permute-start | bytes 786440 | tf_op jit(solution)/shard_map/ppermute | solution.py:171
  13.7 13.2 %collective-permute-start.5 = (bf16[512,256]{1,0:T(8,128)(2,1)S(1)}, bf16[512,256]{1,0:T(8,128)(2,1)S(1)}, u32[]{:S(2)}, u32[]{:S(2)}) collective-permute-start(bf16[512,256]{1,0:T(8,128)(2,1)S(1)} %shard_map.102.raw.refs_12_), channel_id=1, source_target_pairs={{0,6},{2,4},{4,2},{6,0},{8,14},{10,12},{12,10},{14,8},{16,22},{18,... | collective-permute-start | bytes 786440 | tf_op jit(solution)/shard_map/ppermute | solution.py:171
  15.2 13.3 %collective-permute-start.4 = (bf16[512,256]{1,0:T(8,128)(2,1)S(1)}, bf16[512,256]{1,0:T(8,128)(2,1)S(1)}, u32[]{:S(2)}, u32[]{:S(2)}) collective-permute-start(bf16[512,256]{1,0:T(8,128)(2,1)S(1)} %shard_map.102.raw.refs_12_), channel_id=1, source_target_pairs={{0,4},{2,6},{4,0},{6,2},{8,12},{10,14},{12,8},{14,10},{16,20},{18,... | collective-permute-start | bytes 786440 | tf_op jit(solution)/shard_map/ppermute | solution.py:171
  15.7 0.9 %copy-start = (bf16[128,1024]{1,0:T(8,128)(2,1)S(1)}, bf16[128,1024]{1,0:T(8,128)(2,1)}, u32[]{:S(2)}) copy-start(bf16[128,1024]{1,0:T(8,128)(2,1)} %w_in.1) | copy-start | bytes 786436
  16.7 0.9 %copy-start.1 = (bf16[1024,128]{1,0:T(8,128)(2,1)S(1)}, bf16[1024,128]{1,0:T(8,128)(2,1)}, u32[]{:S(2)}) copy-start(bf16[1024,128]{1,0:T(8,128)(2,1)} %w_out.1) | copy-start | bytes 786436
  17.6 0.7 %copy-start.2 = (f32[1024]{0:T(1024)S(1)}, f32[1024]{0:T(1024)}, u32[]{:S(2)}) copy-start(f32[1024]{0:T(1024)} %param.9) | copy-start | bytes 12292
  18.3 0.7 %copy-start.3 = (f32[128]{0:T(128)S(1)}, f32[128]{0:T(128)}, u32[]{:S(2)}) copy-start(f32[128]{0:T(128)} %param.11) | copy-start | bytes 1540
  20.1 4.6 %collective-permute-start.6 = (bf16[512,256]{1,0:T(8,128)(2,1)S(1)}, bf16[512,256]{1,0:T(8,128)(2,1)S(1)}, u32[]{:S(2)}, u32[]{:S(2)}) collective-permute-start(bf16[512,256]{1,0:T(8,128)(2,1)S(1)} %get-tuple-element.39.refs_0_.refs_2_), channel_id=1, source_target_pairs={{0,1},{1,0},{2,3},{3,2},{4,5},{5,4},{6,7},{7,6},{8,9},{9,8},{10,11... | collective-permute-start | bytes 786440 | tf_op jit(solution)/shard_map/ppermute | solution.py:171
  22.6 2.1 %collective-permute-start.7 = (bf16[512,256]{1,0:T(8,128)(2,1)S(1)}, bf16[512,256]{1,0:T(8,128)(2,1)S(1)}, u32[]{:S(2)}, u32[]{:S(2)}) collective-permute-start(bf16[512,256]{1,0:T(8,128)(2,1)S(1)} %get-tuple-element.44.refs_1_.refs_3_), channel_id=1, source_target_pairs={{0,1},{1,0},{2,3},{3,2},{4,5},{5,4},{6,7},{7,6},{8,9},{9,8},{10,11... | collective-permute-start | bytes 786440 | tf_op jit(solution)/shard_map/ppermute | solution.py:171
  28.1 7.4 %collective-permute-start.9 = (bf16[512,256]{1,0:T(8,128)(2,1)S(1)}, bf16[512,256]{1,0:T(8,128)(2,1)S(1)}, u32[]{:S(2)}, u32[]{:S(2)}) collective-permute-start(bf16[512,256]{1,0:T(8,128)(2,1)S(1)} %get-tuple-element.50.refs_3_), channel_id=1, source_target_pairs={{0,1},{1,0},{2,3},{3,2},{4,5},{5,4},{6,7},{7,6},{8,9},{9,8},{10,11... | collective-permute-start | bytes 786440 | tf_op jit(solution)/shard_map/ppermute | solution.py:171
  29.7 5.9 %collective-permute-start.8 = (bf16[512,256]{1,0:T(8,128)(2,1)S(1)}, bf16[512,256]{1,0:T(8,128)(2,1)S(1)}, u32[]{:S(2)}, u32[]{:S(2)}) collective-permute-start(bf16[512,256]{1,0:T(8,128)(2,1)S(1)} %get-tuple-element.52.refs_2_), channel_id=1, source_target_pairs={{0,1},{1,0},{2,3},{3,2},{4,5},{5,4},{6,7},{7,6},{8,9},{9,8},{10,11... | collective-permute-start | bytes 786440 | tf_op jit(solution)/shard_map/ppermute | solution.py:171
  43.7 3.1 %collective-permute-start.10 = (f32[136,1024]{1,0:T(8,128)S(1)}, f32[136,1024]{1,0:T(8,128)S(1)}, u32[]{:S(2)}, u32[]{:S(2)}) collective-permute-start(f32[136,1024]{1,0:T(8,128)S(1)} %get-tuple-element.62.mine), channel_id=1, source_target_pairs={{0,1},{1,0},{2,3},{3,2},{4,5},{5,4},{6,7},{7,6},{8,9},{9,8},{10,11... | collective-permute-start | bytes 1671176 | tf_op jit(solution)/shard_map/ppermute | solution.py:171
  44.8 2.0 %collective-permute-start.11 = (f32[128,1024]{1,0:T(8,128)S(1)}, f32[128,1024]{1,0:T(8,128)S(1)}, u32[]{:S(2)}, u32[]{:S(2)}) collective-permute-start(f32[128,1024]{1,0:T(8,128)S(1)} %shard_map.111.mine_out), channel_id=1, source_target_pairs={{0,1},{1,0},{2,3},{3,2},{4,5},{5,4},{6,7},{7,6},{8,9},{9,8},{10,11... | collective-permute-start | bytes 1572872 | tf_op jit(solution)/shard_map/ppermute | solution.py:171

commit v7 on v6

--- a/solution.py
+++ b/solution.py
@@ -138,14 +138,16 @@
     grads, (mine_grad, sums), first, second = refs[4:-8], refs[-8:-6], refs[-6:-3], refs[-3:]
     rows = feat_grad_out.shape[0]
     din = sums.shape[1] - 8
+    down = jnp.broadcast_to(scales[...], (LANES, feat)).T[:, :1]
     for i, value in enumerate(all_sums(half, feat, own, other, early, first, second)):
-        feat_grad = (before[i][...] + value).T * scales[...]
+        across = (before[i][...] + value) * down
+        feat_grad = across.T
         if i == 0:
             mine = lax.axis_index("blk") // inner
             mine_grad[...] = feat_grad
             feat_grad_out[...] = mine_grad[pl.ds(pl.multiple_of(mine * rows, rows), rows), :]
         feat_grad_b = feat_grad.astype(BF16)
-        grads[i][...] = feat_grad_b
+        grads[i][...] = across.astype(BF16)
         pre_grad = dot(feat_grad_b, w_out[...], NT) * slope[i][...]
         sums[i, :din, :] = factor * dot(raw[i][:, :din], pre_grad.astype(BF16), TN)
         sums[i, din:, :] = factor * jnp.sum(pre_grad.reshape(-1, 8, pre_grad.shape[1]), axis=0)
@@ -155,7 +157,7 @@
 def out_kernel(inner, factor, *refs):
     grads, hidden, (part, sums) = refs[:inner], refs[inner : 2 * inner], refs[2 * inner :]
     for i in range(inner):
-        sums[i] = factor * dot(grads[i][...], hidden[i][...], TN)
+        sums[i] = factor * dot(grads[i][...], hidden[i][...])
     part[...] = tree([sums[i] for i in range(inner)])
 
 
@@ -214,7 +216,7 @@
         [
             jax.ShapeDtypeStruct((rows, feat), F32),
             jax.ShapeDtypeStruct((din + 8, hid), F32),
-            *[jax.ShapeDtypeStruct((size, feat), BF16)] * inner,
+            *[jax.ShapeDtypeStruct((feat, size), BF16)] * inner,
         ],
         *own, *other, *before, *raws, *slope, *early_other, w_out, scales,
         scratch=[pltpu.VMEM((size, feat), F32), pltpu.VMEM((inner, din + 8, hid), F32), *part_of(half), *part_of(half)],

time: 48.3 us -> 48.6 us (level)
  no operation moved by 1% of the time
where the time goes in v7:
time: 48.6 us; the launch traced here: 48.3 us
  Pallas kernels  24.7 us (51%)
  starting transfers between devices  10.7 us (22%)
  waiting for transfers between devices  8.16 us (17%)
  local copies, waits for them, and re-layouts  3.24 us (7%)
  other arithmetic  0.8 us (2%)
  between operations  0.75 us (2%)
    pallas_call x11, Pallas kernels, call(): pl.pallas_call(kernel, out_shape=out, in_specs=[VMEM] * len(args), out_sp...  24.7 us
    ppermute x12, starting transfers between devices, swap(): lax.ppermute(value, axis, [(source, source ^ bits) for source in range(co...  10.7 us
    ppermute x12, waiting for transfers between devices, swap(): lax.ppermute(value, axis, [(source, source ^ bits) for source in range(co...  8.16 us
    unnamed x8, local copies, waits for them, and re-layouts  3.24 us
  transfers between devices with their start and end apart: 12, of which 5 were waited for; matrix products, arithmetic and copies ran while one was open for 0% of the time, Pallas kernels for 31%

profile of v7, /device:TPU:0, one launch (start us, length us, event | category | flops | bytes accessed | tf_op | source)
XLA Modules:
  0.0 48.3 jit_solution(3614555985737253725)
XLA Ops:
  0.6 0.8 %pad_maximum_fusion.refs_0_ = bf16[256,128]{1,0:T(8,128)(2,1)S(1)} fusion(bf16[64,128]{1,0:T(8,128)(2,1)} %bitcast.7, bf16[64,128]{1,0:T(8,128)(2,1)} %bitcast.8, bf16[128,128]{1,0:T(8,128)(2,1)} %param.7), kind=kLoop, calls=%fused_computation | loop fusion | flops 196608 | bytes 131072 | tf_op jit(solution)/shard_map/concatenate | solution.py:185
  1.4 5.0 %collective-permute-start.2 = (bf16[256,128]{1,0:T(8,128)(2,1)S(1)}, bf16[256,128]{1,0:T(8,128)(2,1)S(1)}, u32[]{:S(2)}, u32[]{:S(2)}) collective-permute-start(bf16[256,128]{1,0:T(8,128)(2,1)S(1)} %pad_maximum_fusion.refs_0_), channel_id=1, source_target_pairs={{0,24},{2,26},{4,28},{6,30},{8,16},{10,18},{12,20},{14,22},{16,8},... | collective-permute-start | bytes 196616 | tf_op jit(solution)/shard_map/ppermute | solution.py:173
  6.5 0.6 %collective-permute-start = (bf16[256,128]{1,0:T(8,128)(2,1)S(1)}, bf16[256,128]{1,0:T(8,128)(2,1)S(1)}, u32[]{:S(2)}, u32[]{:S(2)}) collective-permute-start(bf16[256,128]{1,0:T(8,128)(2,1)S(1)} %pad_maximum_fusion.refs_0_), channel_id=1, source_target_pairs={{0,8},{2,10},{4,12},{6,14},{8,0},{10,2},{12,4},{14,6},{16,24},{18,... | collective-permute-start | bytes 196616 | tf_op jit(solution)/shard_map/ppermute | solution.py:173
  7.1 1.9 %collective-permute-done.2.refs_3_ = bf16[256,128]{1,0:T(8,128)(2,1)S(1)} collective-permute-done((bf16[256,128]{1,0:T(8,128)(2,1)S(1)}, bf16[256,128]{1,0:T(8,128)(2,1)S(1)}, u32[]{:S(2)}, u32[]{:S(2)}) %collective-permute-start.2) | collective-permute-done | bytes 65568 | tf_op jit(solution)/shard_map/ppermute | solution.py:173
  9.0 3.0 %collective-permute-done.1.refs_2_ = bf16[256,128]{1,0:T(8,128)(2,1)S(1)} collective-permute-done((bf16[256,128]{1,0:T(8,128)(2,1)S(1)}, bf16[256,128]{1,0:T(8,128)(2,1)S(1)}, u32[]{:S(2)}, u32[]{:S(2)}) %collective-permute-start.1) | collective-permute-done | bytes 65568 | tf_op jit(solution)/shard_map/ppermute | solution.py:173
  12.1 0.1 shard_map.102.raw.refs_12_
  12.2 1.6 %collective-permute-start.3 = (bf16[512,256]{1,0:T(8,128)(2,1)S(1)}, bf16[512,256]{1,0:T(8,128)(2,1)S(1)}, u32[]{:S(2)}, u32[]{:S(2)}) collective-permute-start(bf16[512,256]{1,0:T(8,128)(2,1)S(1)} %shard_map.102.raw.refs_12_), channel_id=1, source_target_pairs={{0,2},{2,0},{4,6},{6,4},{8,10},{10,8},{12,14},{14,12},{16,18},{18,... | collective-permute-start | bytes 786440 | tf_op jit(solution)/shard_map/ppermute | solution.py:173
  13.7 1.5 %collective-permute-start.5 = (bf16[512,256]{1,0:T(8,128)(2,1)S(1)}, bf16[512,256]{1,0:T(8,128)(2,1)S(1)}, u32[]{:S(2)}, u32[]{:S(2)}) collective-permute-start(bf16[512,256]{1,0:T(8,128)(2,1)S(1)} %shard_map.102.raw.refs_12_), channel_id=1, source_target_pairs={{0,6},{2,4},{4,2},{6,0},{8,14},{10,12},{12,10},{14,8},{16,22},{18,... | collective-permute-start | bytes 786440 | tf_op jit(solution)/shard_map/ppermute | solution.py:173
  15.2 0.5 %collective-permute-start.4 = (bf16[512,256]{1,0:T(8,128)(2,1)S(1)}, bf16[512,256]{1,0:T(8,128)(2,1)S(1)}, u32[]{:S(2)}, u32[]{:S(2)}) collective-permute-start(bf16[512,256]{1,0:T(8,128)(2,1)S(1)} %shard_map.102.raw.refs_12_), channel_id=1, source_target_pairs={{0,4},{2,6},{4,0},{6,2},{8,12},{10,14},{12,8},{14,10},{16,20},{18,... | collective-permute-start | bytes 786440 | tf_op jit(solution)/shard_map/ppermute | solution.py:173
  15.7 0.9 %copy-done = bf16[128,1024]{1,0:T(8,128)(2,1)S(1)} copy-done((bf16[128,1024]{1,0:T(8,128)(2,1)S(1)}, bf16[128,1024]{1,0:T(8,128)(2,1)}, u32[]{:S(2)}) %copy-start) | copy-done | bytes 262168
  16.7 0.9 %copy-done.1 = bf16[1024,128]{1,0:T(8,128)(2,1)S(1)} copy-done((bf16[1024,128]{1,0:T(8,128)(2,1)S(1)}, bf16[1024,128]{1,0:T(8,128)(2,1)}, u32[]{:S(2)}) %copy-start.1) | copy-done | bytes 262168
  17.6 0.7 %copy-done.2 = f32[1024]{0:T(1024)S(1)} copy-done((f32[1024]{0:T(1024)S(1)}, f32[1024]{0:T(1024)}, u32[]{:S(2)}) %copy-start.2) | copy-done | bytes 4120
  18.3 0.7 %copy-done.3 = f32[128]{0:T(128)S(1)} copy-done((f32[128]{0:T(128)S(1)}, f32[128]{0:T(128)}, u32[]{:S(2)}) %copy-start.3) | copy-done | bytes 536
  19.0 1.1 %shard_map.103 = (bf16[512,256]{1,0:T(8,128)(2,1)S(1)}, bf16[512,1024]{1,0:T(8,128)(2,1)S(1)}, f32[512,1024]{1,0:T(8,128)S(1)}, bf16[128,1024]{1,0:T(8,128)(2,1)...) custom-call(bf16[512,256]{1,0:T(8,128)(2,1)S(1)} %shard_map.102.raw.refs_12_, ...), custom_call_target="tpu_custom_call" | custom-call | flops 268435456 | bytes 791040 | tf_op jit(solution)/shard_map/pallas_call | solution.py:37
  20.1 0.1 collective-permute-start.6
  20.2 1.3 %collective-permute-done.3.raw.refs_13_ = bf16[512,256]{1,0:T(8,128)(2,1)S(1)} collective-permute-done((bf16[512,256]{1,0:T(8,128)(2,1)S(1)}, bf16[512,256]{1,0:T(8,128)(2,1)S(1)}, u32[]{:S(2)}, u32[]{:S(2)}) %collective-permute-start.3) | collective-permute-done | bytes 262176 | tf_op jit(solution)/shard_map/ppermute | solution.py:173
  21.5 1.1 %shard_map.104 = (bf16[512,256]{1,0:T(8,128)(2,1)S(1)}, bf16[512,1024]{1,0:T(8,128)(2,1)S(1)}, f32[512,1024]{1,0:T(8,128)S(1)}) custom-call(bf16[512,256]{1,0:T(8,128)(2,1)S(1)} %collective-permute-done.3.raw.refs_13_, bf16[128,1024]{1,0:T(8,128)(2,1)S(1)} %get-tuple-element.40.w_in, f32[1,1024]{1,0:T(1,128)S(1)} %get-tuple-element.41.b_in, ...), custom_call_target="tpu_custom_call" | custom-call | flops 268435456 | bytes 791040 | tf_op jit(solution)/shard_map/pallas_call | solution.py:37
  22.6 0.1 collective-permute-start.7
  22.7 2.0 %shard_map.105 = (f32[128,512]{1,0:T(8,128)S(1)}, f32[128,512]{1,0:T(8,128)S(1)}) custom-call(bf16[512,256]{1,0:T(8,128)(2,1)S(1)} %get-tuple-element.39.refs_0_.refs_2_, bf16[512,256]{1,0:T(8,128)(2,1)S(1)} %get-tuple-element.44.refs_1_.refs_3_, bf16[512,256]{1,0:T(8,128)(2,1)S(1)} %get-tuple-element.39.refs_0_.refs_2_, ...), custom_call_target="tpu_custom_call" | custom-call | flops 25769803776 | bytes 1048576 | tf_op jit(solution)/shard_map/pallas_call | solution.py:37
  24.8 2.1 %shard_map.106 = (f32[128,512]{1,0:T(8,128)S(1)}, f32[128,512]{1,0:T(8,128)S(1)}) custom-call(bf16[512,256]{1,0:T(8,128)(2,1)S(1)} %get-tuple-element.39.refs_0_.refs_2_, bf16[512,256]{1,0:T(8,128)(2,1)S(1)} %get-tuple-element.44.refs_1_.refs_3_, bf16[512,256]{1,0:T(8,128)(2,1)S(1)} %collective-permute-done.6.refs_2_.refs_4_, ...), custom_call_target="tpu_custom_call" | custom-call | flops 3221225472 | bytes 1048576 | tf_op jit(solution)/shard_map/pallas_call | solution.py:37
  26.8 0.2 collective-permute-done.5.raw.refs_15_
  27.0 1.1 %shard_map.107 = (bf16[512,256]{1,0:T(8,128)(2,1)S(1)}, bf16[512,1024]{1,0:T(8,128)(2,1)S(1)}, f32[512,1024]{1,0:T(8,128)S(1)}) custom-call(bf16[512,256]{1,0:T(8,128)(2,1)S(1)} %collective-permute-done.5.raw.refs_15_, bf16[128,1024]{1,0:T(8,128)(2,1)S(1)} %get-tuple-element.40.w_in, f32[1,1024]{1,0:T(1,128)S(1)} %get-tuple-element.41.b_in, ...), custom_call_target="tpu_custom_call" | custom-call | flops 268435456 | bytes 791040 | tf_op jit(solution)/shard_map/pallas_call | solution.py:37
  28.1 0.4 collective-permute-start.9
  28.5 1.1 %shard_map.108 = (bf16[512,256]{1,0:T(8,128)(2,1)S(1)}, bf16[512,1024]{1,0:T(8,128)(2,1)S(1)}, f32[512,1024]{1,0:T(8,128)S(1)}) custom-call(bf16[512,256]{1,0:T(8,128)(2,1)S(1)} %collective-permute-done.4.raw.refs_14_, bf16[128,1024]{1,0:T(8,128)(2,1)S(1)} %get-tuple-element.40.w_in, f32[1,1024]{1,0:T(1,128)S(1)} %get-tuple-element.41.b_in, ...), custom_call_target="tpu_custom_call" | custom-call | flops 268435456 | bytes 791040 | tf_op jit(solution)/shard_map/pallas_call | solution.py:37
  29.7 0.2 collective-permute-start.8
  29.9 5.6 %shard_map.109 = (f32[128,512]{1,0:T(8,128)S(1)}, f32[128,512]{1,0:T(8,128)S(1)}, f32[128,512]{1,0:T(8,128)S(1)}, f32[128,512]{1,0:T(8,128)S(1)}) custom-call(bf16[512,256]{1,0:T(8,128)(2,1)S(1)} %get-tuple-element.39.refs_0_.refs_2_, bf16[512,256]{1,0:T(8,128)(2,1)S(1)} %get-tuple-element.44.refs_1_.refs_3_, ...), custom_call_target="tpu_custom_call" | custom-call | flops 3221225472 | bytes 1572864 | tf_op jit(solution)/shard_map/pallas_call | solution.py:37
  35.5 8.4 %shard_map.110 = (f32[128,128]{1,0:T(8,128)}, f32[136,1024]{1,0:T(8,128)S(1)}, bf16[128,512]{1,0:T(8,128)(2,1)S(1)}, bf16[128,512]{1,0:T(8,128)(2,1)S(1)}, bf16[...) custom-call(bf16[512,256]{1,0:T(8,128)(2,1)S(1)} %get-tuple-element.39.refs_0_.refs_2_, ...), custom_call_target="tpu_custom_call" | custom-call | flops 3221225472 | bytes 13369856 | tf_op jit(solution)/shard_map/pallas_call | solution.py:37
  44.0 0.4 collective-permute-start.10
  44.4 0.7 %shard_map.111.mine_out = f32[128,1024]{1,0:T(8,128)S(1)} custom-call(bf16[128,512]{1,0:T(8,128)(2,1)S(1)} %get-tuple-element.63.refs_0_, bf16[128,512]{1,0:T(8,128)(2,1)S(1)} %get-tuple-element.64.refs_1_, bf16[128,512]{1,0:T(8,128)(2,1)S(1)} %get-tuple-element.65.refs_2_, bf16[128,512]{1,0:T(8,128)(2,1)S(1)} %get-tuple-element.66.refs_3_, ...), custom_call_target="tpu_custom_call" | custom-call | bytes 4718592 | tf_op jit(solution)/shard_map/pallas_call | solution.py:37
  45.1 0.2 collective-permute-start.11
  45.4 1.7 %collective-permute-done.11.other_out = f32[128,1024]{1,0:T(8,128)S(1)} collective-permute-done((f32[128,1024]{1,0:T(8,128)S(1)}, f32[128,1024]{1,0:T(8,128)S(1)}, u32[]{:S(2)}, u32[]{:S(2)}) %collective-permute-start.11) | collective-permute-done | bytes 524320 | tf_op jit(solution)/shard_map/ppermute | solution.py:173
  47.1 1.2 %shard_map.112 = (f32[128,1024]{1,0:T(8,128)}, f32[1,1024]{1,0:T(1,128)}, f32[1024,128]{1,0:T(8,128)}) custom-call(f32[136,1024]{1,0:T(8,128)S(1)} %get-tuple-element.62.mine, f32[136,1024]{1,0:T(8,128)S(1)} %collective-permute-done.10.other, f32[128,1024]{1,0:T(8,128)S(1)} %shard_map.111.mine_out, f32[128,1024]{1,0:T(8,128)S(1)} %collective-permute-done.11.other_out), custom_call_target="tpu_custom_call" | custom-call | bytes 2162688 | tf_op jit(solution)/shard_map/pallas_call | solution.py:37
  (12 shorter events, 0.0 us)
Async XLA Ops:
  1.4 7.6 %collective-permute-start.2 = (bf16[256,128]{1,0:T(8,128)(2,1)S(1)}, bf16[256,128]{1,0:T(8,128)(2,1)S(1)}, u32[]{:S(2)}, u32[]{:S(2)}) collective-permute-start(bf16[256,128]{1,0:T(8,128)(2,1)S(1)} %pad_maximum_fusion.refs_0_), channel_id=1, source_target_pairs={{0,24},{2,26},{4,28},{6,30},{8,16},{10,18},{12,20},{14,22},{16,8},... | collective-permute-start | bytes 196616 | tf_op jit(solution)/shard_map/ppermute | solution.py:173
  6.5 5.6 %collective-permute-start.1 = (bf16[256,128]{1,0:T(8,128)(2,1)S(1)}, bf16[256,128]{1,0:T(8,128)(2,1)S(1)}, u32[]{:S(2)}, u32[]{:S(2)}) collective-permute-start(bf16[256,128]{1,0:T(8,128)(2,1)S(1)} %pad_maximum_fusion.refs_0_), channel_id=1, source_target_pairs={{0,16},{2,18},{4,20},{6,22},{8,24},{10,26},{12,28},{14,30},{16,0},... | collective-permute-start | bytes 196616 | tf_op jit(solution)/shard_map/ppermute | solution.py:173
  6.5 5.6 %collective-permute-start = (bf16[256,128]{1,0:T(8,128)(2,1)S(1)}, bf16[256,128]{1,0:T(8,128)(2,1)S(1)}, u32[]{:S(2)}, u32[]{:S(2)}) collective-permute-start(bf16[256,128]{1,0:T(8,128)(2,1)S(1)} %pad_maximum_fusion.refs_0_), channel_id=1, source_target_pairs={{0,8},{2,10},{4,12},{6,14},{8,0},{10,2},{12,4},{14,6},{16,24},{18,... | collective-permute-start | bytes 196616 | tf_op jit(solution)/shard_map/ppermute | solution.py:173
  12.2 9.3 %collective-permute-start.3 = (bf16[512,256]{1,0:T(8,128)(2,1)S(1)}, bf16[512,256]{1,0:T(8,128)(2,1)S(1)}, u32[]{:S(2)}, u32[]{:S(2)}) collective-permute-start(bf16[512,256]{1,0:T(8,128)(2,1)S(1)} %shard_map.102.raw.refs_12_), channel_id=1, source_target_pairs={{0,2},{2,0},{4,6},{6,4},{8,10},{10,8},{12,14},{14,12},{16,18},{18,... | collective-permute-start | bytes 786440 | tf_op jit(solution)/shard_map/ppermute | solution.py:173
  13.7 13.2 %collective-permute-start.5 = (bf16[512,256]{1,0:T(8,128)(2,1)S(1)}, bf16[512,256]{1,0:T(8,128)(2,1)S(1)}, u32[]{:S(2)}, u32[]{:S(2)}) collective-permute-start(bf16[512,256]{1,0:T(8,128)(2,1)S(1)} %shard_map.102.raw.refs_12_), channel_id=1, source_target_pairs={{0,6},{2,4},{4,2},{6,0},{8,14},{10,12},{12,10},{14,8},{16,22},{18,... | collective-permute-start | bytes 786440 | tf_op jit(solution)/shard_map/ppermute | solution.py:173
  15.2 13.3 %collective-permute-start.4 = (bf16[512,256]{1,0:T(8,128)(2,1)S(1)}, bf16[512,256]{1,0:T(8,128)(2,1)S(1)}, u32[]{:S(2)}, u32[]{:S(2)}) collective-permute-start(bf16[512,256]{1,0:T(8,128)(2,1)S(1)} %shard_map.102.raw.refs_12_), channel_id=1, source_target_pairs={{0,4},{2,6},{4,0},{6,2},{8,12},{10,14},{12,8},{14,10},{16,20},{18,... | collective-permute-start | bytes 786440 | tf_op jit(solution)/shard_map/ppermute | solution.py:173
  15.7 0.9 %copy-start = (bf16[128,1024]{1,0:T(8,128)(2,1)S(1)}, bf16[128,1024]{1,0:T(8,128)(2,1)}, u32[]{:S(2)}) copy-start(bf16[128,1024]{1,0:T(8,128)(2,1)} %w_in.1) | copy-start | bytes 786436
  16.7 0.9 %copy-start.1 = (bf16[1024,128]{1,0:T(8,128)(2,1)S(1)}, bf16[1024,128]{1,0:T(8,128)(2,1)}, u32[]{:S(2)}) copy-start(bf16[1024,128]{1,0:T(8,128)(2,1)} %w_out.1) | copy-start | bytes 786436
  17.6 0.7 %copy-start.2 = (f32[1024]{0:T(1024)S(1)}, f32[1024]{0:T(1024)}, u32[]{:S(2)}) copy-start(f32[1024]{0:T(1024)} %param.9) | copy-start | bytes 12292
  18.3 0.7 %copy-start.3 = (f32[128]{0:T(128)S(1)}, f32[128]{0:T(128)}, u32[]{:S(2)}) copy-start(f32[128]{0:T(128)} %param.11) | copy-start | bytes 1540
  20.1 4.6 %collective-permute-start.6 = (bf16[512,256]{1,0:T(8,128)(2,1)S(1)}, bf16[512,256]{1,0:T(8,128)(2,1)S(1)}, u32[]{:S(2)}, u32[]{:S(2)}) collective-permute-start(bf16[512,256]{1,0:T(8,128)(2,1)S(1)} %get-tuple-element.39.refs_0_.refs_2_), channel_id=1, source_target_pairs={{0,1},{1,0},{2,3},{3,2},{4,5},{5,4},{6,7},{7,6},{8,9},{9,8},{10,11... | collective-permute-start | bytes 786440 | tf_op jit(solution)/shard_map/ppermute | solution.py:173
  22.6 2.1 %collective-permute-start.7 = (bf16[512,256]{1,0:T(8,128)(2,1)S(1)}, bf16[512,256]{1,0:T(8,128)(2,1)S(1)}, u32[]{:S(2)}, u32[]{:S(2)}) collective-permute-start(bf16[512,256]{1,0:T(8,128)(2,1)S(1)} %get-tuple-element.44.refs_1_.refs_3_), channel_id=1, source_target_pairs={{0,1},{1,0},{2,3},{3,2},{4,5},{5,4},{6,7},{7,6},{8,9},{9,8},{10,11... | collective-permute-start | bytes 786440 | tf_op jit(solution)/shard_map/ppermute | solution.py:173
  28.1 7.4 %collective-permute-start.9 = (bf16[512,256]{1,0:T(8,128)(2,1)S(1)}, bf16[512,256]{1,0:T(8,128)(2,1)S(1)}, u32[]{:S(2)}, u32[]{:S(2)}) collective-permute-start(bf16[512,256]{1,0:T(8,128)(2,1)S(1)} %get-tuple-element.50.refs_3_), channel_id=1, source_target_pairs={{0,1},{1,0},{2,3},{3,2},{4,5},{5,4},{6,7},{7,6},{8,9},{9,8},{10,11... | collective-permute-start | bytes 786440 | tf_op jit(solution)/shard_map/ppermute | solution.py:173
  29.7 5.9 %collective-permute-start.8 = (bf16[512,256]{1,0:T(8,128)(2,1)S(1)}, bf16[512,256]{1,0:T(8,128)(2,1)S(1)}, u32[]{:S(2)}, u32[]{:S(2)}) collective-permute-start(bf16[512,256]{1,0:T(8,128)(2,1)S(1)} %get-tuple-element.52.refs_2_), channel_id=1, source_target_pairs={{0,1},{1,0},{2,3},{3,2},{4,5},{5,4},{6,7},{7,6},{8,9},{9,8},{10,11... | collective-permute-start | bytes 786440 | tf_op jit(solution)/shard_map/ppermute | solution.py:173
  44.0 3.1 %collective-permute-start.10 = (f32[136,1024]{1,0:T(8,128)S(1)}, f32[136,1024]{1,0:T(8,128)S(1)}, u32[]{:S(2)}, u32[]{:S(2)}) collective-permute-start(f32[136,1024]{1,0:T(8,128)S(1)} %get-tuple-element.62.mine), channel_id=1, source_target_pairs={{0,1},{1,0},{2,3},{3,2},{4,5},{5,4},{6,7},{7,6},{8,9},{9,8},{10,11... | collective-permute-start | bytes 1671176 | tf_op jit(solution)/shard_map/ppermute | solution.py:173
  45.1 2.0 %collective-permute-start.11 = (f32[128,1024]{1,0:T(8,128)S(1)}, f32[128,1024]{1,0:T(8,128)S(1)}, u32[]{:S(2)}, u32[]{:S(2)}) collective-permute-start(f32[128,1024]{1,0:T(8,128)S(1)} %shard_map.111.mine_out), channel_id=1, source_target_pairs={{0,1},{1,0},{2,3},{3,2},{4,5},{5,4},{6,7},{7,6},{8,9},{9,8},{10,11... | collective-permute-start | bytes 1572872 | tf_op jit(solution)/shard_map/ppermute | solution.py:173
